TPU v7x, 32 devices: a whole 2x2x4 slice. The times are simulated.
32 devices in a mesh: group: 4 (over y, x), member: 8 (over z, core).
Axes of the slice: x: 2, y: 2, z: 4, core: 2. Of those that a mesh axis runs over, the one named last changes fastest.
Arguments:
- features: bfloat16 [32768, 1024], P(('group', 'member')), may hold values from -6 to 6
- w_self: bfloat16 [1024, 1024], replicated, may hold values from -0.1875 to 0.1875
- w_neigh: bfloat16 [1024, 1024], replicated, may hold values from -0.1875 to 0.1875
- bias: bfloat16 [1024], replicated, may hold values from -3 to 3
- hub_rows: int32 [192], P(('group', 'member')), may hold values from 0 to 1023
- hub_nbrs: int32 [32768, 8], P(('group', 'member')), may hold values from 0 to 191
- local_nbrs: int32 [32768, 16], P(('group', 'member')), may hold values from 0 to 1023
- halo_nbrs: int32 [32768, 16], P(('group', 'member')), may hold values from 0 to 1023
- degrees: int32 [3, 32768], P(None, ('group', 'member')), may hold values from 0 to 16, as said below
- send_rows: int32 [32, 8, 128], P(('group', 'member')), may hold values from 0 to 1023
Outputs:
- hidden_out: bfloat16 [32768, 1024], P(('group', 'member'))
Inputs may be any that keep to these rules, and one draw needn't show every extreme that they name: degrees[0] is at least 1 and reaches 16; degrees[1] reaches 8; degrees[2] reaches 16, each in every draw.
All inputs are finite; a program needn't handle non-finite values.
Results may differ from a plain program's by a relative error of at most 0.002.
Values may be sent and summed in bfloat16 or wider, within the bound.
No kernel may reach another device: no remote copies, remote signals or barrier semaphores. Data moves between devices by JAX's collectives and lax.ppermute only.
A program may use at most 128 MiB of HBM per device.

v0:
```python
import math

import jax
import jax.numpy as jnp
from jax import lax
from jax.sharding import PartitionSpec as P


def count_table(index_list, valid_mask, total):
    numbers = jnp.arange(total, dtype=jnp.int32)
    tallies = jnp.zeros((index_list.shape[0], total), jnp.float32)
    for slot in range(index_list.shape[1]):
        hits = (index_list[:, slot][:, None] == numbers[None, :]) & valid_mask[:, slot][:, None]
        tallies = tallies + hits.astype(jnp.float32)
    return tallies.astype(jnp.bfloat16)


def block_mean(
    self_features,
    hub_lookup_matrix,
    neighbour_positions,
    local_index_list,
    hub_index_list,
    halo_index_list,
    deg,
):
    klocal = local_index_list.shape[1]
    khub = hub_index_list.shape[1]
    khalo = halo_index_list.shape[1]
    local_valid_mask = jnp.arange(klocal)[None, :] < deg[0][:, None]
    hub_valid_mask = jnp.arange(khub)[None, :] < deg[1][:, None]
    halo_valid_mask = jnp.arange(khalo)[None, :] < deg[2][:, None]
    local_counts = count_table(local_index_list, local_valid_mask, self_features.shape[0])
    neighbour_sum = jnp.dot(local_counts, self_features, preferred_element_type=jnp.float32)
    hub_counts = count_table(hub_index_list, hub_valid_mask, hub_lookup_matrix.shape[0])
    neighbour_sum = neighbour_sum + jnp.dot(
        hub_counts, hub_lookup_matrix, preferred_element_type=jnp.float32
    )
    halo_counts = count_table(halo_index_list, halo_valid_mask, neighbour_positions.shape[0])
    neighbour_sum = neighbour_sum + jnp.dot(
        halo_counts, neighbour_positions, preferred_element_type=jnp.float32
    )
    count = (
        jnp.sum(local_valid_mask.astype(jnp.float32), axis=1)
        + jnp.sum(hub_valid_mask.astype(jnp.float32), axis=1)
        + jnp.sum(halo_valid_mask.astype(jnp.float32), axis=1)
    )
    return (neighbour_sum / count[:, None]).astype(jnp.bfloat16)


def per_device(
    features, w_self, w_neigh, bias, hub_rows, hub_nbrs, local_nbrs, halo_nbrs, degrees, send_rows
):
    rows_here = features.shape[0]
    width = features.shape[1]
    peers = send_rows.shape[1]
    caps = send_rows.shape[2]
    mine = jnp.take(features, hub_rows, axis=0)
    hub_lookup_matrix = lax.all_gather(mine, ("group", "member"), axis=0, tiled=True)
    outgoing = jnp.take(features, send_rows.reshape(peers * caps), axis=0).reshape(
        peers, caps, width
    )
    received = lax.all_to_all(outgoing, "member", split_axis=0, concat_axis=0, tiled=True)
    neighbour_positions = received.reshape(peers * caps, width)
    blk = math.gcd(rows_here, 256)
    nblocks = rows_here // blk
    local_index_list = local_nbrs.reshape(nblocks, blk, local_nbrs.shape[1])
    hub_index_list = hub_nbrs.reshape(nblocks, blk, hub_nbrs.shape[1])
    halo_index_list = halo_nbrs.reshape(nblocks, blk, halo_nbrs.shape[1])
    deg = degrees.reshape(3, nblocks, blk).transpose(1, 0, 2)

    def one(item):
        return block_mean(
            features, hub_lookup_matrix, neighbour_positions, item[0], item[1], item[2], item[3]
        )

    neigh_mean = lax.map(one, (local_index_list, hub_index_list, halo_index_list, deg)).reshape(
        rows_here, width
    )
    value = jnp.dot(features, w_self, preferred_element_type=jnp.float32)
    value = value + jnp.dot(neigh_mean, w_neigh, preferred_element_type=jnp.float32)
    value = value + bias.astype(jnp.float32)[None, :]
    return jnp.maximum(value, 0.0).astype(jnp.bfloat16)


def solution(mesh):
    in_specs = (
        P(("group", "member"), None),
        P(),
        P(),
        P(),
        P(("group", "member")),
        P(("group", "member"), None),
        P(("group", "member"), None),
        P(("group", "member"), None),
        P(None, ("group", "member")),
        P(("group", "member"), None, None),
    )
    out_specs = P(("group", "member"), None)
    return jax.shard_map(
        per_device, mesh=mesh, in_specs=in_specs, out_specs=out_specs, check_vma=False
    )
```

profile of v0, /device:TPU:0, one launch (start us, length us, event | category | flops | bytes accessed | tf_op | source)
XLA Modules:
  0.0 173.2 jit_solution(1874724149700012314)
XLA Ops:
  0.0 0.8 compare_and_fusion
  1.5 7.9 %gather_fusion.1 = bf16[1024,1024]{1,0:T(8,128)(2,1)} fusion(bf16[1024,1024]{1,0:T(8,128)(2,1)} %param.12, s32[1024]{0:T(1024)S(1)} %broadcast_clamp_fusion), kind=kCustom, calls=%fused_computation.1 | custom fusion | bytes 4198400 | tf_op jit(solution)/shard_map/jit(_take)/gather | solution.py:60
  9.4 3.2 %broadcast_select_fusion = bf16[8,128,1024]{2,1,0:T(8,128)(2,1)} fusion(bf16[8,128,1024]{2,1,0:T(8,128)(2,1)} %bitcast.181, pred[8,128]{1,0:T(8,128)(4,1)S(1)} %compare_and_fusion), kind=kLoop, calls=%fused_computation.229 | loop fusion | flops 1048576 | bytes 4195328 | tf_op jit(solution)/shard_map/jit(_take)/select_n | solution.py:60
  12.6 6.5 %all-to-all-start = ((bf16[8,128,1024]{2,1,0:T(8,128)(2,1)}), bf16[8,128,1024]{2,1,0:T(8,128)(2,1)}, u32[]{:S(2)}, u32[]{:S(2)}) async-start(bf16[8,128,1024]{2,1,0:T(8,128)(2,1)} %broadcast_select_fusion), calls=%async_computation | async-start | bytes 4194304 | tf_op jit(solution)/shard_map/all_to_all | solution.py:63
  19.1 2.4 %gather_fusion = bf16[6,1024]{1,0:T(8,128)(2,1)S(1)} fusion(bf16[1024,1024]{1,0:T(8,128)(2,1)} %param.12, s32[1024]{0:T(1024)S(1)} %pad_clamp_fusion), kind=kCustom, calls=%fused_computation | custom fusion | bytes 24600 | tf_op jit(solution)/shard_map/jit(_take)/gather | solution.py:58
  21.6 78.4 %all-gather = bf16[32,6,1024]{2,1,0:T(8,128)(2,1)S(1)} all-gather(bf16[1,6,1024]{2,1,0:T(8,128)(2,1)S(1)} %select_bitcast_fusion), channel_id=1, replica_groups=mesh['group'=4,'member'=8] {'group','member'}, dimensions={0}, use_global_device_ids=true | all-gather | bytes 405504 | tf_op jit(solution)/shard_map/all_gather | solution.py:59
  100.3 5.8 %fusion.130 = f32[1024,1024]{1,0:T(8,128)} fusion(bf16[1024,1024]{1,0:T(8,128)(2,1)} %param.12, bf16[1024,1024]{1,0:T(8,128)(2,1)S(1)} %copy-done), kind=kOutput, calls=%fused_computation.241 | convolution fusion | flops 2147483648 | bytes 8388608 | tf_op jit(solution)/shard_map/dot_general | solution.py:80
  106.1 59.9 %while.10 = (s32[]{:T(128)}, bf16[4,256,1024]{2,1,0:T(8,128)(2,1)}, s32[4,256,16]{1,0,2:T(4,128)S(1)}, s32[4,3,256]{2,1,0:T(4,128)}, bf16[1024,1024]{1,0:T(8,128...) while((s32[]{:T(128)}, bf16[4,256,1024]{2,1,0:T(8,128)(2,1)}, ...), condition=%wide.region_4.5_spmd, body=%wide.region_0.4_spmd.sunk | while | flops 1210621696 | bytes 9638569 | solution.py:77
  106.1 0.8 constant_dynamic-slice_fusion.8
  107.1 5.6 %fusion.153 = f32[256,1024]{1,0:T(8,128)S(1)} fusion(bf16[1024,1024]{1,0:T(8,128)(2,1)} %get-tuple-element.435, s32[256]{0:T(256)S(1)} %bitcast.192, s32[256]{0:T(256)S(1)} %bitcast.193, s32[256]{0:T(256)S(1)} %bitcast.194, s32[256]{0:T(256)S(1)} %bitcast.195, s32[256]{0:T(256)S(1)} %bitcast.196, s32[256]{0:T(256)S(1)} %bitcast.197, ...), kind=kOutput, calls=%fused_computation.74.clone.1 | convolution fusion | flops 553648128 | bytes 3166208 | tf_op jit(solution)/shard_map/while/body/eval_jaxpr/dot_general | solution.py:34
  112.8 5.6 %fusion.151 = f32[256,1024]{1,0:T(8,128)S(1)} fusion(bf16[1024,1024]{1,0:T(8,128)(2,1)} %get-tuple-element.439, s32[256]{0:T(256)S(1)} %bitcast.208, s32[256]{0:T(256)S(1)} %bitcast.209, s32[256]{0:T(256)S(1)} %bitcast.210, s32[256]{0:T(256)S(1)} %bitcast.211, s32[256]{0:T(256)S(1)} %bitcast.212, s32[256]{0:T(256)S(1)} %bitcast.213, ...), kind=kOutput, calls=%fused_computation.75.clone.1 | convolution fusion | flops 553648128 | bytes 3166208 | tf_op jit(solution)/shard_map/while/body/eval_jaxpr/dot_general | solution.py:40
  119.2 1.9 %fusion.155 = bf16[4,256,1024]{2,1,0:T(8,128)(2,1)} fusion(bf16[4,256,1024]{2,1,0:T(8,128)(2,1)} %get-tuple-element.419, s32[]{:T(128)} %get-tuple-element.418, f32[256,1024]{1,0:T(8,128)S(1)} %fusion.151, f32[256,1024]{1,0:T(8,128)S(1)} %fusion.153, bf16[192,1024]{1,0:T(8,128)(2,1)S(1)} %get-tuple-element.437, f32[256]{0:T(256)S(1)} %add_add_fusion.2, ...), kind=kOutput, calls=%fused_computation.7.clone.1 | convolution fusion | flops 103284736 | bytes 3026432 | tf_op jit(solution)/shard_map/while/body/eval_jaxpr/dot_general | solution.py:36
  121.1 0.8 constant_dynamic-slice_fusion.8
  122.1 5.6 %fusion.153 = f32[256,1024]{1,0:T(8,128)S(1)} fusion(bf16[1024,1024]{1,0:T(8,128)(2,1)} %get-tuple-element.435, s32[256]{0:T(256)S(1)} %bitcast.192, s32[256]{0:T(256)S(1)} %bitcast.193, s32[256]{0:T(256)S(1)} %bitcast.194, s32[256]{0:T(256)S(1)} %bitcast.195, s32[256]{0:T(256)S(1)} %bitcast.196, s32[256]{0:T(256)S(1)} %bitcast.197, ...), kind=kOutput, calls=%fused_computation.74.clone.1 | convolution fusion | flops 553648128 | bytes 3166208 | tf_op jit(solution)/shard_map/while/body/eval_jaxpr/dot_general | solution.py:34
  127.8 5.6 %fusion.151 = f32[256,1024]{1,0:T(8,128)S(1)} fusion(bf16[1024,1024]{1,0:T(8,128)(2,1)} %get-tuple-element.439, s32[256]{0:T(256)S(1)} %bitcast.208, s32[256]{0:T(256)S(1)} %bitcast.209, s32[256]{0:T(256)S(1)} %bitcast.210, s32[256]{0:T(256)S(1)} %bitcast.211, s32[256]{0:T(256)S(1)} %bitcast.212, s32[256]{0:T(256)S(1)} %bitcast.213, ...), kind=kOutput, calls=%fused_computation.75.clone.1 | convolution fusion | flops 553648128 | bytes 3166208 | tf_op jit(solution)/shard_map/while/body/eval_jaxpr/dot_general | solution.py:40
  134.2 1.9 %fusion.155 = bf16[4,256,1024]{2,1,0:T(8,128)(2,1)} fusion(bf16[4,256,1024]{2,1,0:T(8,128)(2,1)} %get-tuple-element.419, s32[]{:T(128)} %get-tuple-element.418, f32[256,1024]{1,0:T(8,128)S(1)} %fusion.151, f32[256,1024]{1,0:T(8,128)S(1)} %fusion.153, bf16[192,1024]{1,0:T(8,128)(2,1)S(1)} %get-tuple-element.437, f32[256]{0:T(256)S(1)} %add_add_fusion.2, ...), kind=kOutput, calls=%fused_computation.7.clone.1 | convolution fusion | flops 103284736 | bytes 3026432 | tf_op jit(solution)/shard_map/while/body/eval_jaxpr/dot_general | solution.py:36
  136.1 0.8 constant_dynamic-slice_fusion.8
  137.1 5.6 %fusion.153 = f32[256,1024]{1,0:T(8,128)S(1)} fusion(bf16[1024,1024]{1,0:T(8,128)(2,1)} %get-tuple-element.435, s32[256]{0:T(256)S(1)} %bitcast.192, s32[256]{0:T(256)S(1)} %bitcast.193, s32[256]{0:T(256)S(1)} %bitcast.194, s32[256]{0:T(256)S(1)} %bitcast.195, s32[256]{0:T(256)S(1)} %bitcast.196, s32[256]{0:T(256)S(1)} %bitcast.197, ...), kind=kOutput, calls=%fused_computation.74.clone.1 | convolution fusion | flops 553648128 | bytes 3166208 | tf_op jit(solution)/shard_map/while/body/eval_jaxpr/dot_general | solution.py:34
  142.8 5.6 %fusion.151 = f32[256,1024]{1,0:T(8,128)S(1)} fusion(bf16[1024,1024]{1,0:T(8,128)(2,1)} %get-tuple-element.439, s32[256]{0:T(256)S(1)} %bitcast.208, s32[256]{0:T(256)S(1)} %bitcast.209, s32[256]{0:T(256)S(1)} %bitcast.210, s32[256]{0:T(256)S(1)} %bitcast.211, s32[256]{0:T(256)S(1)} %bitcast.212, s32[256]{0:T(256)S(1)} %bitcast.213, ...), kind=kOutput, calls=%fused_computation.75.clone.1 | convolution fusion | flops 553648128 | bytes 3166208 | tf_op jit(solution)/shard_map/while/body/eval_jaxpr/dot_general | solution.py:40
  149.2 1.9 %fusion.155 = bf16[4,256,1024]{2,1,0:T(8,128)(2,1)} fusion(bf16[4,256,1024]{2,1,0:T(8,128)(2,1)} %get-tuple-element.419, s32[]{:T(128)} %get-tuple-element.418, f32[256,1024]{1,0:T(8,128)S(1)} %fusion.151, f32[256,1024]{1,0:T(8,128)S(1)} %fusion.153, bf16[192,1024]{1,0:T(8,128)(2,1)S(1)} %get-tuple-element.437, f32[256]{0:T(256)S(1)} %add_add_fusion.2, ...), kind=kOutput, calls=%fused_computation.7.clone.1 | convolution fusion | flops 103284736 | bytes 3026432 | tf_op jit(solution)/shard_map/while/body/eval_jaxpr/dot_general | solution.py:36
  152.0 5.6 %fusion.153 = f32[256,1024]{1,0:T(8,128)S(1)} fusion(bf16[1024,1024]{1,0:T(8,128)(2,1)} %get-tuple-element.435, s32[256]{0:T(256)S(1)} %bitcast.192, s32[256]{0:T(256)S(1)} %bitcast.193, s32[256]{0:T(256)S(1)} %bitcast.194, s32[256]{0:T(256)S(1)} %bitcast.195, s32[256]{0:T(256)S(1)} %bitcast.196, s32[256]{0:T(256)S(1)} %bitcast.197, ...), kind=kOutput, calls=%fused_computation.74.clone.1 | convolution fusion | flops 553648128 | bytes 3166208 | tf_op jit(solution)/shard_map/while/body/eval_jaxpr/dot_general | solution.py:34
  157.7 5.6 %fusion.151 = f32[256,1024]{1,0:T(8,128)S(1)} fusion(bf16[1024,1024]{1,0:T(8,128)(2,1)} %get-tuple-element.439, s32[256]{0:T(256)S(1)} %bitcast.208, s32[256]{0:T(256)S(1)} %bitcast.209, s32[256]{0:T(256)S(1)} %bitcast.210, s32[256]{0:T(256)S(1)} %bitcast.211, s32[256]{0:T(256)S(1)} %bitcast.212, s32[256]{0:T(256)S(1)} %bitcast.213, ...), kind=kOutput, calls=%fused_computation.75.clone.1 | convolution fusion | flops 553648128 | bytes 3166208 | tf_op jit(solution)/shard_map/while/body/eval_jaxpr/dot_general | solution.py:40
  164.1 1.9 %fusion.155 = bf16[4,256,1024]{2,1,0:T(8,128)(2,1)} fusion(bf16[4,256,1024]{2,1,0:T(8,128)(2,1)} %get-tuple-element.419, s32[]{:T(128)} %get-tuple-element.418, f32[256,1024]{1,0:T(8,128)S(1)} %fusion.151, f32[256,1024]{1,0:T(8,128)S(1)} %fusion.153, bf16[192,1024]{1,0:T(8,128)(2,1)S(1)} %get-tuple-element.437, f32[256]{0:T(256)S(1)} %add_add_fusion.2, ...), kind=kOutput, calls=%fused_computation.7.clone.1 | convolution fusion | flops 103284736 | bytes 3026432 | tf_op jit(solution)/shard_map/while/body/eval_jaxpr/dot_general | solution.py:36
  166.1 7.1 %maximum_convert_fusion = bf16[1024,1024]{1,0:T(8,128)(2,1)} fusion(f32[1024,1024]{1,0:T(8,128)} %fusion.130, f32[1024]{0:T(1024)S(1)} %convert_element_type.147, bf16[1024,1024]{1,0:T(8,128)(2,1)} %bitcast.56, bf16[1024,1024]{1,0:T(8,128)(2,1)} %param.14), kind=kOutput, calls=%fused_computation.228 | convolution fusion | flops 2151677952 | bytes 10489856 | tf_op jit(solution)/shard_map/dot_general | solution.py:81
  (87 shorter events, 5.9 us)
Async XLA Ops:
  0.0 100.3 %copy-start = (bf16[1024,1024]{1,0:T(8,128)(2,1)S(1)}, bf16[1024,1024]{1,0:T(8,128)(2,1)}, u32[]{:S(2)}) copy-start(bf16[1024,1024]{1,0:T(8,128)(2,1)} %param.13) | copy-start | bytes 6291460
  12.6 6.5 %copy-start.4 = (s32[6]{0:T(128)S(1)}, s32[6]{0:T(128)}, u32[]{:S(2)}) copy-start(s32[6]{0:T(128)} %param.16) | copy-start | bytes 76
  12.6 87.6 %copy-start.1 = (s32[1024,16]{0,1:T(8,128)S(1)}, s32[1024,16]{0,1:T(8,128)}, u32[]{:S(2)}) copy-start(s32[1024,16]{0,1:T(8,128)} %param.18) | copy-start | bytes 196612
  12.6 87.6 %copy-start.2 = (s32[1024,16]{0,1:T(8,128)S(1)}, s32[1024,16]{0,1:T(8,128)}, u32[]{:S(2)}) copy-start(s32[1024,16]{0,1:T(8,128)} %param.19) | copy-start | bytes 196612
  12.6 87.7 %copy-start.3 = (bf16[1024]{0:T(1024)(128)(2,1)S(1)}, bf16[1024]{0:T(1024)(128)(2,1)}, u32[]{:S(2)}) copy-start(bf16[1024]{0:T(1024)(128)(2,1)} %param.15) | copy-start | bytes 6148
  12.6 93.5 %all-to-all-start = ((bf16[8,128,1024]{2,1,0:T(8,128)(2,1)}), bf16[8,128,1024]{2,1,0:T(8,128)(2,1)}, u32[]{:S(2)}, u32[]{:S(2)}) async-start(bf16[8,128,1024]{2,1,0:T(8,128)(2,1)} %broadcast_select_fusion), calls=%async_computation | async-start | bytes 4194304 | tf_op jit(solution)/shard_map/all_to_all | solution.py:63
where the time goes:
time: 174 us; the launch traced here: 173 us
  blocking collectives  78.4 us (45%)
  matrix products  65.3 us (38%)
  local copies, waits for them, and re-layouts  17.5 us (10%)
  starting transfers between devices  6.47 us (4%)
  other arithmetic  5.1 us (3%)
    all_gather x1, blocking collectives, per_device(): lax.all_gather(mine, ('group', 'member'), axis=0, tiled=True)  78.4 us
    dot_general x4, matrix products, block_mean(): jnp.dot(local_counts, self_features, preferred_element_type=jnp.float32)  22.3 us
    dot_general x4, matrix products, block_mean(): jnp.dot(halo_counts, neighbour_positions, preferred_element_type=jnp.floa...  22.3 us
    gather x1, local copies, waits for them, and re-layouts, per_device(): jnp.take(features, send_rows.reshape(peers * caps), axis=0)  7.87 us
    dot_general x4, matrix products, block_mean(): jnp.dot(hub_counts, hub_lookup_matrix, preferred_element_type=jnp.float32)  7.72 us
    dot_general x1, matrix products, per_device(): jnp.dot(neigh_mean, w_neigh, preferred_element_type=jnp.float32)  7.11 us
    all_to_all x1, starting transfers between devices, per_device(): lax.all_to_all(outgoing, 'member', split_axis=0, concat_axis=0, tiled=True)  6.47 us
    dot_general x1, matrix products, per_device(): value = jnp.dot(features, w_self, preferred_element_type=jnp.float32)  5.85 us
  transfers between devices with their start and end apart: 1, of which 0 were waited for; matrix products, arithmetic and copies ran while one was open for 5% of the time, Pallas kernels for 0%

commit v1 on v0

v1 whole, which is shorter than its diff:
```python
import functools

import jax
import jax.numpy as jnp
from jax import lax
from jax.experimental import pallas as pl
from jax.experimental.pallas import tpu as pltpu
from jax.sharding import PartitionSpec as P

LANES = 128
HUB_PAD = 8
VM = pl.BlockSpec(memory_space=pltpu.VMEM)
SM = pl.BlockSpec(memory_space=pltpu.SMEM)


def call(kernel, out_shape, in_specs, limit, flops, bytes_accessed):
    single = not isinstance(out_shape, (list, tuple))
    return pl.pallas_call(
        kernel,
        out_shape=out_shape,
        in_specs=in_specs,
        out_specs=VM if single else [VM] * len(out_shape),
        compiler_params=pltpu.CompilerParams(vmem_limit_bytes=limit),
        cost_estimate=pl.CostEstimate(flops=flops, bytes_accessed=bytes_accessed, transcendentals=0),
    )


def gather_kernel(shifts, with_hub, splits, me_ref, rows_ref, hub_ref, feat_ref, *out_refs):
    me = me_ref[0]
    rows_here = feat_ref.shape[0]
    caps = rows_ref.shape[1]
    picks = []
    if with_hub:
        row_at = lax.broadcasted_iota(jnp.int32, (16, rows_here), 1)
        line = lax.broadcasted_iota(jnp.int32, (16, rows_here), 0)
        hit = jnp.zeros((16, rows_here), jnp.float32)
        for h in range(hub_ref.shape[0]):
            hit = hit + jnp.where((line == h) & (row_at == hub_ref[h]), 1.0, 0.0)
        picks.append(hit.astype(jnp.bfloat16))
    row_at = lax.broadcasted_iota(jnp.int32, (caps, rows_here), 1)
    for shift in shifts:
        wanted = rows_ref[pl.ds(me ^ shift, 1), :]
        wanted = jnp.transpose(jnp.broadcast_to(wanted, (8, caps)))[:, :1]
        picks.append(jnp.where(row_at == wanted, 1.0, 0.0).astype(jnp.bfloat16))
    picked = jnp.dot(
        jnp.concatenate(picks, axis=0), feat_ref[...], preferred_element_type=jnp.float32
    ).astype(jnp.bfloat16)
    at = 0
    out = 0
    if with_hub:
        out_refs[0][...] = picked[:HUB_PAD]
        at, out = 16, 1
    for shift in shifts:
        block = picked[at : at + caps]
        at += caps
        parts = splits.get(shift, 1)
        width = block.shape[1] // parts
        for part in range(parts):
            out_refs[out][...] = block[:, part * width : (part + 1) * width]
            out += 1


def add_counts(index, valid, offset, width, out_ref, row, column):
    rb, kmax = index.shape
    slot = lax.broadcasted_iota(jnp.int32, index.shape, 1)
    index = jnp.where(slot < valid, index, -1).astype(jnp.int16)
    columns = [jnp.broadcast_to(index[:, k : k + 1], (rb, LANES)) for k in range(kmax)]
    lane = lax.broadcasted_iota(jnp.int32, (rb, LANES), 1).astype(jnp.int16)
    one = jnp.ones((rb, LANES), jnp.bfloat16)
    zero = jnp.zeros((rb, LANES), jnp.bfloat16)
    for g in range(width // LANES):
        number = lane + jnp.asarray(offset + g * LANES, jnp.int16)
        total = zero
        for k in range(kmax):
            total = total + jnp.where(columns[k] == number, one, zero)
        out_ref[pl.ds(row, rb), column + g * LANES : column + (g + 1) * LANES] = total


def table_kernel(rb, peers, local_ref, hub_ref, halo_ref, deg_ref, local_out, hub_out, halo_out):
    def body(i, carry):
        row = pl.multiple_of(i * rb, rb)
        deg = deg_ref[pl.ds(row, rb), :]
        add_counts(local_ref[pl.ds(row, rb), :], deg[:, 0:1], 0, local_out.shape[1], local_out, row, 0)
        add_counts(hub_ref[pl.ds(row, rb), :], deg[:, 1:2], 0, hub_out.shape[1], hub_out, row, 0)
        add_counts(halo_ref[pl.ds(row, rb), :], deg[:, 2:3], 0, halo_out.shape[1], halo_out, row, 0)
        return carry

    lax.fori_loop(0, local_ref.shape[0] // rb, body, 0)


def own_kernel(rb, feat_ref, w_ref, bias_ref, out_ref):
    bias = bias_ref[...].astype(jnp.float32)

    def body(i, carry):
        row = pl.multiple_of(i * rb, rb)
        out_ref[pl.ds(row, rb), :] = (
            jnp.dot(feat_ref[pl.ds(row, rb), :], w_ref[...], preferred_element_type=jnp.float32) + bias
        )
        return carry

    lax.fori_loop(0, feat_ref.shape[0] // rb, body, 0)


def sum_kernel(rb, count, local_ref, hub_ref, halo_ref, feat_ref, table_ref, *refs):
    blocks, out_ref = refs[:count], refs[count]
    caps = blocks[0].shape[0]

    def body(i, carry):
        row = pl.multiple_of(i * rb, rb)
        total = jnp.dot(local_ref[pl.ds(row, rb), :], feat_ref[...], preferred_element_type=jnp.float32)
        total = total + jnp.dot(hub_ref[pl.ds(row, rb), :], table_ref[...], preferred_element_type=jnp.float32)
        for b in range(count):
            total = total + jnp.dot(
                halo_ref[pl.ds(row, rb), b * caps : (b + 1) * caps],
                blocks[b][...],
                preferred_element_type=jnp.float32,
            )
        out_ref[pl.ds(row, rb), :] = total
        return carry

    lax.fori_loop(0, local_ref.shape[0] // rb, body, 0)


def last_kernel(rb, parts, sum_ref, own_ref, halo_ref, deg_ref, w_ref, *refs):
    blocks, out_ref = refs[:parts], refs[parts]
    caps = blocks[0].shape[0]
    width = blocks[0].shape[1]
    at = halo_ref.shape[1] - caps

    def body(i, carry):
        row = pl.multiple_of(i * rb, rb)
        deg = deg_ref[pl.ds(row, rb), :]
        scale = 1.0 / (deg[:, 0:1] + deg[:, 1:2] + deg[:, 2:3]).astype(jnp.float32)
        value = own_ref[pl.ds(row, rb), :]
        for part in range(parts):
            span = slice(part * width, (part + 1) * width)
            total = sum_ref[pl.ds(row, rb), span] + jnp.dot(
                halo_ref[pl.ds(row, rb), at:], blocks[part][...], preferred_element_type=jnp.float32
            )
            mean = (total * scale).astype(jnp.bfloat16)
            value = value + jnp.dot(mean, w_ref[span, :], preferred_element_type=jnp.float32)
        out_ref[pl.ds(row, rb), :] = jnp.maximum(value, 0.0).astype(jnp.bfloat16)
        return carry

    lax.fori_loop(0, sum_ref.shape[0] // rb, body, 0)


def per_device(groups, features, w_self, w_neigh, bias, hub_rows, hub_nbrs, local_nbrs, halo_nbrs, degrees, send_rows):
    rows_here, width = features.shape
    peers, caps = send_rows.shape[1:]
    hub_dev = hub_rows.shape[0]
    bf16, f32 = jnp.bfloat16, jnp.float32
    me = lax.axis_index("member")
    group = lax.axis_index("group")
    me_arr = me.reshape(1).astype(jnp.int32)
    rows = send_rows.reshape(peers, caps)

    order = list(range(peers // 2, peers - 1)) + list(range(1, peers // 2)) + [0, peers - 1]
    early, late = order[:-1], order[-1]
    splits = {late: 2}

    def gather(shifts, with_hub):
        outs = [jax.ShapeDtypeStruct((HUB_PAD, width), bf16)] if with_hub else []
        for shift in shifts:
            parts = splits.get(shift, 1)
            outs += [jax.ShapeDtypeStruct((caps, width // parts), bf16)] * parts
        return call(
            functools.partial(gather_kernel, shifts, with_hub, splits),
            outs,
            [SM, VM, SM, VM],
            24 << 20,
            2 * len(shifts) * caps * rows_here * width,
            2 * rows_here * width + 2 * len(shifts) * caps * width,
        )(me_arr, rows, hub_rows, features)

    def swap(block, axis, size, shift):
        return lax.ppermute(block, axis, [(i, i ^ shift) for i in range(size)])

    first = gather(order[:1], True)
    hubs, sent = first[0], {order[0]: first[1:]}
    rest = gather(order[1:], False)
    at = 0
    for shift in order[1:]:
        parts = splits.get(shift, 1)
        sent[shift] = rest[at : at + parts]
        at += parts
    got = {}
    for shift in order:
        got[shift] = sent[shift] if shift == 0 else [swap(b, "member", peers, shift) for b in sent[shift]]

    bits = [("member", 1 << b) for b in range(1, peers.bit_length() - 1)]
    bits += [("group", 1 << b) for b in range(groups.bit_length() - 1)]
    bits += [("member", 1)]
    distance = {"member": jnp.int32(0), "group": jnp.int32(0)}
    owner = hub_nbrs // hub_dev
    apart = {"member": (owner % peers) ^ me, "group": (owner // peers) ^ group}
    block_at = jnp.zeros_like(hub_nbrs)
    for n, (axis, bit) in enumerate(bits):
        other = swap(hubs, axis, peers if axis == "member" else groups, bit)
        hubs = jnp.concatenate([hubs, other], axis=0)
        block_at = block_at + jnp.where((apart[axis] & bit) != 0, 1 << n, 0)
    hub_index = block_at * HUB_PAD + hub_nbrs % hub_dev
    halo_apart = (halo_nbrs // caps) ^ me
    halo_place = jnp.zeros_like(halo_nbrs)
    for n, shift in enumerate(order):
        halo_place = jnp.where(halo_apart == shift, n, halo_place)
    halo_index = halo_place * caps + halo_nbrs % caps
    deg = degrees.T

    hub_slots = hubs.shape[0]
    halo_slots = peers * caps
    local_counts, hub_counts, halo_counts = call(
        functools.partial(table_kernel, 64, peers),
        [
            jax.ShapeDtypeStruct((rows_here, rows_here), bf16),
            jax.ShapeDtypeStruct((rows_here, hub_slots), bf16),
            jax.ShapeDtypeStruct((rows_here, halo_slots), bf16),
        ],
        [VM] * 4,
        32 << 20,
        24 * rows_here * (rows_here + halo_slots),
        2 * rows_here * (rows_here + hub_slots + halo_slots),
    )(local_nbrs, hub_index, halo_index, deg)

    own = call(
        functools.partial(own_kernel, 256),
        jax.ShapeDtypeStruct((rows_here, width), f32),
        [VM] * 3,
        32 << 20,
        2 * rows_here * width * width,
        8 * rows_here * width,
    )(features, w_self, bias.reshape(1, width))

    total = call(
        functools.partial(sum_kernel, 256, len(early)),
        jax.ShapeDtypeStruct((rows_here, width), f32),
        [VM] * (5 + len(early)),
        40 << 20,
        2 * rows_here * width * (rows_here + hub_slots + halo_slots),
        8 * rows_here * width,
    )(local_counts, hub_counts, halo_counts, features, hubs, *[got[s][0] for s in early])

    return call(
        functools.partial(last_kernel, 256, splits[late]),
        jax.ShapeDtypeStruct((rows_here, width), bf16),
        [VM] * (5 + splits[late]),
        40 << 20,
        2 * rows_here * width * (width + caps),
        8 * rows_here * width,
    )(total, own, halo_counts, deg, w_neigh, *got[late])


def solution(mesh):
    both = ("group", "member")
    in_specs = (
        P(both, None),
        P(),
        P(),
        P(),
        P(both),
        P(both, None),
        P(both, None),
        P(both, None),
        P(None, both),
        P(both, None, None),
    )
    return jax.shard_map(
        functools.partial(per_device, mesh.shape["group"]),
        mesh=mesh,
        in_specs=in_specs,
        out_specs=P(both, None),
        check_vma=False,
    )
```

time: 174 us -> 110 us (0.63)
  the two profiles are of different devices: /device:TPU:0 before, /device:TPU:29 now
where the time goes in v1:
time: 110 us; the launch traced here: 109 us
  Pallas kernels  34.3 us (31%)
  waiting for transfers between devices  33.2 us (30%)
  local copies, waits for them, and re-layouts  19.5 us (18%)
  starting transfers between devices  17.2 us (16%)
  other arithmetic  4.74 us (4%)
    ppermute x13, waiting for transfers between devices, swap(): return lax.ppermute(block, axis, [(i, i ^ shift) for i in range(size)])  33.2 us
    unnamed x54, local copies, waits for them, and re-layouts  17.6 us
    ppermute x13, starting transfers between devices, swap(): return lax.ppermute(block, axis, [(i, i ^ shift) for i in range(size)])  17.2 us
    pallas_call x1, Pallas kernels, per_device(): call(functools.partial(table_kernel, 64, peers), [jax.ShapeDtypeStruct((r...  12.2 us
    pallas_call x1, Pallas kernels, per_device(): call(functools.partial(sum_kernel, 256, len(early)), jax.ShapeDtypeStruct...  8.24 us
    pallas_call x2, Pallas kernels, gather(): call(functools.partial(gather_kernel, shifts, with_hub, splits), outs, [S...  5.52 us
    pallas_call x1, Pallas kernels, per_device(): call(functools.partial(last_kernel, 256, splits[late]), jax.ShapeDtypeStr...  5.5 us
    pallas_call x1, Pallas kernels, per_device(): call(functools.partial(own_kernel, 256), jax.ShapeDtypeStruct((rows_here,...  2.84 us
  transfers between devices with their start and end apart: 13, of which 4 were waited for; matrix products, arithmetic and copies ran while one was open for 11% of the time, Pallas kernels for 25%

profile of v1, /device:TPU:29, one launch (start us, length us, event | category | flops | bytes accessed | tf_op | source)
XLA Modules:
  0.0 109.2 jit_solution(3491996547930119123)
XLA Ops:
  0.0 1.6 %copy-done = bf16[1024,1024]{1,0:T(8,128)(2,1)S(1)} copy-done((bf16[1024,1024]{1,0:T(8,128)(2,1)S(1)}, bf16[1024,1024]{1,0:T(8,128)(2,1)}, u32[]{:S(2)}) %copy-start) | copy-done | bytes 2097176
  2.9 1.9 %shard_map.101 = (bf16[8,1024]{1,0:T(8,128)(2,1)S(1)}, bf16[128,1024]{1,0:T(8,128)(2,1)}) custom-call(s32[1]{0:T(128)} %bitcast.1.me_ref, s32[8,128]{1,0:T(8,128)S(1)} %bitcast.5, s32[6]{0:T(128)S(1)} %copy-done.9, bf16[1024,1024]{1,0:T(8,128)(2,1)S(1)} %copy-done), custom_call_target="tpu_custom_call" | custom-call | flops 268435456 | bytes 2359296 | tf_op jit(solution)/shard_map/pallas_call | solution.py:167
  5.0 3.6 %shard_map.102 = (bf16[128,1024]{1,0:T(8,128)(2,1)}, bf16[128,1024]{1,0:T(8,128)(2,1)}, bf16[128,1024]{1,0:T(8,128)(2,1)}, bf16[128,1024]{1,0:T(8,128)(2,1)S(1)}...) custom-call(s32[1]{0:T(128)} %bitcast.1.me_ref, ...), custom_call_target="tpu_custom_call" | custom-call | flops 1879048192 | bytes 3932160 | tf_op jit(solution)/shard_map/pallas_call | solution.py:167
  8.7 3.5 %collective-permute-start.6 = (bf16[128,1024]{1,0:T(8,128)(2,1)}, bf16[128,1024]{1,0:T(8,128)(2,1)S(1)}, u32[]{:S(2)}, u32[]{:S(2)}) collective-permute-start(bf16[128,1024]{1,0:T(8,128)(2,1)} %get-tuple-element.23), channel_id=1, source_target_pairs={{0,5},{1,4},{2,7},{3,6},{4,1},{5,0},{6,3},{7,2},{8,13},{9,12},{10,... | collective-permute-start | bytes 786440 | tf_op jit(solution)/shard_map/ppermute | solution.py:177
  12.2 1.1 collective-permute-start.7
  15.1 2.3 %fusion.2.hub_ref = s32[1024,8]{1,0:T(8,128)S(1)} fusion(s32[1024,8]{1,0:T(8,128)} %copy.15, s32[1024,8]{1,0:T(8,128)S(1)} %copy.16, s32[1024,8]{1,0:T(8,128)S(1)} %copy.11, s32[]{:T(128)S(6)} %axis_index.25, s32[]{:T(128)} %axis_index.22), kind=kLoop, calls=%fused_computation.13 | loop fusion | flops 425984 | bytes 131080 | tf_op jit(solution)/shard_map/add | solution.py:202
  19.9 1.8 %copy.17 = s32[1024,16]{1,0:T(8,128)} copy(s32[1024,16]{0,1:T(8,128)} %param.17) | data formatting | bytes 131072 | tf_op args[7]
  22.7 19.8 %collective-permute-done.1 = bf16[16,1024]{1,0:T(8,128)(2,1)S(1)} collective-permute-done((bf16[16,1024]{1,0:T(8,128)(2,1)}, bf16[16,1024]{1,0:T(8,128)(2,1)S(1)}, u32[]{:S(2)}, u32[]{:S(2)}) %collective-permute-start.1) | collective-permute-done | bytes 32800 | tf_op jit(solution)/shard_map/ppermute | solution.py:177
  42.5 1.3 %collective-permute-start.2 = (bf16[32,1024]{1,0:T(8,128)(2,1)S(1)}, bf16[32,1024]{1,0:T(8,128)(2,1)S(1)}, u32[]{:S(2)}, u32[]{:S(2)}) collective-permute-start(bf16[32,1024]{1,0:T(8,128)(2,1)S(1)} %pad_maximum_fusion.1), channel_id=1, source_target_pairs={{0,8},{8,0},{16,24},{24,16},{1,9},{9,1},{17,25},{25,17},{2,10},{10... | collective-permute-start | bytes 196616 | tf_op jit(solution)/shard_map/ppermute | solution.py:177
  44.4 1.3 %collective-permute-done.2 = bf16[32,1024]{1,0:T(8,128)(2,1)S(1)} collective-permute-done((bf16[32,1024]{1,0:T(8,128)(2,1)S(1)}, bf16[32,1024]{1,0:T(8,128)(2,1)S(1)}, u32[]{:S(2)}, u32[]{:S(2)}) %collective-permute-start.2) | collective-permute-done | bytes 65568 | tf_op jit(solution)/shard_map/ppermute | solution.py:177
  47.2 2.4 %collective-permute-done.3 = bf16[64,1024]{1,0:T(8,128)(2,1)S(1)} collective-permute-done((bf16[64,1024]{1,0:T(8,128)(2,1)S(1)}, bf16[64,1024]{1,0:T(8,128)(2,1)S(1)}, u32[]{:S(2)}, u32[]{:S(2)}) %collective-permute-start.3) | collective-permute-done | bytes 131104 | tf_op jit(solution)/shard_map/ppermute | solution.py:177
  50.2 4.2 %collective-permute-start.4 = (bf16[128,1024]{1,0:T(8,128)(2,1)}, bf16[128,1024]{1,0:T(8,128)(2,1)S(1)}, u32[]{:S(2)}, u32[]{:S(2)}) collective-permute-start(bf16[128,1024]{1,0:T(8,128)(2,1)} %get-tuple-element.31), channel_id=1, source_target_pairs={{0,1},{1,0},{2,3},{3,2},{4,5},{5,4},{6,7},{7,6},{8,9},{9,8},{10,11... | collective-permute-start | bytes 786440 | tf_op jit(solution)/shard_map/ppermute | solution.py:177
  54.4 1.8 %fusion.4.halo_ref = s32[1024,16]{1,0:T(8,128)S(1)} fusion(s32[1024,16]{1,0:T(8,128)} %copy.17, s32[]{:T(128)} %axis_index.22), kind=kLoop, calls=%fused_computation.15 | loop fusion | flops 589824 | bytes 131076 | tf_op jit(solution)/shard_map/add | solution.py:207
  56.2 12.2 %shard_map.100 = (bf16[1024,1024]{1,0:T(8,128)(2,1)S(1)}, bf16[1024,256]{1,0:T(8,128)(2,1)S(1)}, bf16[1024,1024]{1,0:T(8,128)(2,1)S(1)}) custom-call(s32[1024,16]{1,0:T(8,128)S(1)} %copy.22.local_ref, s32[1024,8]{1,0:T(8,128)S(1)} %fusion.2.hub_ref, s32[1024,16]{1,0:T(8,128)S(1)} %fusion.4.halo_ref, s32[1024,3]{1,0:T(8,128)S(1)} %bitcast.3), custom_call_target="tpu_custom_call" | custom-call | flops 50331648 | bytes 4718592 | tf_op jit(solution)/shard_map/pallas_call | solution.py:212
  68.5 1.7 %collective-permute-start.10 = (bf16[128,1024]{1,0:T(8,128)(2,1)S(1)}, bf16[128,1024]{1,0:T(8,128)(2,1)S(1)}, u32[]{:S(2)}, u32[]{:S(2)}) collective-permute-start(bf16[128,1024]{1,0:T(8,128)(2,1)S(1)} %get-tuple-element.27), channel_id=1, source_target_pairs={{0,3},{1,2},{2,1},{3,0},{4,7},{5,6},{6,5},{7,4},{8,11},{9,10},{10,... | collective-permute-start | bytes 786440 | tf_op jit(solution)/shard_map/ppermute | solution.py:177
  70.2 2.8 %shard_map.104.own_ref = f32[1024,1024]{1,0:T(8,128)S(1)} custom-call(bf16[1024,1024]{1,0:T(8,128)(2,1)S(1)} %copy-done.1, bf16[1024,1024]{1,0:T(8,128)(2,1)S(1)} %copy-done.4, bf16[1,1024]{1,0:T(2,128)(2,1)S(1)} %reshape.11.bias_ref), custom_call_target="tpu_custom_call" | custom-call | flops 2147483648 | bytes 8388608 | tf_op jit(solution)/shard_map/pallas_call | solution.py:225
  73.8 1.1 collective-permute-start.11
  75.6 2.5 %collective-permute-start.12 = (bf16[128,512]{1,0:T(8,128)(2,1)S(1)}, bf16[128,512]{1,0:T(8,128)(2,1)S(1)}, u32[]{:S(2)}, u32[]{:S(2)}) collective-permute-start(bf16[128,512]{1,0:T(8,128)(2,1)S(1)} %copy-done.15), channel_id=1, source_target_pairs={{0,7},{1,6},{2,5},{3,4},{4,3},{5,2},{6,1},{7,0},{8,15},{9,14},{10,... | collective-permute-start | bytes 393224 | tf_op jit(solution)/shard_map/ppermute | solution.py:177
  78.0 9.7 %collective-permute-done.10.refs_5_ = bf16[128,1024]{1,0:T(8,128)(2,1)S(1)} collective-permute-done((bf16[128,1024]{1,0:T(8,128)(2,1)S(1)}, bf16[128,1024]{1,0:T(8,128)(2,1)S(1)}, u32[]{:S(2)}, u32[]{:S(2)}) %collective-permute-start.10) | collective-permute-done | bytes 262176 | tf_op jit(solution)/shard_map/ppermute | solution.py:177
  89.6 8.2 %shard_map.103.sum_ref = f32[1024,1024]{1,0:T(8,128)S(1)} custom-call(bf16[1024,1024]{1,0:T(8,128)(2,1)S(1)} %get-tuple-element.18.local_ref, bf16[1024,256]{1,0:T(8,128)(2,1)S(1)} %get-tuple-element.19.hub_ref, bf16[1024,1024]{1,0:T(8,128)(2,1)S(1)} %get-tuple-element.20.halo_ref, bf16[1024,1024]{1,0:T(8,128)(2,1)S(1)} %copy-done.1, ...), custom_call_target="tpu_custom_call" | custom-call | flops 4831838208 | bytes 8388608 | tf_op jit(solution)/shard_map/pallas_call | solution.py:234
  97.9 2.0 %copy-done.2 = f32[1024,1024]{1,0:T(8,128)} copy-done((f32[1024,1024]{1,0:T(8,128)}, f32[1024,1024]{1,0:T(8,128)S(1)}, u32[]{:S(2)}) %copy-start.2) | copy-done | bytes 4194328
  99.9 2.2 %copy-done.3 = f32[1024,1024]{1,0:T(8,128)S(1)} copy-done((f32[1024,1024]{1,0:T(8,128)S(1)}, f32[1024,1024]{1,0:T(8,128)}, u32[]{:S(2)}) %copy-start.3) | copy-done | bytes 4194328
  102.1 1.6 %copy-done.7 = bf16[1024,1024]{1,0:T(8,128)(2,1)S(1)} copy-done((bf16[1024,1024]{1,0:T(8,128)(2,1)S(1)}, bf16[1024,1024]{1,0:T(8,128)(2,1)}, u32[]{:S(2)}) %copy-start.7) | copy-done | bytes 2097176
  103.7 5.5 %shard_map.105 = bf16[1024,1024]{1,0:T(8,128)(2,1)} custom-call(f32[1024,1024]{1,0:T(8,128)S(1)} %copy-done.3, f32[1024,1024]{1,0:T(8,128)S(1)} %shard_map.104.own_ref, bf16[1024,1024]{1,0:T(8,128)(2,1)S(1)} %copy-done.7, s32[1024,3]{1,0:T(8,128)S(1)} %bitcast.4, bf16[1024,1024]{1,0:T(8,128)(2,1)S(1)} %copy-done.5, ...), custom_call_target="tpu_custom_call" | custom-call | flops 2415919104 | bytes 8388608 | tf_op jit(solution)/shard_map/pallas_call | solution.py:243
  (73 shorter events, 13.0 us)
Async XLA Ops:
  4.8 12.7 %collective-permute-start = (bf16[8,1024]{1,0:T(8,128)(2,1)S(1)}, bf16[8,1024]{1,0:T(8,128)(2,1)S(1)}, u32[]{:S(2)}, u32[]{:S(2)}) collective-permute-start(bf16[8,1024]{1,0:T(8,128)(2,1)S(1)} %get-tuple-element.21), channel_id=1, source_target_pairs={{0,2},{1,3},{2,0},{3,1},{4,6},{5,7},{6,4},{7,5},{8,10},{9,11},{10,... | collective-permute-start | bytes 49160 | tf_op jit(solution)/shard_map/ppermute | solution.py:177
  5.0 8.7 %copy-start.20 = (s32[1024,8]{0,1:T(8,128)S(1)}, s32[1024,8]{0,1:T(8,128)}, u32[]{:S(2)}) copy-start(s32[1024,8]{0,1:T(8,128)} %param.15) | copy-start | bytes 98308
  5.0 63.4 %collective-permute-start.5 = (bf16[128,1024]{1,0:T(8,128)(2,1)}, bf16[128,1024]{1,0:T(8,128)(2,1)S(1)}, u32[]{:S(2)}, u32[]{:S(2)}) collective-permute-start(bf16[128,1024]{1,0:T(8,128)(2,1)} %get-tuple-element.22), channel_id=1, source_target_pairs={{0,4},{1,5},{2,6},{3,7},{4,0},{5,1},{6,2},{7,3},{8,12},{9,13},{10,... | collective-permute-start | bytes 786440 | tf_op jit(solution)/shard_map/ppermute | solution.py:177
  8.7 9.4 %copy-start.18 = (bf16[128,1024]{1,0:T(8,128)(2,1)}, bf16[128,1024]{1,0:T(8,128)(2,1)S(1)}, u32[]{:S(2)}) copy-start(bf16[128,1024]{1,0:T(8,128)(2,1)S(1)} %get-tuple-element.28.refs_6_) | copy-start | bytes 786436
  8.7 11.2 %copy-start.14 = (bf16[128,512]{1,0:T(8,128)(2,1)}, bf16[128,512]{1,0:T(8,128)(2,1)S(1)}, u32[]{:S(2)}) copy-start(bf16[128,512]{1,0:T(8,128)(2,1)S(1)} %get-tuple-element.30) | copy-start | bytes 393220
  8.7 11.2 %copy-start.16 = (bf16[128,512]{1,0:T(8,128)(2,1)}, bf16[128,512]{1,0:T(8,128)(2,1)S(1)}, u32[]{:S(2)}) copy-start(bf16[128,512]{1,0:T(8,128)(2,1)S(1)} %get-tuple-element.29) | copy-start | bytes 393220
  8.7 11.0 %copy-start.22 = (bf16[1024]{0:T(1024)(128)(2,1)S(1)}, bf16[1024]{0:T(1024)(128)(2,1)}, u32[]{:S(2)}) copy-start(bf16[1024]{0:T(1024)(128)(2,1)} %param.13) | copy-start | bytes 6148
  8.7 11.0 %copy-start.21 = (s32[1024,16]{0,1:T(8,128)S(1)}, s32[1024,16]{0,1:T(8,128)}, u32[]{:S(2)}) copy-start(s32[1024,16]{0,1:T(8,128)} %param.16) | copy-start | bytes 196612
  8.7 64.3 %collective-permute-start.6 = (bf16[128,1024]{1,0:T(8,128)(2,1)}, bf16[128,1024]{1,0:T(8,128)(2,1)S(1)}, u32[]{:S(2)}, u32[]{:S(2)}) collective-permute-start(bf16[128,1024]{1,0:T(8,128)(2,1)} %get-tuple-element.23), channel_id=1, source_target_pairs={{0,5},{1,4},{2,7},{3,6},{4,1},{5,0},{6,3},{7,2},{8,13},{9,12},{10,... | collective-permute-start | bytes 786440 | tf_op jit(solution)/shard_map/ppermute | solution.py:177
  12.2 62.6 %collective-permute-start.7 = (bf16[128,1024]{1,0:T(8,128)(2,1)}, bf16[128,1024]{1,0:T(8,128)(2,1)S(1)}, u32[]{:S(2)}, u32[]{:S(2)}) collective-permute-start(bf16[128,1024]{1,0:T(8,128)(2,1)} %get-tuple-element.24), channel_id=1, source_target_pairs={{0,6},{1,7},{2,4},{3,5},{4,2},{5,3},{6,0},{7,1},{8,14},{9,15},{10,... | collective-permute-start | bytes 786440 | tf_op jit(solution)/shard_map/ppermute | solution.py:177
  13.3 64.8 %collective-permute-start.8 = (bf16[128,1024]{1,0:T(8,128)(2,1)}, bf16[128,1024]{1,0:T(8,128)(2,1)}, u32[]{:S(2)}, u32[]{:S(2)}) collective-permute-start(bf16[128,1024]{1,0:T(8,128)(2,1)} %get-tuple-element.25), channel_id=1, source_target_pairs={{0,1},{1,0},{2,3},{3,2},{4,5},{5,4},{6,7},{7,6},{8,9},{9,8},{10,11... | collective-permute-start | bytes 786440 | tf_op jit(solution)/shard_map/ppermute | solution.py:177
  18.1 24.4 %collective-permute-start.1 = (bf16[16,1024]{1,0:T(8,128)(2,1)}, bf16[16,1024]{1,0:T(8,128)(2,1)S(1)}, u32[]{:S(2)}, u32[]{:S(2)}) collective-permute-start(bf16[16,1024]{1,0:T(8,128)(2,1)} %pad_maximum_fusion.2), channel_id=1, source_target_pairs={{0,4},{1,5},{2,6},{3,7},{4,0},{5,1},{6,2},{7,3},{8,12},{9,13},{10,... | collective-permute-start | bytes 98312 | tf_op jit(solution)/shard_map/ppermute | solution.py:177
  42.5 27.7 %copy-start.4 = (bf16[1024,1024]{1,0:T(8,128)(2,1)S(1)}, bf16[1024,1024]{1,0:T(8,128)(2,1)}, u32[]{:S(2)}) copy-start(bf16[1024,1024]{1,0:T(8,128)(2,1)} %w_ref.2) | copy-start | bytes 6291460
  42.5 27.7 %copy-start.1 = (bf16[1024,1024]{1,0:T(8,128)(2,1)S(1)}, bf16[1024,1024]{1,0:T(8,128)(2,1)}, u32[]{:S(2)}) copy-start(bf16[1024,1024]{1,0:T(8,128)(2,1)} %feat_ref.7) | copy-start | bytes 6291460
  42.5 3.2 %collective-permute-start.2 = (bf16[32,1024]{1,0:T(8,128)(2,1)S(1)}, bf16[32,1024]{1,0:T(8,128)(2,1)S(1)}, u32[]{:S(2)}, u32[]{:S(2)}) collective-permute-start(bf16[32,1024]{1,0:T(8,128)(2,1)S(1)} %pad_maximum_fusion.1), channel_id=1, source_target_pairs={{0,8},{8,0},{16,24},{24,16},{1,9},{9,1},{17,25},{25,17},{2,10},{10... | collective-permute-start | bytes 196616 | tf_op jit(solution)/shard_map/ppermute | solution.py:177
  45.7 3.9 %collective-permute-start.3 = (bf16[64,1024]{1,0:T(8,128)(2,1)S(1)}, bf16[64,1024]{1,0:T(8,128)(2,1)S(1)}, u32[]{:S(2)}, u32[]{:S(2)}) collective-permute-start(bf16[64,1024]{1,0:T(8,128)(2,1)S(1)} %pad_maximum_fusion), channel_id=1, source_target_pairs={{0,16},{8,24},{16,0},{24,8},{1,17},{9,25},{17,1},{25,9},{2,18},{10... | collective-permute-start | bytes 393224 | tf_op jit(solution)/shard_map/ppermute | solution.py:177
  50.2 18.2 %collective-permute-start.4 = (bf16[128,1024]{1,0:T(8,128)(2,1)}, bf16[128,1024]{1,0:T(8,128)(2,1)S(1)}, u32[]{:S(2)}, u32[]{:S(2)}) collective-permute-start(bf16[128,1024]{1,0:T(8,128)(2,1)} %get-tuple-element.31), channel_id=1, source_target_pairs={{0,1},{1,0},{2,3},{3,2},{4,5},{5,4},{6,7},{7,6},{8,9},{9,8},{10,11... | collective-permute-start | bytes 786440 | tf_op jit(solution)/shard_map/ppermute | solution.py:177
  68.4 19.4 %copy-start.6 = (bf16[1024,1024]{1,0:T(8,128)(2,1)}, bf16[1024,1024]{1,0:T(8,128)(2,1)S(1)}, u32[]{:S(2)}) copy-start(bf16[1024,1024]{1,0:T(8,128)(2,1)S(1)} %get-tuple-element.20.halo_ref) | copy-start | bytes 6291460
  68.4 9.6 %collective-permute-start.9 = (bf16[128,1024]{1,0:T(8,128)(2,1)S(1)}, bf16[128,1024]{1,0:T(8,128)(2,1)S(1)}, u32[]{:S(2)}, u32[]{:S(2)}) collective-permute-start(bf16[128,1024]{1,0:T(8,128)(2,1)S(1)} %get-tuple-element.26), channel_id=1, source_target_pairs={{0,2},{1,3},{2,0},{3,1},{4,6},{5,7},{6,4},{7,5},{8,10},{9,11},{10,... | collective-permute-start | bytes 786440 | tf_op jit(solution)/shard_map/ppermute | solution.py:177
  68.5 19.2 %copy-start.19 = (bf16[128,1024]{1,0:T(8,128)(2,1)S(1)}, bf16[128,1024]{1,0:T(8,128)(2,1)}, u32[]{:S(2)}) copy-start(bf16[128,1024]{1,0:T(8,128)(2,1)} %copy-done.18) | copy-start | bytes 786436
  68.5 19.2 %collective-permute-start.10 = (bf16[128,1024]{1,0:T(8,128)(2,1)S(1)}, bf16[128,1024]{1,0:T(8,128)(2,1)S(1)}, u32[]{:S(2)}, u32[]{:S(2)}) collective-permute-start(bf16[128,1024]{1,0:T(8,128)(2,1)S(1)} %get-tuple-element.27), channel_id=1, source_target_pairs={{0,3},{1,2},{2,1},{3,0},{4,7},{5,6},{6,5},{7,4},{8,11},{9,10},{10,... | collective-permute-start | bytes 786440 | tf_op jit(solution)/shard_map/ppermute | solution.py:177
  73.8 26.1 %collective-permute-start.11 = (bf16[128,512]{1,0:T(8,128)(2,1)S(1)}, bf16[128,512]{1,0:T(8,128)(2,1)S(1)}, u32[]{:S(2)}, u32[]{:S(2)}) collective-permute-start(bf16[128,512]{1,0:T(8,128)(2,1)S(1)} %copy-done.17), channel_id=1, source_target_pairs={{0,7},{1,6},{2,5},{3,4},{4,3},{5,2},{6,1},{7,0},{8,15},{9,14},{10,... | collective-permute-start | bytes 393224 | tf_op jit(solution)/shard_map/ppermute | solution.py:177
  75.6 24.3 %collective-permute-start.12 = (bf16[128,512]{1,0:T(8,128)(2,1)S(1)}, bf16[128,512]{1,0:T(8,128)(2,1)S(1)}, u32[]{:S(2)}, u32[]{:S(2)}) collective-permute-start(bf16[128,512]{1,0:T(8,128)(2,1)S(1)} %copy-done.15), channel_id=1, source_target_pairs={{0,7},{1,6},{2,5},{3,4},{4,3},{5,2},{6,1},{7,0},{8,15},{9,14},{10,... | collective-permute-start | bytes 393224 | tf_op jit(solution)/shard_map/ppermute | solution.py:177
  89.6 10.2 %copy-start.5 = (bf16[1024,1024]{1,0:T(8,128)(2,1)S(1)}, bf16[1024,1024]{1,0:T(8,128)(2,1)}, u32[]{:S(2)}) copy-start(bf16[1024,1024]{1,0:T(8,128)(2,1)} %w_ref.3) | copy-start | bytes 6291460
  (12 other events, 24.3 us)

commit v2 on v0

v2 whole, which is shorter than its diff:
```python
import functools

import jax
import jax.numpy as jnp
from jax import lax
from jax.experimental import pallas as pl
from jax.experimental.pallas import tpu as pltpu
from jax.sharding import PartitionSpec as P

LANES = 128
HUB_PAD = 8
VM = pl.BlockSpec(memory_space=pltpu.VMEM)
ANY = pl.BlockSpec(memory_space=pl.ANY)
SM = pl.BlockSpec(memory_space=pltpu.SMEM)
BF, F32 = jnp.bfloat16, jnp.float32


def call(kernel, out_shape, in_specs, limit, flops, bytes_accessed, scratch=(), out_specs=None, aliases=None):
    single = not isinstance(out_shape, (list, tuple))
    return pl.pallas_call(
        kernel,
        out_shape=out_shape,
        in_specs=in_specs,
        out_specs=out_specs or (VM if single else [VM] * len(out_shape)),
        scratch_shapes=list(scratch),
        input_output_aliases=aliases or {},
        compiler_params=pltpu.CompilerParams(vmem_limit_bytes=limit),
        cost_estimate=pl.CostEstimate(flops=flops, bytes_accessed=bytes_accessed, transcendentals=0),
    )


def column_of(row, rows):
    return jnp.transpose(jnp.broadcast_to(row, (8, rows)))[:, :1]


def pick_matrix(rows_ref, shift, rows_here):
    me = lax.axis_index("member")
    caps = rows_ref.shape[1]
    wanted = column_of(rows_ref[pl.ds(me ^ shift, 1), :], caps)
    row_at = lax.broadcasted_iota(jnp.int32, (caps, rows_here), 1)
    return jnp.where(row_at == wanted, 1.0, 0.0).astype(BF)


def hub_matrix(hub_ref, rows_here):
    row_at = lax.broadcasted_iota(jnp.int32, (HUB_PAD, rows_here), 1)
    line = lax.broadcasted_iota(jnp.int32, (HUB_PAD, rows_here), 0)
    hit = jnp.zeros((HUB_PAD, rows_here), F32)
    for h in range(hub_ref.shape[0]):
        hit = hit + jnp.where((line == h) & (row_at == hub_ref[h]), 1.0, 0.0)
    return hit.astype(BF)


def first_kernel(shifts, chunks, rows_hbm, hub_hbm, feat_hbm, *refs):
    outs, hub_out = refs[: len(shifts)], refs[len(shifts)]
    rows_ref, hub_ref, feat_ref, sems = refs[len(shifts) + 1 :]
    rows_here = feat_ref.shape[0]
    part = rows_here // chunks
    copies = [
        pltpu.make_async_copy(rows_hbm, rows_ref, sems.at[0]),
        pltpu.make_async_copy(hub_hbm, hub_ref, sems.at[1]),
    ]
    for c in range(chunks):
        span = pl.ds(c * part, part)
        copies.append(pltpu.make_async_copy(feat_hbm.at[span, :], feat_ref.at[span, :], sems.at[2 + c]))
    for copy in copies:
        copy.start()
    copies[0].wait()
    copies[1].wait()
    picks = [pick_matrix(rows_ref, shift, rows_here) for shift in shifts]
    picks.append(hub_matrix(hub_ref, rows_here))
    for copy in copies[2:]:
        copy.wait()
    caps = rows_ref.shape[1]
    picked = jnp.dot(jnp.concatenate(picks, axis=0), feat_ref[...], preferred_element_type=F32).astype(BF)
    hubs = picked[len(shifts) * caps :]
    hub_out[...] = hubs
    for n in range(len(shifts)):
        outs[n][...] = jnp.concatenate([picked[n * caps : (n + 1) * caps], hubs], axis=0)


def rest_kernel(shifts, parts, rows_ref, feat_ref, *outs):
    rows_here, width = feat_ref.shape
    caps = rows_ref.shape[1]
    picks = [pick_matrix(rows_ref, shift, rows_here) for shift in shifts]
    picked = jnp.dot(jnp.concatenate(picks, axis=0), feat_ref[...], preferred_element_type=F32).astype(BF)
    for n in range(len(shifts) - 1):
        outs[n][...] = picked[n * caps : (n + 1) * caps]
    for p in range(parts):
        outs[len(shifts) - 1 + p][...] = picked[-caps:, p * (width // parts) : (p + 1) * (width // parts)]


def join_kernel(caps, *refs):
    out_ref = refs[-1]
    at = 0
    for ref in refs[:-1]:
        start = caps if ref.shape[0] == caps + HUB_PAD else 0
        size = ref.shape[0] - start
        out_ref[at : at + size, :] = ref[start:, :]
        at += size


def add_counts(index, width, out_ref, row, column):
    rb, kmax = index.shape
    index = index.astype(jnp.int16)
    columns = [jnp.broadcast_to(index[:, k : k + 1], (rb, LANES)) for k in range(kmax)]
    lane = lax.broadcasted_iota(jnp.int32, (rb, LANES), 1).astype(jnp.int16)
    one = jnp.ones((rb, LANES), BF)
    zero = jnp.zeros((rb, LANES), BF)
    for g in range(width // LANES):
        number = lane + jnp.asarray(g * LANES, jnp.int16)
        total = zero
        for k in range(kmax):
            total = total + jnp.where(columns[k] == number, one, zero)
        out_ref[pl.ds(row, rb), column + g * LANES : column + (g + 1) * LANES] = total


def table_kernel(rb, peers, caps, hub_dev, magic, local_ref, hub_ref, halo_ref, deg_ref, out_ref):
    me = lax.axis_index("member")
    group = lax.axis_index("group")
    rows_here = local_ref.shape[1]
    halo_slots = peers * caps
    hub_slots = out_ref.shape[1] - rows_here - halo_slots
    near = hub_slots // (2 * HUB_PAD)
    half = peers // 2

    def body(i, carry):
        row = pl.multiple_of(i * rb, rb)
        span = pl.ds(row, rb)

        def masked(ref, which, index):
            slot = lax.broadcasted_iota(jnp.int32, index.shape, 0)
            index = jnp.where(slot < deg_ref[which : which + 1, span], index, -1)
            return jnp.transpose(index)

        local = masked(local_ref, 0, local_ref[:, span])
        hub = hub_ref[:, span]
        owner = (hub * magic) >> 16
        apart = (owner & (peers - 1)) ^ me
        line = (owner >> (peers.bit_length() - 1)) ^ group
        place = (apart & 1) * near + line * half + (apart >> 1)
        hub = masked(hub_ref, 1, place * HUB_PAD + hub - owner * hub_dev)
        halo = masked(halo_ref, 2, halo_ref[:, span] ^ (me * caps))
        add_counts(local, rows_here, out_ref, row, 0)
        add_counts(hub, hub_slots, out_ref, row, rows_here)
        add_counts(halo, halo_slots, out_ref, row, rows_here + hub_slots)
        return carry

    lax.fori_loop(0, rows_here // rb, body, 0)


def own_kernel(rb, feat_ref, w_ref, bias_ref, count_ref, own_ref, sum_ref):
    bias = bias_ref[...].astype(F32)
    rows_here = feat_ref.shape[0]

    def body(i, carry):
        span = pl.ds(pl.multiple_of(i * rb, rb), rb)
        own_ref[span, :] = jnp.dot(feat_ref[span, :], w_ref[...], preferred_element_type=F32) + bias
        sum_ref[span, :] = jnp.dot(count_ref[span, :rows_here], feat_ref[...], preferred_element_type=F32)
        return carry

    lax.fori_loop(0, rows_here // rb, body, 0)


def sum_kernel(rb, caps, blocks, sum_ref, count_ref, *refs):
    parts, out_ref, joined = refs[:blocks], refs[blocks], refs[blocks + 1]
    rows_here = sum_ref.shape[0]
    at = 0
    for ref in parts:
        size = caps if ref.shape[0] == caps + HUB_PAD else ref.shape[0]
        joined[at : at + size, :] = ref[:size, :]
        at += size

    def body(i, carry):
        span = pl.ds(pl.multiple_of(i * rb, rb), rb)
        out_ref[span, :] = sum_ref[span, :] + jnp.dot(
            count_ref[span, rows_here : rows_here + at], joined[...], preferred_element_type=F32
        )
        return carry

    lax.fori_loop(0, rows_here // rb, body, 0)


def mean_part(span, cols, sum_ref, count_ref, deg_ref, block_ref, w_ref, value):
    caps = block_ref.shape[0]
    deg = deg_ref[0:1, span] + deg_ref[1:2, span] + deg_ref[2:3, span]
    scale = column_of(1.0 / deg.astype(F32), deg.shape[1])
    at = count_ref.shape[1] - caps
    total = sum_ref[span, cols] + jnp.dot(count_ref[span, at:], block_ref[...], preferred_element_type=F32)
    mean = (total * scale).astype(BF)
    return value + jnp.dot(mean, w_ref[cols, :], preferred_element_type=F32)


def late_kernel(rb, cols, own_ref, sum_ref, count_ref, deg_ref, w_ref, block_ref, out_ref):
    def body(i, carry):
        span = pl.ds(pl.multiple_of(i * rb, rb), rb)
        out_ref[span, :] = mean_part(span, cols, sum_ref, count_ref, deg_ref, block_ref, w_ref, own_ref[span, :])
        return carry

    lax.fori_loop(0, sum_ref.shape[0] // rb, body, 0)


def last_kernel(rb, cols, own_ref, sum_ref, count_ref, deg_ref, w_ref, block_ref, out_hbm, out_ref, sems):
    steps = sum_ref.shape[0] // rb
    copies = []
    for i in range(steps):
        span = pl.ds(i * rb, rb)
        value = mean_part(span, cols, sum_ref, count_ref, deg_ref, block_ref, w_ref, own_ref[span, :])
        out_ref[span, :] = jnp.maximum(value, 0.0).astype(BF)
        copies.append(pltpu.make_async_copy(out_ref.at[span, :], out_hbm.at[span, :], sems.at[i]))
        copies[-1].start()
    for copy in copies:
        copy.wait()


def per_device(groups, features, w_self, w_neigh, bias, hub_rows, hub_nbrs, local_nbrs, halo_nbrs, degrees, send_rows):
    rows_here, width = features.shape
    peers, caps = send_rows.shape[1:]
    hub_dev = hub_rows.shape[0]
    hubs_all = hub_dev * peers * groups
    magic = -(-(1 << 16) // hub_dev)
    assert all((h * magic) >> 16 == h // hub_dev for h in range(hubs_all))
    assert peers & (peers - 1) == 0 and groups & (groups - 1) == 0
    rows = send_rows.reshape(peers, caps)
    vec = functools.partial(jax.ShapeDtypeStruct)

    evens = [s for s in range(peers // 2, peers, 2)] + [s for s in range(2, peers // 2, 2)]
    last = peers - 1
    odds = [s for s in range(peers // 2 + 1, peers - 1, 2)] + [s for s in range(1, peers // 2, 2)]
    parts = 2

    def swap(block, axis, shift):
        size = peers if axis == "member" else groups
        return lax.ppermute(block, axis, [(i, i ^ shift) for i in range(size)])

    chunks = 4
    firsts = call(
        functools.partial(first_kernel, evens, chunks),
        [vec((caps + HUB_PAD, width), BF)] * len(evens) + [vec((HUB_PAD, width), BF)],
        [ANY] * 3,
        16 << 20,
        2 * len(evens) * caps * rows_here * width,
        2 * rows_here * width,
        scratch=[
            pltpu.VMEM((peers, caps), jnp.int32),
            pltpu.SMEM((hub_dev,), jnp.int32),
            pltpu.VMEM((rows_here, width), BF),
            pltpu.SemaphoreType.DMA((2 + chunks,)),
        ],
    )(rows, hub_rows, features)
    got = {shift: swap(block, "member", shift) for shift, block in zip(evens, firsts)}
    others = odds + [0, last]
    rest = call(
        functools.partial(rest_kernel, others, parts),
        [vec((caps, width), BF)] * (len(others) - 1) + [vec((caps, width // parts), BF)] * parts,
        [VM] * 2,
        16 << 20,
        2 * len(others) * caps * rows_here * width,
        2 * rows_here * width,
    )(rows, features)
    for shift, block in zip(odds, rest):
        got[shift] = swap(block, "member", shift)
    got[0] = rest[len(odds)]
    late = [swap(block, "member", last) for block in rest[len(odds) + 1 :]]

    def join(*blocks):
        total = sum(HUB_PAD if b.shape[0] == caps + HUB_PAD else b.shape[0] for b in blocks)
        return call(
            functools.partial(join_kernel, caps), vec((total, width), BF), [VM] * len(blocks), 4 << 20, 0, 4 * total * width
        )(*blocks)

    hubs = join(firsts[-1], *[got[s] for s in range(2, peers, 2)])
    for bit in range(groups.bit_length() - 1):
        hubs = join(hubs, swap(hubs, "group", 1 << bit))
    other_hubs = swap(hubs, "member", 1)

    hub_slots = 2 * hubs.shape[0]
    counts = call(
        functools.partial(table_kernel, LANES, peers, caps, hub_dev, magic),
        vec((rows_here, rows_here + hub_slots + peers * caps), BF),
        [VM] * 4,
        16 << 20,
        24 * rows_here * (rows_here + peers * caps),
        2 * rows_here * (rows_here + hub_slots + peers * caps),
    )(local_nbrs.T, hub_nbrs.T, halo_nbrs.T, degrees)

    own, local_sum = call(
        functools.partial(own_kernel, 256),
        [vec((rows_here, width), F32)] * 2,
        [VM] * 4,
        16 << 20,
        4 * rows_here * width * width,
        8 * rows_here * width,
    )(features, w_self, bias.reshape(1, width), counts)

    early = [hubs, other_hubs] + [got[s] for s in range(last)]
    total = call(
        functools.partial(sum_kernel, 256, caps, len(early)),
        vec((rows_here, width), F32),
        [VM] * (2 + len(early)),
        16 << 20,
        2 * rows_here * width * (hub_slots + last * caps),
        8 * rows_here * width,
        scratch=[pltpu.VMEM((hub_slots + last * caps, width), BF)],
    )(local_sum, counts, *early)

    step = width // parts
    value = own
    for p in range(parts - 1):
        value = call(
            functools.partial(late_kernel, 256, slice(p * step, (p + 1) * step)),
            vec((rows_here, width), F32),
            [VM] * 6,
            16 << 20,
            2 * rows_here * step * (width + caps),
            8 * rows_here * width,
        )(value, total, counts, degrees, w_neigh, late[p])
    return call(
        functools.partial(last_kernel, 256, slice((parts - 1) * step, width)),
        vec((rows_here, width), BF),
        [VM] * 6,
        16 << 20,
        2 * rows_here * step * (width + caps),
        8 * rows_here * width,
        scratch=[pltpu.VMEM((rows_here, width), BF), pltpu.SemaphoreType.DMA((rows_here // 256,))],
        out_specs=ANY,
    )(value, total, counts, degrees, w_neigh, late[-1])


def solution(mesh):
    both = ("group", "member")
    in_specs = (
        P(both, None),
        P(),
        P(),
        P(),
        P(both),
        P(both, None),
        P(both, None),
        P(both, None),
        P(None, both),
        P(both, None, None),
    )
    return jax.shard_map(
        functools.partial(per_device, mesh.shape["group"]),
        mesh=mesh,
        in_specs=in_specs,
        out_specs=P(both, None),
        check_vma=False,
    )
```

time: 174 us -> 71.3 us (0.41)
  the two profiles are of different devices: /device:TPU:0 before, /device:TPU:1 now
where the time goes in v2:
time: 71.3 us; the launch traced here: 71.1 us
  Pallas kernels  27.5 us (39%)
  starting transfers between devices  20.6 us (29%)
  waiting for transfers between devices  19.9 us (28%)
  local copies, waits for them, and re-layouts  2.97 us (4%)
    ppermute x11, starting transfers between devices, swap(): return lax.ppermute(block, axis, [(i, i ^ shift) for i in range(size)])  20.6 us
    ppermute x11, waiting for transfers between devices, swap(): return lax.ppermute(block, axis, [(i, i ^ shift) for i in range(size)])  19.9 us
    pallas_call x1, Pallas kernels, per_device(): call(functools.partial(table_kernel, LANES, peers, caps, hub_dev, magic),...  9.48 us
    pallas_call x1, Pallas kernels, per_device(): call(functools.partial(own_kernel, 256), [vec((rows_here, width), F32)] *...  5 us
    pallas_call x1, Pallas kernels, per_device(): call(functools.partial(sum_kernel, 256, caps, len(early)), vec((rows_here...  3.53 us
    unnamed x20, local copies, waits for them, and re-layouts  2.96 us
    pallas_call x1, Pallas kernels, per_device(): call(functools.partial(last_kernel, 256, slice((parts - 1) * step, width)...  2.82 us
    pallas_call x1, Pallas kernels, per_device(): call(functools.partial(late_kernel, 256, slice(p * step, (p + 1) * step))...  2.79 us
  transfers between devices with their start and end apart: 11, of which 3 were waited for; matrix products, arithmetic and copies ran while one was open for 0% of the time, Pallas kernels for 32%

profile of v2, /device:TPU:1, one launch (start us, length us, event | category | flops | bytes accessed | tf_op | source)
XLA Modules:
  0.0 71.1 jit_solution(2548486706965993459)
XLA Ops:
  0.0 1.6 %copy-done.5 = bf16[1024,1024]{1,0:T(8,128)(2,1)S(1)} copy-done((bf16[1024,1024]{1,0:T(8,128)(2,1)S(1)}, bf16[1024,1024]{1,0:T(8,128)(2,1)}, u32[]{:S(2)}) %copy-start.5) | copy-done | bytes 2097176
  1.6 0.7 copy-done.7
  2.3 0.7 copy-done.8
  3.0 2.0 %shard_map.102 = (bf16[136,1024]{1,0:T(8,128)(2,1)S(1)}, bf16[136,1024]{1,0:T(8,128)(2,1)S(1)}, bf16[136,1024]{1,0:T(8,128)(2,1)S(1)}, bf16[8,1024]{1,0:T(8,128)(2,1)S(1)}) custom-call(s32[8,128]{1,0:T(8,128)S(1)} %bitcast.7, s32[6]{0:T(128)S(1)} %copy-done.8, bf16[1024,1024]{1,0:T(8,128)(2,1)S(1)} %copy-done.5), custom_call_target="tpu_custom_call" | custom-call | flops 805306368 | bytes 2097152 | tf_op jit(solution)/shard_map/pallas_call | solution.py:236
  4.9 2.2 %collective-permute-start = (bf16[136,1024]{1,0:T(8,128)(2,1)S(1)}, bf16[136,1024]{1,0:T(8,128)(2,1)S(1)}, u32[]{:S(2)}, u32[]{:S(2)}) collective-permute-start(bf16[136,1024]{1,0:T(8,128)(2,1)S(1)} %get-tuple-element.20), channel_id=1, source_target_pairs={{0,2},{1,3},{2,0},{3,1},{4,6},{5,7},{6,4},{7,5},{8,10},{9,11},{10,... | collective-permute-start | bytes 835592 | tf_op jit(solution)/shard_map/ppermute | solution.py:233
  7.1 2.3 %collective-permute-start.1 = (bf16[136,1024]{1,0:T(8,128)(2,1)S(1)}, bf16[136,1024]{1,0:T(8,128)(2,1)S(1)}, u32[]{:S(2)}, u32[]{:S(2)}) collective-permute-start(bf16[136,1024]{1,0:T(8,128)(2,1)S(1)} %get-tuple-element.21), channel_id=1, source_target_pairs={{0,4},{1,5},{2,6},{3,7},{4,0},{5,1},{6,2},{7,3},{8,12},{9,13},{10,... | collective-permute-start | bytes 835592 | tf_op jit(solution)/shard_map/ppermute | solution.py:233
  9.4 0.0 collective-permute-start.2
  9.4 9.3 %collective-permute-done.refs_1_.refs_4_ = bf16[136,1024]{1,0:T(8,128)(2,1)S(1)} collective-permute-done((bf16[136,1024]{1,0:T(8,128)(2,1)S(1)}, bf16[136,1024]{1,0:T(8,128)(2,1)S(1)}, u32[]{:S(2)}, u32[]{:S(2)}) %collective-permute-start) | collective-permute-done | bytes 278560 | tf_op jit(solution)/shard_map/ppermute | solution.py:233
  18.7 8.7 %collective-permute-done.2.refs_3_.refs_8_ = bf16[136,1024]{1,0:T(8,128)(2,1)S(1)} collective-permute-done((bf16[136,1024]{1,0:T(8,128)(2,1)S(1)}, bf16[136,1024]{1,0:T(8,128)(2,1)S(1)}, u32[]{:S(2)}, u32[]{:S(2)}) %collective-permute-start.2) | collective-permute-done | bytes 278560 | tf_op jit(solution)/shard_map/ppermute | solution.py:233
  27.4 1.2 %collective-permute-start.3 = (bf16[32,1024]{1,0:T(8,128)(2,1)S(1)}, bf16[32,1024]{1,0:T(8,128)(2,1)S(1)}, u32[]{:S(2)}, u32[]{:S(2)}) collective-permute-start(bf16[32,1024]{1,0:T(8,128)(2,1)S(1)} %shard_map.103.refs_0_), channel_id=1, source_target_pairs={{0,8},{8,0},{16,24},{24,16},{1,9},{9,1},{17,25},{25,17},{2,10},{10... | collective-permute-start | bytes 196616 | tf_op jit(solution)/shard_map/ppermute | solution.py:233
  28.6 1.9 %collective-permute-done.3.refs_1_ = bf16[32,1024]{1,0:T(8,128)(2,1)S(1)} collective-permute-done((bf16[32,1024]{1,0:T(8,128)(2,1)S(1)}, bf16[32,1024]{1,0:T(8,128)(2,1)S(1)}, u32[]{:S(2)}, u32[]{:S(2)}) %collective-permute-start.3) | collective-permute-done | bytes 65568 | tf_op jit(solution)/shard_map/ppermute | solution.py:233
  30.5 0.0 copy-start.6
  30.5 1.3 %collective-permute-start.4 = (bf16[64,1024]{1,0:T(8,128)(2,1)S(1)}, bf16[64,1024]{1,0:T(8,128)(2,1)S(1)}, u32[]{:S(2)}, u32[]{:S(2)}) collective-permute-start(bf16[64,1024]{1,0:T(8,128)(2,1)S(1)} %shard_map.104.refs_0_), channel_id=1, source_target_pairs={{0,16},{8,24},{16,0},{24,8},{1,17},{9,25},{17,1},{25,9},{2,18},{10... | collective-permute-start | bytes 393224 | tf_op jit(solution)/shard_map/ppermute | solution.py:233
  31.8 1.8 %shard_map.106 = (bf16[128,1024]{1,0:T(8,128)(2,1)S(1)}, bf16[128,1024]{1,0:T(8,128)(2,1)S(1)}, bf16[128,1024]{1,0:T(8,128)(2,1)S(1)}, bf16[128,1024]{1,0:T(8,12...) custom-call(s32[8,128]{1,0:T(8,128)S(1)} %bitcast.8, bf16[1024,1024]{1,0:T(8,128)(2,1)S(1)} %copy-done.5), custom_call_target="tpu_custom_call" | custom-call | flops 1342177280 | bytes 2097152 | tf_op jit(solution)/shard_map/pallas_call | solution.py:252
  33.7 6.8 %collective-permute-start.9 = (bf16[128,512]{1,0:T(8,128)(2,1)S(1)}, bf16[128,512]{1,0:T(8,128)(2,1)S(1)}, u32[]{:S(2)}, u32[]{:S(2)}) collective-permute-start(bf16[128,512]{1,0:T(8,128)(2,1)S(1)} %get-tuple-element.27), channel_id=1, source_target_pairs={{0,7},{1,6},{2,5},{3,4},{4,3},{5,2},{6,1},{7,0},{8,15},{9,14},{10,... | collective-permute-start | bytes 393224 | tf_op jit(solution)/shard_map/ppermute | solution.py:233
  40.5 4.3 %collective-permute-start.7 = (bf16[128,1024]{1,0:T(8,128)(2,1)S(1)}, bf16[128,1024]{1,0:T(8,128)(2,1)S(1)}, u32[]{:S(2)}, u32[]{:S(2)}) collective-permute-start(bf16[128,1024]{1,0:T(8,128)(2,1)S(1)} %get-tuple-element.25), channel_id=1, source_target_pairs={{0,3},{1,2},{2,1},{3,0},{4,7},{5,6},{6,5},{7,4},{8,11},{9,10},{10,... | collective-permute-start | bytes 786440 | tf_op jit(solution)/shard_map/ppermute | solution.py:233
  44.8 9.5 %shard_map.100.count_ref = bf16[1024,2304]{1,0:T(8,128)(2,1)S(1)} custom-call(s32[16,1024]{1,0:T(8,128)S(1)} %bitcast.4, s32[8,1024]{1,0:T(8,128)S(1)} %bitcast.6, s32[16,1024]{1,0:T(8,128)S(1)} %bitcast.5, s32[3,1024]{1,0:T(4,128)S(1)} %copy-done.1), custom_call_target="tpu_custom_call" | custom-call | flops 50331648 | bytes 4718592 | tf_op jit(solution)/shard_map/pallas_call | solution.py:277
  54.3 0.1 collective-permute-start.5
  54.4 5.0 %shard_map.101 = (f32[1024,1024]{1,0:T(8,128)S(1)}, f32[1024,1024]{1,0:T(8,128)S(1)}) custom-call(bf16[1024,1024]{1,0:T(8,128)(2,1)S(1)} %copy-done.5, bf16[1024,1024]{1,0:T(8,128)(2,1)S(1)} %copy-done.6, bf16[1,1024]{1,0:T(2,128)(2,1)S(1)} %reshape.6.bias_ref, bf16[1024,2304]{1,0:T(8,128)(2,1)S(1)} %shard_map.100.count_ref), custom_call_target="tpu_custom_call" | custom-call | flops 4294967296 | bytes 8388608 | tf_op jit(solution)/shard_map/pallas_call | solution.py:286
  59.4 2.5 %collective-permute-start.10 = (bf16[128,512]{1,0:T(8,128)(2,1)S(1)}, bf16[128,512]{1,0:T(8,128)(2,1)S(1)}, u32[]{:S(2)}, u32[]{:S(2)}) collective-permute-start(bf16[128,512]{1,0:T(8,128)(2,1)S(1)} %get-tuple-element.28), channel_id=1, source_target_pairs={{0,7},{1,6},{2,5},{3,4},{4,3},{5,2},{6,1},{7,0},{8,15},{9,14},{10,... | collective-permute-start | bytes 393224 | tf_op jit(solution)/shard_map/ppermute | solution.py:233
  61.9 0.0 copy-start
  61.9 3.5 %shard_map.107.sum_ref = f32[1024,1024]{1,0:T(8,128)S(1)} custom-call(f32[1024,1024]{1,0:T(8,128)S(1)} %get-tuple-element.18.sum_ref, bf16[1024,2304]{1,0:T(8,128)(2,1)S(1)} %shard_map.100.count_ref, bf16[128,1024]{1,0:T(8,128)(2,1)S(1)} %shard_map.105.refs_0_, bf16[128,1024]{1,0:T(8,128)(2,1)S(1)} %collective-permute-done.5.refs_1_, ...), custom_call_target="tpu_custom_call" | custom-call | flops 2415919104 | bytes 8388608 | tf_op jit(solution)/shard_map/pallas_call | solution.py:296
  65.5 2.8 %shard_map.108.own_ref = f32[1024,1024]{1,0:T(8,128)S(1)} custom-call(f32[1024,1024]{1,0:T(8,128)S(1)} %get-tuple-element.17.own_ref, f32[1024,1024]{1,0:T(8,128)S(1)} %shard_map.107.sum_ref, bf16[1024,2304]{1,0:T(8,128)(2,1)S(1)} %shard_map.100.count_ref, s32[3,1024]{1,0:T(4,128)S(1)} %copy-done.1, bf16[1024,1024]{1,0:T(8,128)(2,1)S(1)} %copy-done, ...), custom_call_target="tpu_custom_call" | custom-call | flops 1207959552 | bytes 8388608 | tf_op jit(solution)/shard_map/pallas_call | solution.py:309
  68.3 2.8 %shard_map.109 = bf16[1024,1024]{1,0:T(8,128)(2,1)} custom-call(f32[1024,1024]{1,0:T(8,128)S(1)} %shard_map.108.own_ref, f32[1024,1024]{1,0:T(8,128)S(1)} %shard_map.107.sum_ref, bf16[1024,2304]{1,0:T(8,128)(2,1)S(1)} %shard_map.100.count_ref, s32[3,1024]{1,0:T(4,128)S(1)} %copy-done.1, bf16[1024,1024]{1,0:T(8,128)(2,1)S(1)} %copy-done, ...), custom_call_target="tpu_custom_call" | custom-call | flops 1207959552 | bytes 8388608 | tf_op jit(solution)/shard_map/pallas_call | solution.py:317
  (29 shorter events, 0.1 us)
Async XLA Ops:
  0.0 1.6 %copy-start.5 = (bf16[1024,1024]{1,0:T(8,128)(2,1)S(1)}, bf16[1024,1024]{1,0:T(8,128)(2,1)}, u32[]{:S(2)}) copy-start(bf16[1024,1024]{1,0:T(8,128)(2,1)} %feat_ref.3) | copy-start | bytes 6291460
  1.6 0.7 copy-start.7
  2.3 0.7 copy-start.8
  2.9 41.8 %copy-start.9 = (bf16[1024]{0:T(1024)(128)(2,1)S(1)}, bf16[1024]{0:T(1024)(128)(2,1)}, u32[]{:S(2)}) copy-start(bf16[1024]{0:T(1024)(128)(2,1)} %param.13) | copy-start | bytes 6148
  2.9 41.8 %copy-start.1 = (s32[3,1024]{1,0:T(4,128)S(1)}, s32[3,1024]{1,0:T(4,128)}, u32[]{:S(2)}) copy-start(s32[3,1024]{1,0:T(4,128)} %deg_ref.5) | copy-start | bytes 36868
  2.9 41.8 %copy-start.2 = (s32[1024,16]{0,1:T(8,128)S(1)}, s32[1024,16]{0,1:T(8,128)}, u32[]{:S(2)}) copy-start(s32[1024,16]{0,1:T(8,128)} %param.16) | copy-start | bytes 196612
  2.9 41.8 %copy-start.3 = (s32[1024,16]{0,1:T(8,128)S(1)}, s32[1024,16]{0,1:T(8,128)}, u32[]{:S(2)}) copy-start(s32[1024,16]{0,1:T(8,128)} %param.17) | copy-start | bytes 196612
  2.9 41.8 %copy-start.4 = (s32[1024,8]{0,1:T(8,128)S(1)}, s32[1024,8]{0,1:T(8,128)}, u32[]{:S(2)}) copy-start(s32[1024,8]{0,1:T(8,128)} %param.15) | copy-start | bytes 98308
  4.9 13.8 %collective-permute-start = (bf16[136,1024]{1,0:T(8,128)(2,1)S(1)}, bf16[136,1024]{1,0:T(8,128)(2,1)S(1)}, u32[]{:S(2)}, u32[]{:S(2)}) collective-permute-start(bf16[136,1024]{1,0:T(8,128)(2,1)S(1)} %get-tuple-element.20), channel_id=1, source_target_pairs={{0,2},{1,3},{2,0},{3,1},{4,6},{5,7},{6,4},{7,5},{8,10},{9,11},{10,... | collective-permute-start | bytes 835592 | tf_op jit(solution)/shard_map/ppermute | solution.py:233
  7.1 11.6 %collective-permute-start.1 = (bf16[136,1024]{1,0:T(8,128)(2,1)S(1)}, bf16[136,1024]{1,0:T(8,128)(2,1)S(1)}, u32[]{:S(2)}, u32[]{:S(2)}) collective-permute-start(bf16[136,1024]{1,0:T(8,128)(2,1)S(1)} %get-tuple-element.21), channel_id=1, source_target_pairs={{0,4},{1,5},{2,6},{3,7},{4,0},{5,1},{6,2},{7,3},{8,12},{9,13},{10,... | collective-permute-start | bytes 835592 | tf_op jit(solution)/shard_map/ppermute | solution.py:233
  9.4 17.9 %collective-permute-start.2 = (bf16[136,1024]{1,0:T(8,128)(2,1)S(1)}, bf16[136,1024]{1,0:T(8,128)(2,1)S(1)}, u32[]{:S(2)}, u32[]{:S(2)}) collective-permute-start(bf16[136,1024]{1,0:T(8,128)(2,1)S(1)} %get-tuple-element.22), channel_id=1, source_target_pairs={{0,6},{1,7},{2,4},{3,5},{4,2},{5,3},{6,0},{7,1},{8,14},{9,15},{10,... | collective-permute-start | bytes 835592 | tf_op jit(solution)/shard_map/ppermute | solution.py:233
  27.4 3.1 %collective-permute-start.3 = (bf16[32,1024]{1,0:T(8,128)(2,1)S(1)}, bf16[32,1024]{1,0:T(8,128)(2,1)S(1)}, u32[]{:S(2)}, u32[]{:S(2)}) collective-permute-start(bf16[32,1024]{1,0:T(8,128)(2,1)S(1)} %shard_map.103.refs_0_), channel_id=1, source_target_pairs={{0,8},{8,0},{16,24},{24,16},{1,9},{9,1},{17,25},{25,17},{2,10},{10... | collective-permute-start | bytes 196616 | tf_op jit(solution)/shard_map/ppermute | solution.py:233
  30.5 23.9 %copy-start.6 = (bf16[1024,1024]{1,0:T(8,128)(2,1)S(1)}, bf16[1024,1024]{1,0:T(8,128)(2,1)}, u32[]{:S(2)}) copy-start(bf16[1024,1024]{1,0:T(8,128)(2,1)} %w_ref.3) | copy-start | bytes 6291460
  30.5 23.7 %collective-permute-start.4 = (bf16[64,1024]{1,0:T(8,128)(2,1)S(1)}, bf16[64,1024]{1,0:T(8,128)(2,1)S(1)}, u32[]{:S(2)}, u32[]{:S(2)}) collective-permute-start(bf16[64,1024]{1,0:T(8,128)(2,1)S(1)} %shard_map.104.refs_0_), channel_id=1, source_target_pairs={{0,16},{8,24},{16,0},{24,8},{1,17},{9,25},{17,1},{25,9},{2,18},{10... | collective-permute-start | bytes 393224 | tf_op jit(solution)/shard_map/ppermute | solution.py:233
  33.7 31.8 %collective-permute-start.9 = (bf16[128,512]{1,0:T(8,128)(2,1)S(1)}, bf16[128,512]{1,0:T(8,128)(2,1)S(1)}, u32[]{:S(2)}, u32[]{:S(2)}) collective-permute-start(bf16[128,512]{1,0:T(8,128)(2,1)S(1)} %get-tuple-element.27), channel_id=1, source_target_pairs={{0,7},{1,6},{2,5},{3,4},{4,3},{5,2},{6,1},{7,0},{8,15},{9,14},{10,... | collective-permute-start | bytes 393224 | tf_op jit(solution)/shard_map/ppermute | solution.py:233
  40.5 18.9 %collective-permute-start.6 = (bf16[128,1024]{1,0:T(8,128)(2,1)S(1)}, bf16[128,1024]{1,0:T(8,128)(2,1)S(1)}, u32[]{:S(2)}, u32[]{:S(2)}) collective-permute-start(bf16[128,1024]{1,0:T(8,128)(2,1)S(1)} %get-tuple-element.24), channel_id=1, source_target_pairs={{0,1},{1,0},{2,3},{3,2},{4,5},{5,4},{6,7},{7,6},{8,9},{9,8},{10,11... | collective-permute-start | bytes 786440 | tf_op jit(solution)/shard_map/ppermute | solution.py:233
  40.5 21.5 %collective-permute-start.7 = (bf16[128,1024]{1,0:T(8,128)(2,1)S(1)}, bf16[128,1024]{1,0:T(8,128)(2,1)S(1)}, u32[]{:S(2)}, u32[]{:S(2)}) collective-permute-start(bf16[128,1024]{1,0:T(8,128)(2,1)S(1)} %get-tuple-element.25), channel_id=1, source_target_pairs={{0,3},{1,2},{2,1},{3,0},{4,7},{5,6},{6,5},{7,4},{8,11},{9,10},{10,... | collective-permute-start | bytes 786440 | tf_op jit(solution)/shard_map/ppermute | solution.py:233
  44.7 17.2 %collective-permute-start.8 = (bf16[128,1024]{1,0:T(8,128)(2,1)S(1)}, bf16[128,1024]{1,0:T(8,128)(2,1)S(1)}, u32[]{:S(2)}, u32[]{:S(2)}) collective-permute-start(bf16[128,1024]{1,0:T(8,128)(2,1)S(1)} %get-tuple-element.26), channel_id=1, source_target_pairs={{0,5},{1,4},{2,7},{3,6},{4,1},{5,0},{6,3},{7,2},{8,13},{9,12},{10,... | collective-permute-start | bytes 786440 | tf_op jit(solution)/shard_map/ppermute | solution.py:233
  54.3 7.6 %collective-permute-start.5 = (bf16[128,1024]{1,0:T(8,128)(2,1)S(1)}, bf16[128,1024]{1,0:T(8,128)(2,1)S(1)}, u32[]{:S(2)}, u32[]{:S(2)}) collective-permute-start(bf16[128,1024]{1,0:T(8,128)(2,1)S(1)} %shard_map.105.refs_0_), channel_id=1, source_target_pairs={{0,1},{1,0},{2,3},{3,2},{4,5},{5,4},{6,7},{7,6},{8,9},{9,8},{10,11... | collective-permute-start | bytes 786440 | tf_op jit(solution)/shard_map/ppermute | solution.py:233
  59.4 8.9 %collective-permute-start.10 = (bf16[128,512]{1,0:T(8,128)(2,1)S(1)}, bf16[128,512]{1,0:T(8,128)(2,1)S(1)}, u32[]{:S(2)}, u32[]{:S(2)}) collective-permute-start(bf16[128,512]{1,0:T(8,128)(2,1)S(1)} %get-tuple-element.28), channel_id=1, source_target_pairs={{0,7},{1,6},{2,5},{3,4},{4,3},{5,2},{6,1},{7,0},{8,15},{9,14},{10,... | collective-permute-start | bytes 393224 | tf_op jit(solution)/shard_map/ppermute | solution.py:233
  61.9 3.6 %copy-start = (bf16[1024,1024]{1,0:T(8,128)(2,1)S(1)}, bf16[1024,1024]{1,0:T(8,128)(2,1)}, u32[]{:S(2)}) copy-start(bf16[1024,1024]{1,0:T(8,128)(2,1)} %w_ref.5) | copy-start | bytes 6291460

commit v3 on v2

v3 whole, which is shorter than its diff:
```python
import functools

import jax
import jax.numpy as jnp
from jax import lax
from jax.experimental import pallas as pl
from jax.experimental.pallas import tpu as pltpu
from jax.sharding import PartitionSpec as P

LANES = 128
HUB_PAD = 8
CHUNKS = 4
VM = pl.BlockSpec(memory_space=pltpu.VMEM)
ANY = pl.BlockSpec(memory_space=pl.ANY)
HBM = pl.BlockSpec(memory_space=pltpu.HBM)
BF, F32, I32 = jnp.bfloat16, jnp.float32, jnp.int32
vec = jax.ShapeDtypeStruct


def call(kernel, out_shape, in_specs, flops, bytes_accessed, limit=16, scratch=(), out_specs=None):
    single = not isinstance(out_shape, (list, tuple))
    return pl.pallas_call(
        kernel,
        out_shape=out_shape,
        in_specs=in_specs,
        out_specs=out_specs or (VM if single else [VM] * len(out_shape)),
        scratch_shapes=list(scratch),
        compiler_params=pltpu.CompilerParams(vmem_limit_bytes=limit << 20),
        cost_estimate=pl.CostEstimate(flops=4 * flops, bytes_accessed=bytes_accessed, transcendentals=0),
    )


def column_of(row, rows):
    return jnp.transpose(jnp.broadcast_to(row, (8, rows)))[:, :1]


def pick_matrix(rows_ref, shift, rows_here):
    me = lax.axis_index("member")
    caps = rows_ref.shape[1]
    wanted = column_of(rows_ref[pl.ds(me ^ shift, 1), :], caps)
    row_at = lax.broadcasted_iota(I32, (caps, rows_here), 1)
    return jnp.where(row_at == wanted, 1.0, 0.0).astype(BF)


def hub_matrix(hub_ref, rows_here):
    row_at = lax.broadcasted_iota(I32, (HUB_PAD, rows_here), 1)
    line = lax.broadcasted_iota(I32, (HUB_PAD, rows_here), 0)
    hit = jnp.zeros((HUB_PAD, rows_here), F32)
    for h in range(hub_ref.shape[0]):
        hit = hit + jnp.where((line == h) & (row_at == hub_ref[h]), 1.0, 0.0)
    return hit.astype(BF)


def load(small, feat_hbm, feat_ref, sems):
    copies = [pltpu.make_async_copy(a, b, sems.at[n]) for n, (a, b) in enumerate(small)]
    part = feat_ref.shape[0] // CHUNKS
    large = []
    for c in range(CHUNKS):
        span = pl.ds(c * part, part)
        large.append(pltpu.make_async_copy(feat_hbm.at[span, :], feat_ref.at[span, :], sems.at[len(small) + c]))
    for copy in copies + large:
        copy.start()
    for copy in copies:
        copy.wait()
    return large


def picked_rows(picks, feat_ref, copies):
    picks = jnp.concatenate(picks, axis=0)
    part = feat_ref.shape[0] // len(copies)
    picked = None
    for c, copy in enumerate(copies):
        copy.wait()
        span = slice(c * part, (c + 1) * part)
        term = jnp.dot(picks[:, span], feat_ref[span, :], preferred_element_type=F32)
        picked = term if picked is None else picked + term
    return picked.astype(BF)


def first_kernel(shifts, rows_hbm, hub_hbm, feat_hbm, *refs):
    outs, hub_out = refs[: len(shifts)], refs[len(shifts)]
    rows_ref, hub_ref, feat_ref, sems = refs[len(shifts) + 1 :]
    large = load([(rows_hbm, rows_ref), (hub_hbm, hub_ref)], feat_hbm, feat_ref, sems)
    rows_here = feat_ref.shape[0]
    caps = rows_ref.shape[1]
    picks = [pick_matrix(rows_ref, shift, rows_here) for shift in shifts]
    picked = picked_rows(picks + [hub_matrix(hub_ref, rows_here)], feat_ref, large)
    hubs = picked[len(shifts) * caps :]
    hub_out[...] = hubs
    for n in range(len(shifts)):
        block = picked[n * caps : (n + 1) * caps]
        outs[n][...] = jnp.concatenate([block, hubs], axis=0) if shifts[n] % 2 == 0 else block


def near_kernel(shifts, rows_hbm, hub_hbm, feat_hbm, after_ref, *refs):
    outs = refs[: len(shifts)]
    rows_ref, hub_ref, feat_ref, sems = refs[len(shifts) :]
    large = load([(rows_hbm, rows_ref), (hub_hbm, hub_ref)], feat_hbm, feat_ref, sems)
    caps = rows_ref.shape[1]
    picked = picked_rows([pick_matrix(rows_ref, shift, feat_ref.shape[0]) for shift in shifts], feat_ref, large)
    for n, shift in enumerate(shifts):
        block = picked[n * caps : (n + 1) * caps]
        outs[n][...] = jnp.concatenate([block, hub_ref[...]], axis=0) if shift and shift % 2 == 0 else block


def rest_kernel(shifts, cols, rows_ref, feat_ref, after_ref, *outs):
    caps = rows_ref.shape[1]
    picks = [pick_matrix(rows_ref, shift, feat_ref.shape[0]) for shift in shifts]
    picked = jnp.dot(jnp.concatenate(picks, axis=0), feat_ref[:, cols], preferred_element_type=F32).astype(BF)
    for n in range(len(shifts)):
        outs[n][...] = picked[n * caps : (n + 1) * caps]


def join_kernel(starts, *refs):
    out_ref = refs[-1]
    at = 0
    for start, ref in zip(starts, refs):
        size = ref.shape[0] - start
        out_ref[at : at + size, :] = ref[start:, :]
        at += size


def add_counts(index, width, out_ref, row, column):
    rb, kmax = index.shape
    index = index.astype(jnp.int16)
    columns = [jnp.broadcast_to(index[:, k : k + 1], (rb, LANES)) for k in range(kmax)]
    lane = lax.broadcasted_iota(I32, (rb, LANES), 1).astype(jnp.int16)
    one = jnp.ones((rb, LANES), BF)
    zero = jnp.zeros((rb, LANES), BF)
    for g in range(width // LANES):
        number = lane + jnp.asarray(g * LANES, jnp.int16)
        total = zero
        for k in range(kmax):
            total = total + jnp.where(columns[k] == number, one, zero)
        out_ref[pl.ds(row, rb), column + g * LANES : column + (g + 1) * LANES] = total


def table_kernel(rb, peers, caps, hub_dev, magic, order, local_ref, hub_ref, halo_ref, deg_ref, after_ref, out_ref):
    me = lax.axis_index("member")
    group = lax.axis_index("group")
    rows_here = local_ref.shape[1]
    halo_slots = peers * caps
    hub_slots = out_ref.shape[1] - rows_here - halo_slots
    half = peers // 2

    def body(i, carry):
        row = pl.multiple_of(i * rb, rb)
        span = pl.ds(row, rb)

        def masked(which, index):
            slot = lax.broadcasted_iota(I32, index.shape, 0)
            return jnp.transpose(jnp.where(slot < deg_ref[which : which + 1, span], index, -1))

        local = masked(0, local_ref[:, span])
        hub = hub_ref[:, span]
        owner = (hub * magic) >> 16
        apart = (owner & (peers - 1)) ^ me
        line = (owner >> (peers.bit_length() - 1)) ^ group
        place = (apart & 1) * (hub_slots // (2 * HUB_PAD)) + line * half + (apart >> 1)
        hub = masked(1, place * HUB_PAD + hub - owner * hub_dev)
        slot = halo_ref[:, span]
        apart = (slot >> (caps.bit_length() - 1)) ^ me
        place = apart
        for n, shift in enumerate(order):
            if n != shift:
                place = jnp.where(apart == shift, n, place)
        halo = masked(2, place * caps + (slot & (caps - 1)))
        add_counts(local, rows_here, out_ref, row, 0)
        add_counts(halo, halo_slots, out_ref, row, rows_here)
        add_counts(hub, hub_slots, out_ref, row, rows_here + halo_slots)
        return carry

    lax.fori_loop(0, rows_here // rb, body, 0)


def own_kernel(rb, feat_ref, w_ref, bias_ref, after_ref, out_ref):
    bias = bias_ref[...].astype(F32)
    for i in range(feat_ref.shape[0] // rb):
        span = pl.ds(i * rb, rb)
        out_ref[span, :] = jnp.dot(feat_ref[span, :], w_ref[...], preferred_element_type=F32) + bias


def local_kernel(rb, feat_ref, count_ref, after_ref, out_ref):
    rows_here = feat_ref.shape[0]
    for i in range(rows_here // rb):
        span = pl.ds(i * rb, rb)
        out_ref[span, :] = jnp.dot(count_ref[span, :rows_here], feat_ref[...], preferred_element_type=F32)


def sum_kernel(rb, sizes, at, sum_ref, count_ref, *refs):
    blocks, (_, out_ref, joined) = refs[: len(sizes)], refs[len(sizes) :]
    row = 0
    for size, ref in zip(sizes, blocks):
        joined[row : row + size, :] = ref[:size, :]
        row += size
    for i in range(sum_ref.shape[0] // rb):
        span = pl.ds(i * rb, rb)
        out_ref[span, :] = sum_ref[span, :] + jnp.dot(
            count_ref[span, at : at + row], joined[...], preferred_element_type=F32
        )


def mean_part(span, at, cols, sum_ref, count_ref, deg_ref, w_ref, block_ref, value):
    deg = deg_ref[0:1, span] + deg_ref[1:2, span] + deg_ref[2:3, span]
    scale = column_of(1.0 / deg.astype(F32), deg.shape[1])
    counts = count_ref[span, at : at + block_ref.shape[0]]
    total = sum_ref[span, cols] + jnp.dot(counts, block_ref[...], preferred_element_type=F32)
    mean = (total * scale).astype(BF)
    return value + jnp.dot(mean, w_ref[cols, :], preferred_element_type=F32)


def late_kernel(rb, at, cols, own_ref, sum_ref, count_ref, deg_ref, w_ref, block_ref, out_ref):
    for i in range(sum_ref.shape[0] // rb):
        span = pl.ds(i * rb, rb)
        out_ref[span, :] = mean_part(span, at, cols, sum_ref, count_ref, deg_ref, w_ref, block_ref, own_ref[span, :])


def last_kernel(rb, at, cols, own_ref, sum_ref, count_ref, deg_ref, w_ref, block_ref, out_hbm, out_ref, sems):
    copies = []
    for i in range(sum_ref.shape[0] // rb):
        span = pl.ds(i * rb, rb)
        value = mean_part(span, at, cols, sum_ref, count_ref, deg_ref, w_ref, block_ref, own_ref[span, :])
        out_ref[span, :] = jnp.maximum(value, 0.0).astype(BF)
        copies.append(pltpu.make_async_copy(out_ref.at[span, :], out_hbm.at[span, :], sems.at[i]))
        copies[-1].start()
    for copy in copies:
        copy.wait()


def per_device(groups, features, w_self, w_neigh, bias, hub_rows, hub_nbrs, local_nbrs, halo_nbrs, degrees, send_rows):
    rows_here, width = features.shape
    peers, caps = send_rows.shape[1:]
    hub_dev = hub_rows.shape[0]
    magic = -(-(1 << 16) // hub_dev)
    assert all((h * magic) >> 16 == h // hub_dev for h in range(hub_dev * peers * groups))
    assert peers >= 8 and groups >= 4 and hub_dev <= HUB_PAD
    assert not any(n & (n - 1) for n in (peers, groups, caps))
    rows = send_rows.reshape(peers, caps)
    hub_slots = HUB_PAD * peers * groups

    top, last = peers // 2, peers - 1
    far = list(range(top, last, 2))
    near = list(range(2, top, 2))
    other = list(range(3, last, 2))
    early = [0, 1] + near + far
    order = early + [last] + other
    spans = [slice(0, width - width // 4), slice(width - width // 4, width)]

    def swap(block, axis, shift):
        size = peers if axis == "member" else groups
        return lax.ppermute(block, axis, [(i, i ^ shift) for i in range(size)])

    scratch = [pltpu.VMEM((rows_here, width), BF), pltpu.SemaphoreType.DMA((2 + CHUNKS,))]
    plain, carrier = vec((caps, width), BF), vec((caps + HUB_PAD, width), BF)
    firsts = call(
        functools.partial(first_kernel, far + [1]),
        [carrier] * len(far) + [plain, vec((HUB_PAD, width), BF)],
        [HBM] * 3,
        0,
        2 * rows_here * width,
        limit=60,
        scratch=[pltpu.VMEM((peers, caps), I32), pltpu.SMEM((hub_dev,), I32)] + scratch,
    )(rows, hub_rows, features)
    hubs = firsts[-1]
    got = {shift: swap(block, "member", shift) for shift, block in zip(far + [1], firsts)}
    nears = call(
        functools.partial(near_kernel, near + [0]),
        [plain if shift % 2 else carrier for shift in near] + [plain],
        [HBM] * 3 + [ANY],
        0,
        2 * rows_here * width,
        limit=60,
        scratch=[pltpu.VMEM((peers, caps), I32), pltpu.VMEM((HUB_PAD, width), BF)] + scratch,
    )(rows, hubs, features, got[1])
    for shift, block in zip(near, nears):
        got[shift] = swap(block, "member", shift)
    got[0] = nears[-1]

    counts = call(
        functools.partial(table_kernel, 2 * LANES, peers, caps, hub_dev, magic, order),
        vec((rows_here, rows_here + peers * caps + hub_slots), BF),
        [VM] * 4 + [ANY],
        24 * rows_here * (rows_here + peers * caps),
        2 * rows_here * (rows_here + hub_slots + peers * caps),
    )(local_nbrs.T, hub_nbrs.T, halo_nbrs.T, degrees, got[0])

    def rest(shifts, cols, after):
        return call(
            functools.partial(rest_kernel, shifts, cols),
            [vec((caps, cols.stop - cols.start), BF)] * len(shifts),
            [VM] * 2 + [ANY],
            2 * len(shifts) * caps * rows_here * width,
            2 * rows_here * width,
        )(rows, features, after)

    def join(*blocks, starts=None, after=()):
        starts = starts or [0] * len(blocks)
        total = sum(b.shape[0] - s for b, s in zip(blocks, starts))
        return call(
            functools.partial(join_kernel, starts),
            vec((total, width), BF),
            [VM] * len(blocks) + [ANY] * len(after),
            0,
            4 * total * width,
            limit=4,
        )(*blocks, *after)

    def add(total, blocks, sizes, at, after, weight=1):
        return call(
            functools.partial(sum_kernel, 512, sizes, at),
            vec((rows_here, width), F32),
            [VM] * (2 + len(blocks)) + [ANY],
            weight * 2 * rows_here * width * sum(sizes),
            8 * rows_here * width,
            scratch=[pltpu.VMEM((sum(sizes), width), BF)],
        )(total, counts, *blocks, after)

    own = call(
        functools.partial(own_kernel, 512),
        vec((rows_here, width), F32),
        [VM] * 3 + [ANY],
        2 * rows_here * width * width,
        8 * rows_here * width,
    )(features, w_self, bias.reshape(1, width), counts)
    total = call(
        functools.partial(local_kernel, 512),
        vec((rows_here, width), F32),
        [VM] * 2 + [ANY],
        2 * rows_here * rows_here * width,
        8 * rows_here * width,
    )(features, counts, own)
    odd = rest(other, slice(0, width), total)
    for shift, block in zip(other, odd):
        got[shift] = swap(block, "member", shift)

    evens = [got[s] for s in range(2, peers, 2)]
    hubs = join(hubs, *evens, starts=[0] + [caps] * len(evens), after=[odd[0]])
    lines = [swap(hubs, "group", shift) for shift in range(1, groups)]
    late = rest([last], spans[0], hubs)
    total = add(total, [got[s] for s in early], [caps] * len(early), rows_here, late[0])
    hubs = join(hubs, *lines, after=[total])
    other_hubs = swap(hubs, "member", 1)
    soon, far_odd = other[:-1] if len(other) > 2 else other[:1], other[-1:]
    at = rows_here + caps * order.index(soon[0])
    total = add(total, [got[s] for s in soon], [caps] * len(soon), at, hubs, 16)
    total = add(total, [hubs, other_hubs], [hub_slots // 2] * 2, rows_here + caps * peers, total)
    late += rest([last], spans[1], total)
    late = [swap(block, "member", last) for block in late]
    at = rows_here + caps * order.index(far_odd[0])
    total = add(total, [got[s] for s in far_odd], [caps] * len(far_odd), at, total)

    at = rows_here + caps * order.index(last)
    value = call(
        functools.partial(late_kernel, 512, at, spans[0]),
        vec((rows_here, width), F32),
        [VM] * 6,
        2 * rows_here * spans[0].stop * width,
        8 * rows_here * width,
    )(own, total, counts, degrees, w_neigh, late[0])
    return call(
        functools.partial(last_kernel, 256, at, spans[1]),
        vec((rows_here, width), BF),
        [VM] * 6,
        2 * rows_here * (width - spans[1].start) * width,
        8 * rows_here * width,
        scratch=[pltpu.VMEM((rows_here, width), BF), pltpu.SemaphoreType.DMA((rows_here // 256,))],
        out_specs=ANY,
    )(value, total, counts, degrees, w_neigh, late[1])


def solution(mesh):
    both = ("group", "member")
    in_specs = (
        P(both, None),
        P(),
        P(),
        P(),
        P(both),
        P(both, None),
        P(both, None),
        P(both, None),
        P(None, both),
        P(both, None, None),
    )
    return jax.shard_map(
        functools.partial(per_device, mesh.shape["group"]),
        mesh=mesh,
        in_specs=in_specs,
        out_specs=P(both, None),
        check_vma=False,
    )
```

time: 71.3 us -> 58 us (0.81)
  the two profiles are of different devices: /device:TPU:1 before, /device:TPU:21 now
where the time goes in v3:
time: 58 us; the launch traced here: 57.7 us
  Pallas kernels  30 us (52%)
  starting transfers between devices  13.3 us (23%)
  waiting for transfers between devices  11.6 us (20%)
  local copies, waits for them, and re-layouts  2.39 us (4%)
    ppermute x12, starting transfers between devices, swap(): return lax.ppermute(block, axis, [(i, i ^ shift) for i in range(size)])  13.3 us
    ppermute x12, waiting for transfers between devices, swap(): return lax.ppermute(block, axis, [(i, i ^ shift) for i in range(size)])  11.6 us
    pallas_call x1, Pallas kernels, per_device(): call(functools.partial(table_kernel, 2 * LANES, peers, caps, hub_dev, mag...  8.86 us
    pallas_call x4, Pallas kernels, add(): call(functools.partial(sum_kernel, 512, sizes, at), vec((rows_here, width...  3.89 us
    pallas_call x1, Pallas kernels, per_device(): call(functools.partial(first_kernel, far + [1]), [carrier] * len(far) + [...  3.32 us
    pallas_call x1, Pallas kernels, per_device(): call(functools.partial(near_kernel, near + [0]), [plain if shift % 2 else...  2.88 us
    pallas_call x1, Pallas kernels, per_device(): call(functools.partial(own_kernel, 512), vec((rows_here, width), F32), [V...  2.37 us
    pallas_call x1, Pallas kernels, per_device(): call(functools.partial(late_kernel, 512, at, spans[0]), vec((rows_here, w...  2.36 us
  transfers between devices with their start and end apart: 12, of which 4 were waited for; matrix products, arithmetic and copies ran while one was open for 1% of the time, Pallas kernels for 42%

profile of v3, /device:TPU:21, one launch (start us, length us, event | category | flops | bytes accessed | tf_op | source)
XLA Modules:
  0.0 57.7 jit_solution(3301052776384031361)
XLA Ops:
  0.0 3.3 %shard_map.100 = (bf16[136,1024]{1,0:T(8,128)(2,1)}, bf16[136,1024]{1,0:T(8,128)(2,1)}, bf16[128,1024]{1,0:T(8,128)(2,1)}, bf16[8,1024]{1,0:T(8,128)(2,1)}) custom-call(s32[8,128]{1,0:T(8,128)} %bitcast.6, s32[6]{0:T(128)} %hub_hbm.1, bf16[1024,1024]{1,0:T(8,128)(2,1)} %feat_ref.9), custom_call_target="tpu_custom_call" | custom-call | bytes 2097152 | tf_op jit(solution)/shard_map/pallas_call | solution.py:255
  3.4 0.7 %collective-permute-start = (bf16[128,1024]{1,0:T(8,128)(2,1)}, bf16[128,1024]{1,0:T(8,128)(2,1)S(1)}, u32[]{:S(2)}, u32[]{:S(2)}) collective-permute-start(bf16[128,1024]{1,0:T(8,128)(2,1)} %get-tuple-element.14), channel_id=1, source_target_pairs={{0,1},{1,0},{2,3},{3,2},{4,5},{5,4},{6,7},{7,6},{8,9},{9,8},{10,11... | collective-permute-start | bytes 786440 | tf_op jit(solution)/shard_map/ppermute | solution.py:251
  4.2 2.4 %collective-permute-start.3 = (bf16[136,1024]{1,0:T(8,128)(2,1)}, bf16[136,1024]{1,0:T(8,128)(2,1)S(1)}, u32[]{:S(2)}, u32[]{:S(2)}) collective-permute-start(bf16[136,1024]{1,0:T(8,128)(2,1)} %get-tuple-element.18), channel_id=1, source_target_pairs={{0,6},{1,7},{2,4},{3,5},{4,2},{5,3},{6,0},{7,1},{8,14},{9,15},{10,... | collective-permute-start | bytes 835592 | tf_op jit(solution)/shard_map/ppermute | solution.py:251
  7.3 0.7 %copy-done.2 = bf16[128,1024]{1,0:T(8,128)(2,1)} copy-done((bf16[128,1024]{1,0:T(8,128)(2,1)}, bf16[128,1024]{1,0:T(8,128)(2,1)S(1)}, u32[]{:S(2)}) %copy-start.2) | copy-done | bytes 262168
  8.0 2.9 %shard_map.101 = (bf16[136,1024]{1,0:T(8,128)(2,1)}, bf16[128,1024]{1,0:T(8,128)(2,1)}) custom-call(s32[8,128]{1,0:T(8,128)} %bitcast.7, bf16[8,1024]{1,0:T(8,128)(2,1)} %get-tuple-element.13.hub_hbm.refs_0_, bf16[1024,1024]{1,0:T(8,128)(2,1)} %feat_ref.9, bf16[128,1024]{1,0:T(8,128)(2,1)} %copy-done.2), custom_call_target="tpu_custom_call" | custom-call | bytes 2097152 | tf_op jit(solution)/shard_map/pallas_call | solution.py:266
  10.9 1.1 %collective-permute-start.1 = (bf16[136,1024]{1,0:T(8,128)(2,1)}, bf16[136,1024]{1,0:T(8,128)(2,1)S(1)}, u32[]{:S(2)}, u32[]{:S(2)}) collective-permute-start(bf16[136,1024]{1,0:T(8,128)(2,1)} %get-tuple-element.16), channel_id=1, source_target_pairs={{0,2},{1,3},{2,0},{3,1},{4,6},{5,7},{6,4},{7,5},{8,10},{9,11},{10,... | collective-permute-start | bytes 835592 | tf_op jit(solution)/shard_map/ppermute | solution.py:251
  12.0 0.9 %copy-done.4 = bf16[128,1024]{1,0:T(8,128)(2,1)S(1)} copy-done((bf16[128,1024]{1,0:T(8,128)(2,1)S(1)}, bf16[128,1024]{1,0:T(8,128)(2,1)}, u32[]{:S(2)}) %copy-start.4) | copy-done | bytes 262168
  13.0 8.9 %shard_map.102.after_ref.count_ref = bf16[1024,2304]{1,0:T(8,128)(2,1)S(1)} custom-call(s32[16,1024]{1,0:T(8,128)S(1)} %bitcast.4, s32[8,1024]{1,0:T(8,128)S(1)} %bitcast.11, s32[16,1024]{1,0:T(8,128)S(1)} %bitcast.5, s32[3,1024]{1,0:T(4,128)S(1)} %copy-done.8, bf16[128,1024]{1,0:T(8,128)(2,1)S(1)} %copy-done.4), custom_call_target="tpu_custom_call" | custom-call | flops 201326592 | bytes 4718592 | tf_op jit(solution)/shard_map/pallas_call | solution.py:279
  21.9 2.4 %shard_map.103.after_ref.own_ref = f32[1024,1024]{1,0:T(8,128)S(1)} custom-call(bf16[1024,1024]{1,0:T(8,128)(2,1)S(1)} %copy-done, bf16[1024,1024]{1,0:T(8,128)(2,1)S(1)} %copy-done.12, bf16[1,1024]{1,0:T(2,128)(2,1)S(1)} %reshape.6.bias_ref, bf16[1024,2304]{1,0:T(8,128)(2,1)S(1)} %shard_map.102.after_ref.count_ref), custom_call_target="tpu_custom_call" | custom-call | flops 8589934592 | bytes 8388608 | tf_op jit(solution)/shard_map/pallas_call | solution.py:318
  24.3 2.3 %shard_map.104.after_ref.sum_ref = f32[1024,1024]{1,0:T(8,128)S(1)} custom-call(bf16[1024,1024]{1,0:T(8,128)(2,1)S(1)} %copy-done, bf16[1024,2304]{1,0:T(8,128)(2,1)S(1)} %shard_map.102.after_ref.count_ref, f32[1024,1024]{1,0:T(8,128)S(1)} %shard_map.103.after_ref.own_ref), custom_call_target="tpu_custom_call" | custom-call | flops 8589934592 | bytes 8388608 | tf_op jit(solution)/shard_map/pallas_call | solution.py:325
  26.6 0.9 %shard_map.105 = (bf16[128,1024]{1,0:T(8,128)(2,1)S(1)}, bf16[128,1024]{1,0:T(8,128)(2,1)S(1)}) custom-call(s32[8,128]{1,0:T(8,128)S(1)} %bitcast.8, bf16[1024,1024]{1,0:T(8,128)(2,1)S(1)} %copy-done, f32[1024,1024]{1,0:T(8,128)S(1)} %shard_map.104.after_ref.sum_ref), custom_call_target="tpu_custom_call" | custom-call | flops 2147483648 | bytes 2097152 | tf_op jit(solution)/shard_map/pallas_call | solution.py:288
  28.3 1.0 %collective-permute-start.4 = (bf16[128,1024]{1,0:T(8,128)(2,1)S(1)}, bf16[128,1024]{1,0:T(8,128)(2,1)S(1)}, u32[]{:S(2)}, u32[]{:S(2)}) collective-permute-start(bf16[128,1024]{1,0:T(8,128)(2,1)S(1)} %get-tuple-element.19.refs_4_), channel_id=1, source_target_pairs={{0,3},{1,2},{2,1},{3,0},{4,7},{5,6},{6,5},{7,4},{8,11},{9,10},{10,... | collective-permute-start | bytes 786440 | tf_op jit(solution)/shard_map/ppermute | solution.py:251
  29.3 2.5 %collective-permute-done.3.refs_3_.refs_4_ = bf16[136,1024]{1,0:T(8,128)(2,1)S(1)} collective-permute-done((bf16[136,1024]{1,0:T(8,128)(2,1)}, bf16[136,1024]{1,0:T(8,128)(2,1)S(1)}, u32[]{:S(2)}, u32[]{:S(2)}) %collective-permute-start.3) | collective-permute-done | bytes 278560 | tf_op jit(solution)/shard_map/ppermute | solution.py:251
  31.8 1.2 %collective-permute-start.7 = (bf16[32,1024]{1,0:T(8,128)(2,1)S(1)}, bf16[32,1024]{1,0:T(8,128)(2,1)S(1)}, u32[]{:S(2)}, u32[]{:S(2)}) collective-permute-start(bf16[32,1024]{1,0:T(8,128)(2,1)S(1)} %shard_map.106.after_ref.refs_0_), channel_id=1, source_target_pairs={{0,24},{8,16},{16,8},{24,0},{1,25},{9,17},{17,9},{25,1},{2,26},{10... | collective-permute-start | bytes 196616 | tf_op jit(solution)/shard_map/ppermute | solution.py:251
  33.0 1.2 %collective-permute-start.6 = (bf16[32,1024]{1,0:T(8,128)(2,1)S(1)}, bf16[32,1024]{1,0:T(8,128)(2,1)S(1)}, u32[]{:S(2)}, u32[]{:S(2)}) collective-permute-start(bf16[32,1024]{1,0:T(8,128)(2,1)S(1)} %shard_map.106.after_ref.refs_0_), channel_id=1, source_target_pairs={{0,16},{8,24},{16,0},{24,8},{1,17},{9,25},{17,1},{25,9},{2,18},{10... | collective-permute-start | bytes 196616 | tf_op jit(solution)/shard_map/ppermute | solution.py:251
  35.0 1.8 %shard_map.108.refs_4_.sum_ref = f32[1024,1024]{1,0:T(8,128)S(1)} custom-call(f32[1024,1024]{1,0:T(8,128)S(1)} %shard_map.104.after_ref.sum_ref, bf16[1024,2304]{1,0:T(8,128)(2,1)S(1)} %shard_map.102.after_ref.count_ref, bf16[128,1024]{1,0:T(8,128)(2,1)S(1)} %copy-done.5, bf16[128,1024]{1,0:T(8,128)(2,1)S(1)} %copy-done.3, ...), custom_call_target="tpu_custom_call" | custom-call | flops 5368709120 | bytes 8388608 | tf_op jit(solution)/shard_map/pallas_call | solution.py:309
  36.9 0.8 %collective-permute-start.10 = (bf16[128,768]{1,0:T(8,128)(2,1)S(1)}, bf16[128,768]{1,0:T(8,128)(2,1)S(1)}, u32[]{:S(2)}, u32[]{:S(2)}) collective-permute-start(bf16[128,768]{1,0:T(8,128)(2,1)S(1)} %shard_map.107.refs_5_), channel_id=1, source_target_pairs={{0,7},{1,6},{2,5},{3,4},{4,3},{5,2},{6,1},{7,0},{8,15},{9,14},{10,... | collective-permute-start | bytes 589832 | tf_op jit(solution)/shard_map/ppermute | solution.py:251
  38.0 1.7 %collective-permute-start.8 = (bf16[128,1024]{1,0:T(8,128)(2,1)S(1)}, bf16[128,1024]{1,0:T(8,128)(2,1)S(1)}, u32[]{:S(2)}, u32[]{:S(2)}) collective-permute-start(bf16[128,1024]{1,0:T(8,128)(2,1)S(1)} %shard_map.109.refs_1_.refs_0_), channel_id=1, source_target_pairs={{0,1},{1,0},{2,3},{3,2},{4,5},{5,4},{6,7},{7,6},{8,9},{9,8},{10,11... | collective-permute-start | bytes 786440 | tf_op jit(solution)/shard_map/ppermute | solution.py:251
  39.7 2.2 %collective-permute-done.4.refs_0_ = bf16[128,1024]{1,0:T(8,128)(2,1)S(1)} collective-permute-done((bf16[128,1024]{1,0:T(8,128)(2,1)S(1)}, bf16[128,1024]{1,0:T(8,128)(2,1)S(1)}, u32[]{:S(2)}, u32[]{:S(2)}) %collective-permute-start.4) | collective-permute-done | bytes 262176 | tf_op jit(solution)/shard_map/ppermute | solution.py:251
  42.6 0.7 %shard_map.111.sum_ref.refs_1_.after_ref = f32[1024,1024]{1,0:T(8,128)S(1)} custom-call(f32[1024,1024]{1,0:T(8,128)S(1)} %shard_map.110.sum_ref.refs_2_, bf16[1024,2304]{1,0:T(8,128)(2,1)S(1)} %shard_map.102.after_ref.count_ref, bf16[128,1024]{1,0:T(8,128)(2,1)S(1)} %shard_map.109.refs_1_.refs_0_, bf16[128,1024]{1,0:T(8,128)(2,1)S(1)} %collective-permute-done.8.refs_1_, ...), custom_call_target="tpu_custom_call" | custom-call | flops 2147483648 | bytes 8388608 | tf_op jit(solution)/shard_map/pallas_call | solution.py:309
  43.7 2.0 %collective-permute-start.11 = (bf16[128,256]{1,0:T(8,128)(2,1)S(1)}, bf16[128,256]{1,0:T(8,128)(2,1)S(1)}, u32[]{:S(2)}, u32[]{:S(2)}) collective-permute-start(bf16[128,256]{1,0:T(8,128)(2,1)S(1)} %shard_map.114), channel_id=1, source_target_pairs={{0,7},{1,6},{2,5},{3,4},{4,3},{5,2},{6,1},{7,0},{8,15},{9,14},{10,... | collective-permute-start | bytes 196616 | tf_op jit(solution)/shard_map/ppermute | solution.py:251
  46.4 6.5 %collective-permute-done.10.block_ref = bf16[128,768]{1,0:T(8,128)(2,1)S(1)} collective-permute-done((bf16[128,768]{1,0:T(8,128)(2,1)S(1)}, bf16[128,768]{1,0:T(8,128)(2,1)S(1)}, u32[]{:S(2)}, u32[]{:S(2)}) %collective-permute-start.10) | collective-permute-done | bytes 196640 | tf_op jit(solution)/shard_map/ppermute | solution.py:251
  53.0 2.4 %shard_map.113.own_ref = f32[1024,1024]{1,0:T(8,128)S(1)} custom-call(f32[1024,1024]{1,0:T(8,128)S(1)} %shard_map.103.after_ref.own_ref, f32[1024,1024]{1,0:T(8,128)S(1)} %shard_map.112.sum_ref, bf16[1024,2304]{1,0:T(8,128)(2,1)S(1)} %shard_map.102.after_ref.count_ref, s32[3,1024]{1,0:T(4,128)S(1)} %copy-done.8, bf16[1024,1024]{1,0:T(8,128)(2,1)S(1)} %copy-done.1, ...), custom_call_target="tpu_custom_call" | custom-call | flops 6442450944 | bytes 8388608 | tf_op jit(solution)/shard_map/pallas_call | solution.py:353
  55.3 2.2 %shard_map.115 = bf16[1024,1024]{1,0:T(8,128)(2,1)} custom-call(f32[1024,1024]{1,0:T(8,128)S(1)} %shard_map.113.own_ref, f32[1024,1024]{1,0:T(8,128)S(1)} %shard_map.112.sum_ref, bf16[1024,2304]{1,0:T(8,128)(2,1)S(1)} %shard_map.102.after_ref.count_ref, s32[3,1024]{1,0:T(4,128)S(1)} %copy-done.8, bf16[1024,1024]{1,0:T(8,128)(2,1)S(1)} %copy-done.1, ...), custom_call_target="tpu_custom_call" | custom-call | flops 2147483648 | bytes 8388608 | tf_op jit(solution)/shard_map/pallas_call | solution.py:360
  (43 shorter events, 4.4 us)
Async XLA Ops:
  0.0 12.0 %copy-start.8 = (s32[3,1024]{1,0:T(4,128)S(1)}, s32[3,1024]{1,0:T(4,128)}, u32[]{:S(2)}) copy-start(s32[3,1024]{1,0:T(4,128)} %deg_ref.5) | copy-start | bytes 36868
  0.0 12.0 %copy-start.7 = (s32[1024,16]{0,1:T(8,128)S(1)}, s32[1024,16]{0,1:T(8,128)}, u32[]{:S(2)}) copy-start(s32[1024,16]{0,1:T(8,128)} %param.17) | copy-start | bytes 196612
  0.0 12.0 %copy-start.6 = (s32[1024,16]{0,1:T(8,128)S(1)}, s32[1024,16]{0,1:T(8,128)}, u32[]{:S(2)}) copy-start(s32[1024,16]{0,1:T(8,128)} %param.16) | copy-start | bytes 196612
  0.0 12.0 %copy-start.11 = (s32[1024,8]{0,1:T(8,128)S(1)}, s32[1024,8]{0,1:T(8,128)}, u32[]{:S(2)}) copy-start(s32[1024,8]{0,1:T(8,128)} %param.15) | copy-start | bytes 98308
  3.3 18.5 %copy-start = (bf16[1024,1024]{1,0:T(8,128)(2,1)S(1)}, bf16[1024,1024]{1,0:T(8,128)(2,1)}, u32[]{:S(2)}) copy-start(bf16[1024,1024]{1,0:T(8,128)(2,1)} %feat_ref.9) | copy-start | bytes 6291460
  3.4 3.9 %collective-permute-start = (bf16[128,1024]{1,0:T(8,128)(2,1)}, bf16[128,1024]{1,0:T(8,128)(2,1)S(1)}, u32[]{:S(2)}, u32[]{:S(2)}) collective-permute-start(bf16[128,1024]{1,0:T(8,128)(2,1)} %get-tuple-element.14), channel_id=1, source_target_pairs={{0,1},{1,0},{2,3},{3,2},{4,5},{5,4},{6,7},{7,6},{8,9},{9,8},{10,11... | collective-permute-start | bytes 786440 | tf_op jit(solution)/shard_map/ppermute | solution.py:251
  4.1 25.2 %collective-permute-start.2 = (bf16[136,1024]{1,0:T(8,128)(2,1)}, bf16[136,1024]{1,0:T(8,128)(2,1)S(1)}, u32[]{:S(2)}, u32[]{:S(2)}) collective-permute-start(bf16[136,1024]{1,0:T(8,128)(2,1)} %get-tuple-element.17), channel_id=1, source_target_pairs={{0,4},{1,5},{2,6},{3,7},{4,0},{5,1},{6,2},{7,3},{8,12},{9,13},{10,... | collective-permute-start | bytes 835592 | tf_op jit(solution)/shard_map/ppermute | solution.py:251
  4.2 27.6 %collective-permute-start.3 = (bf16[136,1024]{1,0:T(8,128)(2,1)}, bf16[136,1024]{1,0:T(8,128)(2,1)S(1)}, u32[]{:S(2)}, u32[]{:S(2)}) collective-permute-start(bf16[136,1024]{1,0:T(8,128)(2,1)} %get-tuple-element.18), channel_id=1, source_target_pairs={{0,6},{1,7},{2,4},{3,5},{4,2},{5,3},{6,0},{7,1},{8,14},{9,15},{10,... | collective-permute-start | bytes 835592 | tf_op jit(solution)/shard_map/ppermute | solution.py:251
  10.9 20.9 %collective-permute-start.1 = (bf16[136,1024]{1,0:T(8,128)(2,1)}, bf16[136,1024]{1,0:T(8,128)(2,1)S(1)}, u32[]{:S(2)}, u32[]{:S(2)}) collective-permute-start(bf16[136,1024]{1,0:T(8,128)(2,1)} %get-tuple-element.16), channel_id=1, source_target_pairs={{0,2},{1,3},{2,0},{3,1},{4,6},{5,7},{6,4},{7,5},{8,10},{9,11},{10,... | collective-permute-start | bytes 835592 | tf_op jit(solution)/shard_map/ppermute | solution.py:251
  12.0 1.0 %copy-start.4 = (bf16[128,1024]{1,0:T(8,128)(2,1)S(1)}, bf16[128,1024]{1,0:T(8,128)(2,1)}, u32[]{:S(2)}) copy-start(bf16[128,1024]{1,0:T(8,128)(2,1)} %get-tuple-element.15.after_ref.refs_0_) | copy-start | bytes 786436
  13.0 8.9 %copy-start.12 = (bf16[1024,1024]{1,0:T(8,128)(2,1)S(1)}, bf16[1024,1024]{1,0:T(8,128)(2,1)}, u32[]{:S(2)}) copy-start(bf16[1024,1024]{1,0:T(8,128)(2,1)} %w_ref.3) | copy-start | bytes 6291460
  24.3 2.3 %copy-start.10 = (s32[1,8,128]{2,1,0:T(8,128)S(1)}, s32[1,8,128]{2,1,0:T(8,128)}, u32[]{:S(2)}) copy-start(s32[1,8,128]{2,1,0:T(8,128)} %param.19) | copy-start | bytes 12292
  26.6 5.2 %copy-start.9 = (bf16[8,1024]{1,0:T(8,128)(2,1)S(1)}, bf16[8,1024]{1,0:T(8,128)(2,1)}, u32[]{:S(2)}) copy-start(bf16[8,1024]{1,0:T(8,128)(2,1)} %get-tuple-element.13.hub_hbm.refs_0_) | copy-start | bytes 49156
  27.5 7.5 %copy-start.3 = (bf16[128,1024]{1,0:T(8,128)(2,1)S(1)}, bf16[128,1024]{1,0:T(8,128)(2,1)}, u32[]{:S(2)}) copy-start(bf16[128,1024]{1,0:T(8,128)(2,1)} %copy-done.2) | copy-start | bytes 786436
  27.6 7.5 %copy-start.5 = (bf16[128,1024]{1,0:T(8,128)(2,1)S(1)}, bf16[128,1024]{1,0:T(8,128)(2,1)}, u32[]{:S(2)}) copy-start(bf16[128,1024]{1,0:T(8,128)(2,1)} %get-tuple-element.15.after_ref.refs_0_) | copy-start | bytes 786436
  27.6 18.2 %collective-permute-start.9 = (bf16[128,1024]{1,0:T(8,128)(2,1)S(1)}, bf16[128,1024]{1,0:T(8,128)(2,1)S(1)}, u32[]{:S(2)}, u32[]{:S(2)}) collective-permute-start(bf16[128,1024]{1,0:T(8,128)(2,1)S(1)} %get-tuple-element.20), channel_id=1, source_target_pairs={{0,5},{1,4},{2,7},{3,6},{4,1},{5,0},{6,3},{7,2},{8,13},{9,12},{10,... | collective-permute-start | bytes 786440 | tf_op jit(solution)/shard_map/ppermute | solution.py:251
  28.3 13.6 %collective-permute-start.4 = (bf16[128,1024]{1,0:T(8,128)(2,1)S(1)}, bf16[128,1024]{1,0:T(8,128)(2,1)S(1)}, u32[]{:S(2)}, u32[]{:S(2)}) collective-permute-start(bf16[128,1024]{1,0:T(8,128)(2,1)S(1)} %get-tuple-element.19.refs_4_), channel_id=1, source_target_pairs={{0,3},{1,2},{2,1},{3,0},{4,7},{5,6},{6,5},{7,4},{8,11},{9,10},{10,... | collective-permute-start | bytes 786440 | tf_op jit(solution)/shard_map/ppermute | solution.py:251
  31.8 5.0 %collective-permute-start.7 = (bf16[32,1024]{1,0:T(8,128)(2,1)S(1)}, bf16[32,1024]{1,0:T(8,128)(2,1)S(1)}, u32[]{:S(2)}, u32[]{:S(2)}) collective-permute-start(bf16[32,1024]{1,0:T(8,128)(2,1)S(1)} %shard_map.106.after_ref.refs_0_), channel_id=1, source_target_pairs={{0,24},{8,16},{16,8},{24,0},{1,25},{9,17},{17,9},{25,1},{2,26},{10... | collective-permute-start | bytes 196616 | tf_op jit(solution)/shard_map/ppermute | solution.py:251
  33.0 4.9 %collective-permute-start.6 = (bf16[32,1024]{1,0:T(8,128)(2,1)S(1)}, bf16[32,1024]{1,0:T(8,128)(2,1)S(1)}, u32[]{:S(2)}, u32[]{:S(2)}) collective-permute-start(bf16[32,1024]{1,0:T(8,128)(2,1)S(1)} %shard_map.106.after_ref.refs_0_), channel_id=1, source_target_pairs={{0,16},{8,24},{16,0},{24,8},{1,17},{9,25},{17,1},{25,9},{2,18},{10... | collective-permute-start | bytes 196616 | tf_op jit(solution)/shard_map/ppermute | solution.py:251
  34.3 3.7 %collective-permute-start.5 = (bf16[32,1024]{1,0:T(8,128)(2,1)S(1)}, bf16[32,1024]{1,0:T(8,128)(2,1)S(1)}, u32[]{:S(2)}, u32[]{:S(2)}) collective-permute-start(bf16[32,1024]{1,0:T(8,128)(2,1)S(1)} %shard_map.106.after_ref.refs_0_), channel_id=1, source_target_pairs={{0,8},{8,0},{16,24},{24,16},{1,9},{9,1},{17,25},{25,17},{2,10},{10... | collective-permute-start | bytes 196616 | tf_op jit(solution)/shard_map/ppermute | solution.py:251
  36.9 16.1 %collective-permute-start.10 = (bf16[128,768]{1,0:T(8,128)(2,1)S(1)}, bf16[128,768]{1,0:T(8,128)(2,1)S(1)}, u32[]{:S(2)}, u32[]{:S(2)}) collective-permute-start(bf16[128,768]{1,0:T(8,128)(2,1)S(1)} %shard_map.107.refs_5_), channel_id=1, source_target_pairs={{0,7},{1,6},{2,5},{3,4},{4,3},{5,2},{6,1},{7,0},{8,15},{9,14},{10,... | collective-permute-start | bytes 589832 | tf_op jit(solution)/shard_map/ppermute | solution.py:251
  38.0 4.6 %collective-permute-start.8 = (bf16[128,1024]{1,0:T(8,128)(2,1)S(1)}, bf16[128,1024]{1,0:T(8,128)(2,1)S(1)}, u32[]{:S(2)}, u32[]{:S(2)}) collective-permute-start(bf16[128,1024]{1,0:T(8,128)(2,1)S(1)} %shard_map.109.refs_1_.refs_0_), channel_id=1, source_target_pairs={{0,1},{1,0},{2,3},{3,2},{4,5},{5,4},{6,7},{7,6},{8,9},{9,8},{10,11... | collective-permute-start | bytes 786440 | tf_op jit(solution)/shard_map/ppermute | solution.py:251
  43.7 9.3 %copy-start.1 = (bf16[1024,1024]{1,0:T(8,128)(2,1)S(1)}, bf16[1024,1024]{1,0:T(8,128)(2,1)}, u32[]{:S(2)}) copy-start(bf16[1024,1024]{1,0:T(8,128)(2,1)} %w_ref.5) | copy-start | bytes 6291460
  43.7 11.6 %collective-permute-start.11 = (bf16[128,256]{1,0:T(8,128)(2,1)S(1)}, bf16[128,256]{1,0:T(8,128)(2,1)S(1)}, u32[]{:S(2)}, u32[]{:S(2)}) collective-permute-start(bf16[128,256]{1,0:T(8,128)(2,1)S(1)} %shard_map.114), channel_id=1, source_target_pairs={{0,7},{1,6},{2,5},{3,4},{4,3},{5,2},{6,1},{7,0},{8,15},{9,14},{10,... | collective-permute-start | bytes 196616 | tf_op jit(solution)/shard_map/ppermute | solution.py:251
  (1 other events, 0.7 us)

commit v4 on v3

--- a/solution.py
+++ b/solution.py
@@ -239,12 +239,12 @@
     hub_slots = HUB_PAD * peers * groups
 
     top, last = peers // 2, peers - 1
-    far = list(range(top, last, 2))
-    near = list(range(2, top, 2))
+    far = [last - 1]
+    near = list(range(top, last - 1, 2)) + list(range(2, top, 2))
     other = list(range(3, last, 2))
     early = [0, 1] + near + far
     order = early + [last] + other
-    spans = [slice(0, width - width // 4), slice(width - width // 4, width)]
+    spans = [slice(0, width // 2), slice(width // 2, width)]
 
     def swap(block, axis, shift):
         size = peers if axis == "member" else groups

time: 58 us -> 57.2 us (0.986)
  starting transfers between devices: 13.3 us -> 12.5 us
    ppermute x12, starting transfers between devices: 13.3 us -> 12.5 us  [swap(): return lax.ppermute(block, axis, [(i, i ^ shift) for i in range(size)])]
    pallas_call x1, Pallas kernels: 2.36 us -> 1.72 us  [per_device(): call(functools.partial(late_kernel, 512, at, spans[0]), vec((rows_here, w...]
where the time goes in v4:
time: 57.2 us; the launch traced here: 57 us
  Pallas kernels  29.9 us (52%)
  starting transfers between devices  12.5 us (22%)
  waiting for transfers between devices  11.7 us (20%)
  local copies, waits for them, and re-layouts  2.39 us (4%)
    ppermute x12, starting transfers between devices, swap(): return lax.ppermute(block, axis, [(i, i ^ shift) for i in range(size)])  12.5 us
    ppermute x12, waiting for transfers between devices, swap(): return lax.ppermute(block, axis, [(i, i ^ shift) for i in range(size)])  11.7 us
    pallas_call x1, Pallas kernels, per_device(): call(functools.partial(table_kernel, 2 * LANES, peers, caps, hub_dev, mag...  8.86 us
    pallas_call x4, Pallas kernels, add(): call(functools.partial(sum_kernel, 512, sizes, at), vec((rows_here, width...  3.89 us
    pallas_call x1, Pallas kernels, per_device(): call(functools.partial(near_kernel, near + [0]), [plain if shift % 2 else...  3.25 us
    pallas_call x1, Pallas kernels, per_device(): call(functools.partial(first_kernel, far + [1]), [carrier] * len(far) + [...  2.96 us
    pallas_call x1, Pallas kernels, per_device(): call(functools.partial(last_kernel, 256, at, spans[1]), vec((rows_here, w...  2.79 us
    pallas_call x1, Pallas kernels, per_device(): call(functools.partial(own_kernel, 512), vec((rows_here, width), F32), [V...  2.34 us
  transfers between devices with their start and end apart: 12, of which 4 were waited for; matrix products, arithmetic and copies ran while one was open for 1% of the time, Pallas kernels for 42%

profile of v4, /device:TPU:21, one launch (start us, length us, event | category | flops | bytes accessed | tf_op | source)
XLA Modules:
  0.0 57.0 jit_solution(7496444425632678834)
XLA Ops:
  0.0 3.0 %shard_map.100 = (bf16[136,1024]{1,0:T(8,128)(2,1)}, bf16[128,1024]{1,0:T(8,128)(2,1)}, bf16[8,1024]{1,0:T(8,128)(2,1)}) custom-call(s32[8,128]{1,0:T(8,128)} %bitcast.6, s32[6]{0:T(128)} %hub_hbm.1, bf16[1024,1024]{1,0:T(8,128)(2,1)} %feat_ref.9), custom_call_target="tpu_custom_call" | custom-call | bytes 2097152 | tf_op jit(solution)/shard_map/pallas_call | solution.py:255
  3.0 0.7 %collective-permute-start = (bf16[128,1024]{1,0:T(8,128)(2,1)}, bf16[128,1024]{1,0:T(8,128)(2,1)S(1)}, u32[]{:S(2)}, u32[]{:S(2)}) collective-permute-start(bf16[128,1024]{1,0:T(8,128)(2,1)} %get-tuple-element.14), channel_id=1, source_target_pairs={{0,1},{1,0},{2,3},{3,2},{4,5},{5,4},{6,7},{7,6},{8,9},{9,8},{10,11... | collective-permute-start | bytes 786440 | tf_op jit(solution)/shard_map/ppermute | solution.py:251
  5.1 0.7 %copy-done.2 = bf16[128,1024]{1,0:T(8,128)(2,1)} copy-done((bf16[128,1024]{1,0:T(8,128)(2,1)}, bf16[128,1024]{1,0:T(8,128)(2,1)S(1)}, u32[]{:S(2)}) %copy-start.2) | copy-done | bytes 262168
  5.8 3.2 %shard_map.101 = (bf16[136,1024]{1,0:T(8,128)(2,1)}, bf16[136,1024]{1,0:T(8,128)(2,1)}, bf16[128,1024]{1,0:T(8,128)(2,1)}) custom-call(s32[8,128]{1,0:T(8,128)} %bitcast.7, bf16[8,1024]{1,0:T(8,128)(2,1)} %get-tuple-element.13.hub_hbm.refs_0_, bf16[1024,1024]{1,0:T(8,128)(2,1)} %feat_ref.9, bf16[128,1024]{1,0:T(8,128)(2,1)} %copy-done.2), custom_call_target="tpu_custom_call" | custom-call | bytes 2097152 | tf_op jit(solution)/shard_map/pallas_call | solution.py:266
  9.1 2.8 %collective-permute-start.1 = (bf16[136,1024]{1,0:T(8,128)(2,1)}, bf16[136,1024]{1,0:T(8,128)(2,1)S(1)}, u32[]{:S(2)}, u32[]{:S(2)}) collective-permute-start(bf16[136,1024]{1,0:T(8,128)(2,1)} %get-tuple-element.16), channel_id=1, source_target_pairs={{0,4},{1,5},{2,6},{3,7},{4,0},{5,1},{6,2},{7,3},{8,12},{9,13},{10,... | collective-permute-start | bytes 835592 | tf_op jit(solution)/shard_map/ppermute | solution.py:251
  11.9 0.9 %copy-done.4 = bf16[128,1024]{1,0:T(8,128)(2,1)S(1)} copy-done((bf16[128,1024]{1,0:T(8,128)(2,1)S(1)}, bf16[128,1024]{1,0:T(8,128)(2,1)}, u32[]{:S(2)}) %copy-start.4) | copy-done | bytes 262168
  12.8 8.9 %shard_map.102.after_ref.count_ref = bf16[1024,2304]{1,0:T(8,128)(2,1)S(1)} custom-call(s32[16,1024]{1,0:T(8,128)S(1)} %bitcast.4, s32[8,1024]{1,0:T(8,128)S(1)} %bitcast.11, s32[16,1024]{1,0:T(8,128)S(1)} %bitcast.5, s32[3,1024]{1,0:T(4,128)S(1)} %copy-done.6, bf16[128,1024]{1,0:T(8,128)(2,1)S(1)} %copy-done.4), custom_call_target="tpu_custom_call" | custom-call | flops 201326592 | bytes 4718592 | tf_op jit(solution)/shard_map/pallas_call | solution.py:279
  21.7 2.3 %shard_map.103.after_ref.own_ref = f32[1024,1024]{1,0:T(8,128)S(1)} custom-call(bf16[1024,1024]{1,0:T(8,128)(2,1)S(1)} %copy-done, bf16[1024,1024]{1,0:T(8,128)(2,1)S(1)} %copy-done.12, bf16[1,1024]{1,0:T(2,128)(2,1)S(1)} %reshape.6.bias_ref, bf16[1024,2304]{1,0:T(8,128)(2,1)S(1)} %shard_map.102.after_ref.count_ref), custom_call_target="tpu_custom_call" | custom-call | flops 8589934592 | bytes 8388608 | tf_op jit(solution)/shard_map/pallas_call | solution.py:318
  24.1 2.3 %shard_map.104.after_ref.sum_ref = f32[1024,1024]{1,0:T(8,128)S(1)} custom-call(bf16[1024,1024]{1,0:T(8,128)(2,1)S(1)} %copy-done, bf16[1024,2304]{1,0:T(8,128)(2,1)S(1)} %shard_map.102.after_ref.count_ref, f32[1024,1024]{1,0:T(8,128)S(1)} %shard_map.103.after_ref.own_ref), custom_call_target="tpu_custom_call" | custom-call | flops 8589934592 | bytes 8388608 | tf_op jit(solution)/shard_map/pallas_call | solution.py:325
  26.4 0.9 %shard_map.105 = (bf16[128,1024]{1,0:T(8,128)(2,1)S(1)}, bf16[128,1024]{1,0:T(8,128)(2,1)S(1)}) custom-call(s32[8,128]{1,0:T(8,128)S(1)} %bitcast.8, bf16[1024,1024]{1,0:T(8,128)(2,1)S(1)} %copy-done, f32[1024,1024]{1,0:T(8,128)S(1)} %shard_map.104.after_ref.sum_ref), custom_call_target="tpu_custom_call" | custom-call | flops 2147483648 | bytes 2097152 | tf_op jit(solution)/shard_map/pallas_call | solution.py:288
  27.4 1.8 %collective-permute-start.9 = (bf16[128,1024]{1,0:T(8,128)(2,1)S(1)}, bf16[128,1024]{1,0:T(8,128)(2,1)S(1)}, u32[]{:S(2)}, u32[]{:S(2)}) collective-permute-start(bf16[128,1024]{1,0:T(8,128)(2,1)S(1)} %get-tuple-element.20), channel_id=1, source_target_pairs={{0,5},{1,4},{2,7},{3,6},{4,1},{5,0},{6,3},{7,2},{8,13},{9,12},{10,... | collective-permute-start | bytes 786440 | tf_op jit(solution)/shard_map/ppermute | solution.py:251
  29.8 1.2 %collective-permute-start.7 = (bf16[32,1024]{1,0:T(8,128)(2,1)S(1)}, bf16[32,1024]{1,0:T(8,128)(2,1)S(1)}, u32[]{:S(2)}, u32[]{:S(2)}) collective-permute-start(bf16[32,1024]{1,0:T(8,128)(2,1)S(1)} %shard_map.106.after_ref.refs_0_), channel_id=1, source_target_pairs={{0,24},{8,16},{16,8},{24,0},{1,25},{9,17},{17,9},{25,1},{2,26},{10... | collective-permute-start | bytes 196616 | tf_op jit(solution)/shard_map/ppermute | solution.py:251
  31.0 1.2 %collective-permute-start.6 = (bf16[32,1024]{1,0:T(8,128)(2,1)S(1)}, bf16[32,1024]{1,0:T(8,128)(2,1)S(1)}, u32[]{:S(2)}, u32[]{:S(2)}) collective-permute-start(bf16[32,1024]{1,0:T(8,128)(2,1)S(1)} %shard_map.106.after_ref.refs_0_), channel_id=1, source_target_pairs={{0,16},{8,24},{16,0},{24,8},{1,17},{9,25},{17,1},{25,9},{2,18},{10... | collective-permute-start | bytes 196616 | tf_op jit(solution)/shard_map/ppermute | solution.py:251
  33.0 1.8 %shard_map.108.refs_4_.sum_ref = f32[1024,1024]{1,0:T(8,128)S(1)} custom-call(f32[1024,1024]{1,0:T(8,128)S(1)} %shard_map.104.after_ref.sum_ref, bf16[1024,2304]{1,0:T(8,128)(2,1)S(1)} %shard_map.102.after_ref.count_ref, bf16[128,1024]{1,0:T(8,128)(2,1)S(1)} %copy-done.5, bf16[128,1024]{1,0:T(8,128)(2,1)S(1)} %copy-done.3, ...), custom_call_target="tpu_custom_call" | custom-call | flops 5368709120 | bytes 8388608 | tf_op jit(solution)/shard_map/pallas_call | solution.py:309
  34.8 2.0 %collective-permute-start.10 = (bf16[128,512]{1,0:T(8,128)(2,1)S(1)}, bf16[128,512]{1,0:T(8,128)(2,1)S(1)}, u32[]{:S(2)}, u32[]{:S(2)}) collective-permute-start(bf16[128,512]{1,0:T(8,128)(2,1)S(1)} %shard_map.107.refs_5_), channel_id=1, source_target_pairs={{0,7},{1,6},{2,5},{3,4},{4,3},{5,2},{6,1},{7,0},{8,15},{9,14},{10,... | collective-permute-start | bytes 393224 | tf_op jit(solution)/shard_map/ppermute | solution.py:251
  37.3 4.9 %collective-permute-done.4.refs_0_ = bf16[128,1024]{1,0:T(8,128)(2,1)S(1)} collective-permute-done((bf16[128,1024]{1,0:T(8,128)(2,1)S(1)}, bf16[128,1024]{1,0:T(8,128)(2,1)S(1)}, u32[]{:S(2)}, u32[]{:S(2)}) %collective-permute-start.4) | collective-permute-done | bytes 262176 | tf_op jit(solution)/shard_map/ppermute | solution.py:251
  42.1 0.7 %shard_map.110.sum_ref.refs_2_ = f32[1024,1024]{1,0:T(8,128)S(1)} custom-call(f32[1024,1024]{1,0:T(8,128)S(1)} %shard_map.108.refs_4_.sum_ref, bf16[1024,2304]{1,0:T(8,128)(2,1)S(1)} %shard_map.102.after_ref.count_ref, bf16[128,1024]{1,0:T(8,128)(2,1)S(1)} %collective-permute-done.4.refs_0_, bf16[128,1024]{1,0:T(8,128)(2,1)S(1)} %shard_map.109.refs_1_.refs_0_), custom_call_target="tpu_custom_call" | custom-call | flops 17179869184 | bytes 8388608 | tf_op jit(solution)/shard_map/pallas_call | solution.py:309
  42.9 0.7 %shard_map.111.sum_ref.refs_1_.after_ref = f32[1024,1024]{1,0:T(8,128)S(1)} custom-call(f32[1024,1024]{1,0:T(8,128)S(1)} %shard_map.110.sum_ref.refs_2_, bf16[1024,2304]{1,0:T(8,128)(2,1)S(1)} %shard_map.102.after_ref.count_ref, bf16[128,1024]{1,0:T(8,128)(2,1)S(1)} %shard_map.109.refs_1_.refs_0_, bf16[128,1024]{1,0:T(8,128)(2,1)S(1)} %collective-permute-done.8.refs_1_, ...), custom_call_target="tpu_custom_call" | custom-call | flops 2147483648 | bytes 8388608 | tf_op jit(solution)/shard_map/pallas_call | solution.py:309
  44.0 1.3 %collective-permute-start.11 = (bf16[128,512]{1,0:T(8,128)(2,1)S(1)}, bf16[128,512]{1,0:T(8,128)(2,1)S(1)}, u32[]{:S(2)}, u32[]{:S(2)}) collective-permute-start(bf16[128,512]{1,0:T(8,128)(2,1)S(1)} %shard_map.114), channel_id=1, source_target_pairs={{0,7},{1,6},{2,5},{3,4},{4,3},{5,2},{6,1},{7,0},{8,15},{9,14},{10,... | collective-permute-start | bytes 393224 | tf_op jit(solution)/shard_map/ppermute | solution.py:251
  45.3 0.7 %shard_map.112.sum_ref = f32[1024,1024]{1,0:T(8,128)S(1)} custom-call(f32[1024,1024]{1,0:T(8,128)S(1)} %shard_map.111.sum_ref.refs_1_.after_ref, bf16[1024,2304]{1,0:T(8,128)(2,1)S(1)} %shard_map.102.after_ref.count_ref, bf16[128,1024]{1,0:T(8,128)(2,1)S(1)} %collective-permute-done.9.refs_0_, f32[1024,1024]{1,0:T(8,128)S(1)} %shard_map.111.sum_ref.refs_1_.after_ref), custom_call_target="tpu_custom_call" | custom-call | flops 1073741824 | bytes 8388608 | tf_op jit(solution)/shard_map/pallas_call | solution.py:309
  46.0 5.2 %collective-permute-done.10.block_ref = bf16[128,512]{1,0:T(8,128)(2,1)S(1)} collective-permute-done((bf16[128,512]{1,0:T(8,128)(2,1)S(1)}, bf16[128,512]{1,0:T(8,128)(2,1)S(1)}, u32[]{:S(2)}, u32[]{:S(2)}) %collective-permute-start.10) | collective-permute-done | bytes 131104 | tf_op jit(solution)/shard_map/ppermute | solution.py:251
  51.2 1.7 %shard_map.113.own_ref = f32[1024,1024]{1,0:T(8,128)S(1)} custom-call(f32[1024,1024]{1,0:T(8,128)S(1)} %shard_map.103.after_ref.own_ref, f32[1024,1024]{1,0:T(8,128)S(1)} %shard_map.112.sum_ref, bf16[1024,2304]{1,0:T(8,128)(2,1)S(1)} %shard_map.102.after_ref.count_ref, s32[3,1024]{1,0:T(4,128)S(1)} %copy-done.6, bf16[1024,1024]{1,0:T(8,128)(2,1)S(1)} %copy-done.1, ...), custom_call_target="tpu_custom_call" | custom-call | flops 4294967296 | bytes 8388608 | tf_op jit(solution)/shard_map/pallas_call | solution.py:353
  52.9 1.1 %collective-permute-done.11.block_ref = bf16[128,512]{1,0:T(8,128)(2,1)S(1)} collective-permute-done((bf16[128,512]{1,0:T(8,128)(2,1)S(1)}, bf16[128,512]{1,0:T(8,128)(2,1)S(1)}, u32[]{:S(2)}, u32[]{:S(2)}) %collective-permute-start.11) | collective-permute-done | bytes 131104 | tf_op jit(solution)/shard_map/ppermute | solution.py:251
  54.0 2.8 %shard_map.115 = bf16[1024,1024]{1,0:T(8,128)(2,1)} custom-call(f32[1024,1024]{1,0:T(8,128)S(1)} %shard_map.113.own_ref, f32[1024,1024]{1,0:T(8,128)S(1)} %shard_map.112.sum_ref, bf16[1024,2304]{1,0:T(8,128)(2,1)S(1)} %shard_map.102.after_ref.count_ref, s32[3,1024]{1,0:T(4,128)S(1)} %copy-done.6, bf16[1024,1024]{1,0:T(8,128)(2,1)S(1)} %copy-done.1, ...), custom_call_target="tpu_custom_call" | custom-call | flops 4294967296 | bytes 8388608 | tf_op jit(solution)/shard_map/pallas_call | solution.py:360
  (43 shorter events, 3.6 us)
Async XLA Ops:
  0.0 11.9 %copy-start.6 = (s32[3,1024]{1,0:T(4,128)S(1)}, s32[3,1024]{1,0:T(4,128)}, u32[]{:S(2)}) copy-start(s32[3,1024]{1,0:T(4,128)} %deg_ref.5) | copy-start | bytes 36868
  0.0 11.9 %copy-start.8 = (s32[1024,16]{0,1:T(8,128)S(1)}, s32[1024,16]{0,1:T(8,128)}, u32[]{:S(2)}) copy-start(s32[1024,16]{0,1:T(8,128)} %param.17) | copy-start | bytes 196612
  0.0 11.9 %copy-start.7 = (s32[1024,16]{0,1:T(8,128)S(1)}, s32[1024,16]{0,1:T(8,128)}, u32[]{:S(2)}) copy-start(s32[1024,16]{0,1:T(8,128)} %param.16) | copy-start | bytes 196612
  0.0 11.9 %copy-start.11 = (s32[1024,8]{0,1:T(8,128)S(1)}, s32[1024,8]{0,1:T(8,128)}, u32[]{:S(2)}) copy-start(s32[1024,8]{0,1:T(8,128)} %param.15) | copy-start | bytes 98308
  3.0 18.7 %copy-start = (bf16[1024,1024]{1,0:T(8,128)(2,1)S(1)}, bf16[1024,1024]{1,0:T(8,128)(2,1)}, u32[]{:S(2)}) copy-start(bf16[1024,1024]{1,0:T(8,128)(2,1)} %feat_ref.9) | copy-start | bytes 6291460
  3.0 2.1 %collective-permute-start = (bf16[128,1024]{1,0:T(8,128)(2,1)}, bf16[128,1024]{1,0:T(8,128)(2,1)S(1)}, u32[]{:S(2)}, u32[]{:S(2)}) collective-permute-start(bf16[128,1024]{1,0:T(8,128)(2,1)} %get-tuple-element.14), channel_id=1, source_target_pairs={{0,1},{1,0},{2,3},{3,2},{4,5},{5,4},{6,7},{7,6},{8,9},{9,8},{10,11... | collective-permute-start | bytes 786440 | tf_op jit(solution)/shard_map/ppermute | solution.py:251
  3.7 26.0 %collective-permute-start.3 = (bf16[136,1024]{1,0:T(8,128)(2,1)}, bf16[136,1024]{1,0:T(8,128)(2,1)S(1)}, u32[]{:S(2)}, u32[]{:S(2)}) collective-permute-start(bf16[136,1024]{1,0:T(8,128)(2,1)} %get-tuple-element.18), channel_id=1, source_target_pairs={{0,6},{1,7},{2,4},{3,5},{4,2},{5,3},{6,0},{7,1},{8,14},{9,15},{10,... | collective-permute-start | bytes 835592 | tf_op jit(solution)/shard_map/ppermute | solution.py:251
  9.1 20.7 %collective-permute-start.1 = (bf16[136,1024]{1,0:T(8,128)(2,1)}, bf16[136,1024]{1,0:T(8,128)(2,1)S(1)}, u32[]{:S(2)}, u32[]{:S(2)}) collective-permute-start(bf16[136,1024]{1,0:T(8,128)(2,1)} %get-tuple-element.16), channel_id=1, source_target_pairs={{0,4},{1,5},{2,6},{3,7},{4,0},{5,1},{6,2},{7,3},{8,12},{9,13},{10,... | collective-permute-start | bytes 835592 | tf_op jit(solution)/shard_map/ppermute | solution.py:251
  11.9 17.9 %collective-permute-start.2 = (bf16[136,1024]{1,0:T(8,128)(2,1)}, bf16[136,1024]{1,0:T(8,128)(2,1)S(1)}, u32[]{:S(2)}, u32[]{:S(2)}) collective-permute-start(bf16[136,1024]{1,0:T(8,128)(2,1)} %get-tuple-element.17), channel_id=1, source_target_pairs={{0,2},{1,3},{2,0},{3,1},{4,6},{5,7},{6,4},{7,5},{8,10},{9,11},{10,... | collective-permute-start | bytes 835592 | tf_op jit(solution)/shard_map/ppermute | solution.py:251
  11.9 1.0 %copy-start.4 = (bf16[128,1024]{1,0:T(8,128)(2,1)S(1)}, bf16[128,1024]{1,0:T(8,128)(2,1)}, u32[]{:S(2)}) copy-start(bf16[128,1024]{1,0:T(8,128)(2,1)} %get-tuple-element.15.after_ref.refs_0_) | copy-start | bytes 786436
  12.8 8.9 %copy-start.12 = (bf16[1024,1024]{1,0:T(8,128)(2,1)S(1)}, bf16[1024,1024]{1,0:T(8,128)(2,1)}, u32[]{:S(2)}) copy-start(bf16[1024,1024]{1,0:T(8,128)(2,1)} %w_ref.3) | copy-start | bytes 6291460
  24.1 2.3 %copy-start.10 = (s32[1,8,128]{2,1,0:T(8,128)S(1)}, s32[1,8,128]{2,1,0:T(8,128)}, u32[]{:S(2)}) copy-start(s32[1,8,128]{2,1,0:T(8,128)} %param.19) | copy-start | bytes 12292
  26.4 3.4 %copy-start.9 = (bf16[8,1024]{1,0:T(8,128)(2,1)S(1)}, bf16[8,1024]{1,0:T(8,128)(2,1)}, u32[]{:S(2)}) copy-start(bf16[8,1024]{1,0:T(8,128)(2,1)} %get-tuple-element.13.hub_hbm.refs_0_) | copy-start | bytes 49156
  27.4 5.6 %copy-start.3 = (bf16[128,1024]{1,0:T(8,128)(2,1)S(1)}, bf16[128,1024]{1,0:T(8,128)(2,1)}, u32[]{:S(2)}) copy-start(bf16[128,1024]{1,0:T(8,128)(2,1)} %copy-done.2) | copy-start | bytes 786436
  27.4 5.6 %copy-start.5 = (bf16[128,1024]{1,0:T(8,128)(2,1)S(1)}, bf16[128,1024]{1,0:T(8,128)(2,1)}, u32[]{:S(2)}) copy-start(bf16[128,1024]{1,0:T(8,128)(2,1)} %get-tuple-element.15.after_ref.refs_0_) | copy-start | bytes 786436
  27.4 17.9 %collective-permute-start.9 = (bf16[128,1024]{1,0:T(8,128)(2,1)S(1)}, bf16[128,1024]{1,0:T(8,128)(2,1)S(1)}, u32[]{:S(2)}, u32[]{:S(2)}) collective-permute-start(bf16[128,1024]{1,0:T(8,128)(2,1)S(1)} %get-tuple-element.20), channel_id=1, source_target_pairs={{0,5},{1,4},{2,7},{3,6},{4,1},{5,0},{6,3},{7,2},{8,13},{9,12},{10,... | collective-permute-start | bytes 786440 | tf_op jit(solution)/shard_map/ppermute | solution.py:251
  29.2 13.0 %collective-permute-start.4 = (bf16[128,1024]{1,0:T(8,128)(2,1)S(1)}, bf16[128,1024]{1,0:T(8,128)(2,1)S(1)}, u32[]{:S(2)}, u32[]{:S(2)}) collective-permute-start(bf16[128,1024]{1,0:T(8,128)(2,1)S(1)} %get-tuple-element.19.refs_4_), channel_id=1, source_target_pairs={{0,3},{1,2},{2,1},{3,0},{4,7},{5,6},{6,5},{7,4},{8,11},{9,10},{10,... | collective-permute-start | bytes 786440 | tf_op jit(solution)/shard_map/ppermute | solution.py:251
  29.8 5.0 %collective-permute-start.7 = (bf16[32,1024]{1,0:T(8,128)(2,1)S(1)}, bf16[32,1024]{1,0:T(8,128)(2,1)S(1)}, u32[]{:S(2)}, u32[]{:S(2)}) collective-permute-start(bf16[32,1024]{1,0:T(8,128)(2,1)S(1)} %shard_map.106.after_ref.refs_0_), channel_id=1, source_target_pairs={{0,24},{8,16},{16,8},{24,0},{1,25},{9,17},{17,9},{25,1},{2,26},{10... | collective-permute-start | bytes 196616 | tf_op jit(solution)/shard_map/ppermute | solution.py:251
  31.0 5.8 %collective-permute-start.6 = (bf16[32,1024]{1,0:T(8,128)(2,1)S(1)}, bf16[32,1024]{1,0:T(8,128)(2,1)S(1)}, u32[]{:S(2)}, u32[]{:S(2)}) collective-permute-start(bf16[32,1024]{1,0:T(8,128)(2,1)S(1)} %shard_map.106.after_ref.refs_0_), channel_id=1, source_target_pairs={{0,16},{8,24},{16,0},{24,8},{1,17},{9,25},{17,1},{25,9},{2,18},{10... | collective-permute-start | bytes 196616 | tf_op jit(solution)/shard_map/ppermute | solution.py:251
  32.3 4.6 %collective-permute-start.5 = (bf16[32,1024]{1,0:T(8,128)(2,1)S(1)}, bf16[32,1024]{1,0:T(8,128)(2,1)S(1)}, u32[]{:S(2)}, u32[]{:S(2)}) collective-permute-start(bf16[32,1024]{1,0:T(8,128)(2,1)S(1)} %shard_map.106.after_ref.refs_0_), channel_id=1, source_target_pairs={{0,8},{8,0},{16,24},{24,16},{1,9},{9,1},{17,25},{25,17},{2,10},{10... | collective-permute-start | bytes 196616 | tf_op jit(solution)/shard_map/ppermute | solution.py:251
  34.8 16.4 %collective-permute-start.10 = (bf16[128,512]{1,0:T(8,128)(2,1)S(1)}, bf16[128,512]{1,0:T(8,128)(2,1)S(1)}, u32[]{:S(2)}, u32[]{:S(2)}) collective-permute-start(bf16[128,512]{1,0:T(8,128)(2,1)S(1)} %shard_map.107.refs_5_), channel_id=1, source_target_pairs={{0,7},{1,6},{2,5},{3,4},{4,3},{5,2},{6,1},{7,0},{8,15},{9,14},{10,... | collective-permute-start | bytes 393224 | tf_op jit(solution)/shard_map/ppermute | solution.py:251
  36.9 6.0 %collective-permute-start.8 = (bf16[128,1024]{1,0:T(8,128)(2,1)S(1)}, bf16[128,1024]{1,0:T(8,128)(2,1)S(1)}, u32[]{:S(2)}, u32[]{:S(2)}) collective-permute-start(bf16[128,1024]{1,0:T(8,128)(2,1)S(1)} %shard_map.109.refs_1_.refs_0_), channel_id=1, source_target_pairs={{0,1},{1,0},{2,3},{3,2},{4,5},{5,4},{6,7},{7,6},{8,9},{9,8},{10,11... | collective-permute-start | bytes 786440 | tf_op jit(solution)/shard_map/ppermute | solution.py:251
  44.0 7.2 %copy-start.1 = (bf16[1024,1024]{1,0:T(8,128)(2,1)S(1)}, bf16[1024,1024]{1,0:T(8,128)(2,1)}, u32[]{:S(2)}) copy-start(bf16[1024,1024]{1,0:T(8,128)(2,1)} %w_ref.5) | copy-start | bytes 6291460
  44.0 10.0 %collective-permute-start.11 = (bf16[128,512]{1,0:T(8,128)(2,1)S(1)}, bf16[128,512]{1,0:T(8,128)(2,1)S(1)}, u32[]{:S(2)}, u32[]{:S(2)}) collective-permute-start(bf16[128,512]{1,0:T(8,128)(2,1)S(1)} %shard_map.114), channel_id=1, source_target_pairs={{0,7},{1,6},{2,5},{3,4},{4,3},{5,2},{6,1},{7,0},{8,15},{9,14},{10,... | collective-permute-start | bytes 393224 | tf_op jit(solution)/shard_map/ppermute | solution.py:251
  (1 other events, 0.7 us)

commit v5 on v4

--- a/solution.py
+++ b/solution.py
@@ -9,6 +9,7 @@
 
 LANES = 128
 HUB_PAD = 8
+HUB_COPY = 16
 CHUNKS = 4
 VM = pl.BlockSpec(memory_space=pltpu.VMEM)
 ANY = pl.BlockSpec(memory_space=pl.ANY)
@@ -43,9 +44,9 @@
 
 
 def hub_matrix(hub_ref, rows_here):
-    row_at = lax.broadcasted_iota(I32, (HUB_PAD, rows_here), 1)
-    line = lax.broadcasted_iota(I32, (HUB_PAD, rows_here), 0)
-    hit = jnp.zeros((HUB_PAD, rows_here), F32)
+    row_at = lax.broadcasted_iota(I32, (HUB_COPY, rows_here), 1)
+    line = lax.broadcasted_iota(I32, (HUB_COPY, rows_here), 0)
+    hit = jnp.zeros((HUB_COPY, rows_here), F32)
     for h in range(hub_ref.shape[0]):
         hit = hit + jnp.where((line == h) & (row_at == hub_ref[h]), 1.0, 0.0)
     return hit.astype(BF)
@@ -89,7 +90,7 @@
     hub_out[...] = hubs
     for n in range(len(shifts)):
         block = picked[n * caps : (n + 1) * caps]
-        outs[n][...] = jnp.concatenate([block, hubs], axis=0) if shifts[n] % 2 == 0 else block
+        outs[n][...] = jnp.concatenate([block, hubs[:HUB_PAD]], axis=0) if shifts[n] % 2 == 0 else block
 
 
 def near_kernel(shifts, rows_hbm, hub_hbm, feat_hbm, after_ref, *refs):
@@ -100,7 +101,7 @@
     picked = picked_rows([pick_matrix(rows_ref, shift, feat_ref.shape[0]) for shift in shifts], feat_ref, large)
     for n, shift in enumerate(shifts):
         block = picked[n * caps : (n + 1) * caps]
-        outs[n][...] = jnp.concatenate([block, hub_ref[...]], axis=0) if shift and shift % 2 == 0 else block
+        outs[n][...] = jnp.concatenate([block, hub_ref[...][:HUB_PAD]], axis=0) if shift and shift % 2 == 0 else block
 
 
 def rest_kernel(shifts, cols, rows_ref, feat_ref, after_ref, *outs):
@@ -111,13 +112,12 @@
         outs[n][...] = picked[n * caps : (n + 1) * caps]
 
 
-def join_kernel(starts, *refs):
+def join_kernel(spans, *refs):
     out_ref = refs[-1]
     at = 0
-    for start, ref in zip(starts, refs):
-        size = ref.shape[0] - start
-        out_ref[at : at + size, :] = ref[start:, :]
-        at += size
+    for (start, stop), ref in zip(spans, refs):
+        out_ref[at : at + stop - start, :] = ref[start:stop, :]
+        at += stop - start
 
 
 def add_counts(index, width, out_ref, row, column):
@@ -200,26 +200,30 @@
         )
 
 
-def mean_part(span, at, cols, sum_ref, count_ref, deg_ref, w_ref, block_ref, value):
-    deg = deg_ref[0:1, span] + deg_ref[1:2, span] + deg_ref[2:3, span]
-    scale = column_of(1.0 / deg.astype(F32), deg.shape[1])
-    counts = count_ref[span, at : at + block_ref.shape[0]]
-    total = sum_ref[span, cols] + jnp.dot(counts, block_ref[...], preferred_element_type=F32)
-    mean = (total * scale).astype(BF)
-    return value + jnp.dot(mean, w_ref[cols, :], preferred_element_type=F32)
-
-
-def late_kernel(rb, at, cols, own_ref, sum_ref, count_ref, deg_ref, w_ref, block_ref, out_ref):
+def means(at, cols, sum_ref, count_ref, deg_ref, block_ref, mean_ref):
+    rb = 512
     for i in range(sum_ref.shape[0] // rb):
         span = pl.ds(i * rb, rb)
-        out_ref[span, :] = mean_part(span, at, cols, sum_ref, count_ref, deg_ref, w_ref, block_ref, own_ref[span, :])
-
-
-def last_kernel(rb, at, cols, own_ref, sum_ref, count_ref, deg_ref, w_ref, block_ref, out_hbm, out_ref, sems):
+        deg = deg_ref[0:1, span] + deg_ref[1:2, span] + deg_ref[2:3, span]
+        scale = column_of(1.0 / deg.astype(F32), rb)
+        counts = count_ref[span, at : at + block_ref.shape[0]]
+        total = sum_ref[span, cols] + jnp.dot(counts, block_ref[...], preferred_element_type=F32)
+        mean_ref[span, :] = (total * scale).astype(BF)
+
+
+def late_kernel(rb, at, cols, own_ref, sum_ref, count_ref, deg_ref, w_ref, block_ref, out_ref, mean_ref):
+    means(at, cols, sum_ref, count_ref, deg_ref, block_ref, mean_ref)
+    for i in range(sum_ref.shape[0] // rb):
+        span = pl.ds(i * rb, rb)
+        out_ref[span, :] = own_ref[span, :] + jnp.dot(mean_ref[span, :], w_ref[cols, :], preferred_element_type=F32)
+
+
+def last_kernel(rb, at, cols, own_ref, sum_ref, count_ref, deg_ref, w_ref, block_ref, out_hbm, mean_ref, out_ref, sems):
+    means(at, cols, sum_ref, count_ref, deg_ref, block_ref, mean_ref)
     copies = []
     for i in range(sum_ref.shape[0] // rb):
         span = pl.ds(i * rb, rb)
-        value = mean_part(span, at, cols, sum_ref, count_ref, deg_ref, w_ref, block_ref, own_ref[span, :])
+        value = own_ref[span, :] + jnp.dot(mean_ref[span, :], w_ref[cols, :], preferred_element_type=F32)
         out_ref[span, :] = jnp.maximum(value, 0.0).astype(BF)
         copies.append(pltpu.make_async_copy(out_ref.at[span, :], out_hbm.at[span, :], sems.at[i]))
         copies[-1].start()
@@ -254,7 +258,7 @@
     plain, carrier = vec((caps, width), BF), vec((caps + HUB_PAD, width), BF)
     firsts = call(
         functools.partial(first_kernel, far + [1]),
-        [carrier] * len(far) + [plain, vec((HUB_PAD, width), BF)],
+        [carrier] * len(far) + [plain, vec((HUB_COPY, width), BF)],
         [HBM] * 3,
         0,
         2 * rows_here * width,
@@ -270,7 +274,7 @@
         0,
         2 * rows_here * width,
         limit=60,
-        scratch=[pltpu.VMEM((peers, caps), I32), pltpu.VMEM((HUB_PAD, width), BF)] + scratch,
+        scratch=[pltpu.VMEM((peers, caps), I32), pltpu.VMEM((HUB_COPY, width), BF)] + scratch,
     )(rows, hubs, features, got[1])
     for shift, block in zip(near, nears):
         got[shift] = swap(block, "member", shift)
@@ -284,26 +288,25 @@
         2 * rows_here * (rows_here + hub_slots + peers * caps),
     )(local_nbrs.T, hub_nbrs.T, halo_nbrs.T, degrees, got[0])
 
-    def rest(shifts, cols, after):
+    def rest(shifts, cols, after, weight=1):
         return call(
             functools.partial(rest_kernel, shifts, cols),
             [vec((caps, cols.stop - cols.start), BF)] * len(shifts),
             [VM] * 2 + [ANY],
-            2 * len(shifts) * caps * rows_here * width,
+            weight * 2 * len(shifts) * caps * rows_here * width,
             2 * rows_here * width,
         )(rows, features, after)
 
-    def join(*blocks, starts=None, after=()):
-        starts = starts or [0] * len(blocks)
-        total = sum(b.shape[0] - s for b, s in zip(blocks, starts))
+    def join(blocks, spans, after):
+        total = sum(stop - start for start, stop in spans)
         return call(
-            functools.partial(join_kernel, starts),
+            functools.partial(join_kernel, spans),
             vec((total, width), BF),
-            [VM] * len(blocks) + [ANY] * len(after),
+            [VM] * len(blocks) + [ANY],
             0,
             4 * total * width,
             limit=4,
-        )(*blocks, *after)
+        )(*blocks, after)
 
     def add(total, blocks, sizes, at, after, weight=1):
         return call(
@@ -334,20 +337,17 @@
         got[shift] = swap(block, "member", shift)
 
     evens = [got[s] for s in range(2, peers, 2)]
-    hubs = join(hubs, *evens, starts=[0] + [caps] * len(evens), after=[odd[0]])
+    hubs = join([hubs, *evens], [(0, HUB_PAD)] + [(caps, caps + HUB_PAD)] * len(evens), odd[0])
     lines = [swap(hubs, "group", shift) for shift in range(1, groups)]
-    late = rest([last], spans[0], hubs)
-    total = add(total, [got[s] for s in early], [caps] * len(early), rows_here, late[0])
-    hubs = join(hubs, *lines, after=[total])
+    late = rest([last], spans[0], hubs, 32)
+    hubs = join([hubs, *lines], [(0, hubs.shape[0])] * groups, late[0])
     other_hubs = swap(hubs, "member", 1)
-    soon, far_odd = other[:-1] if len(other) > 2 else other[:1], other[-1:]
-    at = rows_here + caps * order.index(soon[0])
-    total = add(total, [got[s] for s in soon], [caps] * len(soon), at, hubs, 16)
+    total = add(total, [got[s] for s in early], [caps] * len(early), rows_here, hubs, 16)
     total = add(total, [hubs, other_hubs], [hub_slots // 2] * 2, rows_here + caps * peers, total)
     late += rest([last], spans[1], total)
     late = [swap(block, "member", last) for block in late]
-    at = rows_here + caps * order.index(far_odd[0])
-    total = add(total, [got[s] for s in far_odd], [caps] * len(far_odd), at, total)
+    at = rows_here + caps * order.index(other[0])
+    total = add(total, [got[s] for s in other], [caps] * len(other), at, total)
 
     at = rows_here + caps * order.index(last)
     value = call(
@@ -356,6 +356,7 @@
         [VM] * 6,
         2 * rows_here * spans[0].stop * width,
         8 * rows_here * width,
+        scratch=[pltpu.VMEM((rows_here, spans[0].stop), BF)],
     )(own, total, counts, degrees, w_neigh, late[0])
     return call(
         functools.partial(last_kernel, 256, at, spans[1]),
@@ -363,7 +364,11 @@
         [VM] * 6,
         2 * rows_here * (width - spans[1].start) * width,
         8 * rows_here * width,
-        scratch=[pltpu.VMEM((rows_here, width), BF), pltpu.SemaphoreType.DMA((rows_here // 256,))],
+        scratch=[
+            pltpu.VMEM((rows_here, width - spans[1].start), BF),
+            pltpu.VMEM((rows_here, width), BF),
+            pltpu.SemaphoreType.DMA((rows_here // 256,)),
+        ],
         out_specs=ANY,
     )(value, total, counts, degrees, w_neigh, late[1])
 

time: 57.2 us -> 56.8 us (level)
  Pallas kernels: 29.9 us -> 28.7 us
    pallas_call x4 -> x3, Pallas kernels: 3.89 us -> 3.22 us  [add(): call(functools.partial(sum_kernel, 512, sizes, at), vec((rows_here, width...]
  transfers between devices with their start and end apart: 12 -> 12, of which waited for: 4 -> 5; matrix products, arithmetic and copies ran while one was open for 1% -> 1% of each run, Pallas kernels for 42% -> 41%
where the time goes in v5:
time: 56.8 us; the launch traced here: 56.6 us
  Pallas kernels  28.7 us (51%)
  starting transfers between devices  12.8 us (23%)
  waiting for transfers between devices  12.2 us (21%)
  local copies, waits for them, and re-layouts  2.39 us (4%)
    ppermute x12, starting transfers between devices, swap(): return lax.ppermute(block, axis, [(i, i ^ shift) for i in range(size)])  12.8 us
    ppermute x12, waiting for transfers between devices, swap(): return lax.ppermute(block, axis, [(i, i ^ shift) for i in range(size)])  12.2 us
    pallas_call x1, Pallas kernels, per_device(): call(functools.partial(table_kernel, 2 * LANES, peers, caps, hub_dev, mag...  8.86 us
    pallas_call x1, Pallas kernels, per_device(): call(functools.partial(near_kernel, near + [0]), [plain if shift % 2 else...  3.25 us
    pallas_call x3, Pallas kernels, add(): call(functools.partial(sum_kernel, 512, sizes, at), vec((rows_here, width...  3.22 us
    pallas_call x1, Pallas kernels, per_device(): call(functools.partial(first_kernel, far + [1]), [carrier] * len(far) + [...  2.96 us
    pallas_call x1, Pallas kernels, per_device(): call(functools.partial(last_kernel, 256, at, spans[1]), vec((rows_here, w...  2.4 us
    pallas_call x1, Pallas kernels, per_device(): call(functools.partial(own_kernel, 512), vec((rows_here, width), F32), [V...  2.34 us
  transfers between devices with their start and end apart: 12, of which 5 were waited for; matrix products, arithmetic and copies ran while one was open for 1% of the time, Pallas kernels for 41%

profile of v5, /device:TPU:21, one launch (start us, length us, event | category | flops | bytes accessed | tf_op | source)
XLA Modules:
  0.0 56.6 jit_solution(11483594947247002644)
XLA Ops:
  0.0 3.0 %shard_map.100 = (bf16[136,1024]{1,0:T(8,128)(2,1)}, bf16[128,1024]{1,0:T(8,128)(2,1)}, bf16[16,1024]{1,0:T(8,128)(2,1)}) custom-call(s32[8,128]{1,0:T(8,128)} %bitcast.6, s32[6]{0:T(128)} %hub_hbm.1, bf16[1024,1024]{1,0:T(8,128)(2,1)} %feat_ref.9), custom_call_target="tpu_custom_call" | custom-call | bytes 2097152 | tf_op jit(solution)/shard_map/pallas_call | solution.py:259
  3.0 0.7 %collective-permute-start = (bf16[128,1024]{1,0:T(8,128)(2,1)}, bf16[128,1024]{1,0:T(8,128)(2,1)S(1)}, u32[]{:S(2)}, u32[]{:S(2)}) collective-permute-start(bf16[128,1024]{1,0:T(8,128)(2,1)} %get-tuple-element.14), channel_id=1, source_target_pairs={{0,1},{1,0},{2,3},{3,2},{4,5},{5,4},{6,7},{7,6},{8,9},{9,8},{10,11... | collective-permute-start | bytes 786440 | tf_op jit(solution)/shard_map/ppermute | solution.py:255
  5.1 0.7 %copy-done.2 = bf16[128,1024]{1,0:T(8,128)(2,1)} copy-done((bf16[128,1024]{1,0:T(8,128)(2,1)}, bf16[128,1024]{1,0:T(8,128)(2,1)S(1)}, u32[]{:S(2)}) %copy-start.2) | copy-done | bytes 262168
  5.8 3.2 %shard_map.101 = (bf16[136,1024]{1,0:T(8,128)(2,1)}, bf16[136,1024]{1,0:T(8,128)(2,1)}, bf16[128,1024]{1,0:T(8,128)(2,1)}) custom-call(s32[8,128]{1,0:T(8,128)} %bitcast.7, bf16[16,1024]{1,0:T(8,128)(2,1)} %get-tuple-element.13.hub_hbm.refs_0_, bf16[1024,1024]{1,0:T(8,128)(2,1)} %feat_ref.9, bf16[128,1024]{1,0:T(8,128)(2,1)} %copy-done.2), custom_call_target="tpu_custom_call" | custom-call | bytes 2097152 | tf_op jit(solution)/shard_map/pallas_call | solution.py:270
  9.1 2.8 %collective-permute-start.1 = (bf16[136,1024]{1,0:T(8,128)(2,1)}, bf16[136,1024]{1,0:T(8,128)(2,1)S(1)}, u32[]{:S(2)}, u32[]{:S(2)}) collective-permute-start(bf16[136,1024]{1,0:T(8,128)(2,1)} %get-tuple-element.16), channel_id=1, source_target_pairs={{0,4},{1,5},{2,6},{3,7},{4,0},{5,1},{6,2},{7,3},{8,12},{9,13},{10,... | collective-permute-start | bytes 835592 | tf_op jit(solution)/shard_map/ppermute | solution.py:255
  11.9 0.9 %copy-done.4 = bf16[128,1024]{1,0:T(8,128)(2,1)S(1)} copy-done((bf16[128,1024]{1,0:T(8,128)(2,1)S(1)}, bf16[128,1024]{1,0:T(8,128)(2,1)}, u32[]{:S(2)}) %copy-start.4) | copy-done | bytes 262168
  12.8 8.9 %shard_map.102.after_ref.count_ref = bf16[1024,2304]{1,0:T(8,128)(2,1)S(1)} custom-call(s32[16,1024]{1,0:T(8,128)S(1)} %bitcast.4, s32[8,1024]{1,0:T(8,128)S(1)} %bitcast.11, s32[16,1024]{1,0:T(8,128)S(1)} %bitcast.5, s32[3,1024]{1,0:T(4,128)S(1)} %copy-done.6, bf16[128,1024]{1,0:T(8,128)(2,1)S(1)} %copy-done.4), custom_call_target="tpu_custom_call" | custom-call | flops 201326592 | bytes 4718592 | tf_op jit(solution)/shard_map/pallas_call | solution.py:283
  21.7 2.3 %shard_map.103.after_ref.own_ref = f32[1024,1024]{1,0:T(8,128)S(1)} custom-call(bf16[1024,1024]{1,0:T(8,128)(2,1)S(1)} %copy-done, bf16[1024,1024]{1,0:T(8,128)(2,1)S(1)} %copy-done.12, bf16[1,1024]{1,0:T(2,128)(2,1)S(1)} %reshape.6.bias_ref, bf16[1024,2304]{1,0:T(8,128)(2,1)S(1)} %shard_map.102.after_ref.count_ref), custom_call_target="tpu_custom_call" | custom-call | flops 8589934592 | bytes 8388608 | tf_op jit(solution)/shard_map/pallas_call | solution.py:321
  24.1 2.3 %shard_map.104.after_ref.sum_ref = f32[1024,1024]{1,0:T(8,128)S(1)} custom-call(bf16[1024,1024]{1,0:T(8,128)(2,1)S(1)} %copy-done, bf16[1024,2304]{1,0:T(8,128)(2,1)S(1)} %shard_map.102.after_ref.count_ref, f32[1024,1024]{1,0:T(8,128)S(1)} %shard_map.103.after_ref.own_ref), custom_call_target="tpu_custom_call" | custom-call | flops 8589934592 | bytes 8388608 | tf_op jit(solution)/shard_map/pallas_call | solution.py:328
  26.4 0.9 %shard_map.105 = (bf16[128,1024]{1,0:T(8,128)(2,1)S(1)}, bf16[128,1024]{1,0:T(8,128)(2,1)S(1)}) custom-call(s32[8,128]{1,0:T(8,128)S(1)} %bitcast.8, bf16[1024,1024]{1,0:T(8,128)(2,1)S(1)} %copy-done, f32[1024,1024]{1,0:T(8,128)S(1)} %shard_map.104.after_ref.sum_ref), custom_call_target="tpu_custom_call" | custom-call | flops 2147483648 | bytes 2097152 | tf_op jit(solution)/shard_map/pallas_call | solution.py:292
  27.4 1.8 %collective-permute-start.9 = (bf16[128,1024]{1,0:T(8,128)(2,1)S(1)}, bf16[128,1024]{1,0:T(8,128)(2,1)S(1)}, u32[]{:S(2)}, u32[]{:S(2)}) collective-permute-start(bf16[128,1024]{1,0:T(8,128)(2,1)S(1)} %get-tuple-element.20), channel_id=1, source_target_pairs={{0,5},{1,4},{2,7},{3,6},{4,1},{5,0},{6,3},{7,2},{8,13},{9,12},{10,... | collective-permute-start | bytes 786440 | tf_op jit(solution)/shard_map/ppermute | solution.py:255
  29.8 1.2 %collective-permute-start.6 = (bf16[32,1024]{1,0:T(8,128)(2,1)S(1)}, bf16[32,1024]{1,0:T(8,128)(2,1)S(1)}, u32[]{:S(2)}, u32[]{:S(2)}) collective-permute-start(bf16[32,1024]{1,0:T(8,128)(2,1)S(1)} %shard_map.106.after_ref.refs_0_), channel_id=1, source_target_pairs={{0,24},{8,16},{16,8},{24,0},{1,25},{9,17},{17,9},{25,1},{2,26},{10... | collective-permute-start | bytes 196616 | tf_op jit(solution)/shard_map/ppermute | solution.py:255
  31.0 1.2 %collective-permute-start.5 = (bf16[32,1024]{1,0:T(8,128)(2,1)S(1)}, bf16[32,1024]{1,0:T(8,128)(2,1)S(1)}, u32[]{:S(2)}, u32[]{:S(2)}) collective-permute-start(bf16[32,1024]{1,0:T(8,128)(2,1)S(1)} %shard_map.106.after_ref.refs_0_), channel_id=1, source_target_pairs={{0,16},{8,24},{16,0},{24,8},{1,17},{9,25},{17,1},{25,9},{2,18},{10... | collective-permute-start | bytes 196616 | tf_op jit(solution)/shard_map/ppermute | solution.py:255
  33.0 1.4 %collective-permute-done.6.refs_3_ = bf16[32,1024]{1,0:T(8,128)(2,1)S(1)} collective-permute-done((bf16[32,1024]{1,0:T(8,128)(2,1)S(1)}, bf16[32,1024]{1,0:T(8,128)(2,1)S(1)}, u32[]{:S(2)}, u32[]{:S(2)}) %collective-permute-start.6) | collective-permute-done | bytes 65568 | tf_op jit(solution)/shard_map/ppermute | solution.py:255
  34.3 2.1 %collective-permute-start.10 = (bf16[128,512]{1,0:T(8,128)(2,1)S(1)}, bf16[128,512]{1,0:T(8,128)(2,1)S(1)}, u32[]{:S(2)}, u32[]{:S(2)}) collective-permute-start(bf16[128,512]{1,0:T(8,128)(2,1)S(1)} %shard_map.107.refs_4_), channel_id=1, source_target_pairs={{0,7},{1,6},{2,5},{3,4},{4,3},{5,2},{6,1},{7,0},{8,15},{9,14},{10,... | collective-permute-start | bytes 393224 | tf_op jit(solution)/shard_map/ppermute | solution.py:255
  36.4 0.9 %collective-permute-start.7 = (bf16[128,1024]{1,0:T(8,128)(2,1)S(1)}, bf16[128,1024]{1,0:T(8,128)(2,1)S(1)}, u32[]{:S(2)}, u32[]{:S(2)}) collective-permute-start(bf16[128,1024]{1,0:T(8,128)(2,1)S(1)} %shard_map.108.refs_5_.refs_0_), channel_id=1, source_target_pairs={{0,1},{1,0},{2,3},{3,2},{4,5},{5,4},{6,7},{7,6},{8,9},{9,8},{10,11... | collective-permute-start | bytes 786440 | tf_op jit(solution)/shard_map/ppermute | solution.py:255
  37.3 1.8 %shard_map.109.sum_ref.refs_2_ = f32[1024,1024]{1,0:T(8,128)S(1)} custom-call(f32[1024,1024]{1,0:T(8,128)S(1)} %shard_map.104.after_ref.sum_ref, bf16[1024,2304]{1,0:T(8,128)(2,1)S(1)} %shard_map.102.after_ref.count_ref, bf16[128,1024]{1,0:T(8,128)(2,1)S(1)} %copy-done.5, bf16[128,1024]{1,0:T(8,128)(2,1)S(1)} %copy-done.3, ...), custom_call_target="tpu_custom_call" | custom-call | flops 85899345920 | bytes 8388608 | tf_op jit(solution)/shard_map/pallas_call | solution.py:312
  39.1 0.7 %shard_map.110.sum_ref.refs_2_.after_ref = f32[1024,1024]{1,0:T(8,128)S(1)} custom-call(f32[1024,1024]{1,0:T(8,128)S(1)} %shard_map.109.sum_ref.refs_2_, bf16[1024,2304]{1,0:T(8,128)(2,1)S(1)} %shard_map.102.after_ref.count_ref, bf16[128,1024]{1,0:T(8,128)(2,1)S(1)} %shard_map.108.refs_5_.refs_0_, bf16[128,1024]{1,0:T(8,128)(2,1)S(1)} %collective-permute-done.7.refs_1_, ...), custom_call_target="tpu_custom_call" | custom-call | flops 2147483648 | bytes 8388608 | tf_op jit(solution)/shard_map/pallas_call | solution.py:312
  40.3 1.1 %collective-permute-start.11 = (bf16[128,512]{1,0:T(8,128)(2,1)S(1)}, bf16[128,512]{1,0:T(8,128)(2,1)S(1)}, u32[]{:S(2)}, u32[]{:S(2)}) collective-permute-start(bf16[128,512]{1,0:T(8,128)(2,1)S(1)} %shard_map.113), channel_id=1, source_target_pairs={{0,7},{1,6},{2,5},{3,4},{4,3},{5,2},{6,1},{7,0},{8,15},{9,14},{10,... | collective-permute-start | bytes 393224 | tf_op jit(solution)/shard_map/ppermute | solution.py:255
  42.1 0.7 %shard_map.111.sum_ref = f32[1024,1024]{1,0:T(8,128)S(1)} custom-call(f32[1024,1024]{1,0:T(8,128)S(1)} %shard_map.110.sum_ref.refs_2_.after_ref, bf16[1024,2304]{1,0:T(8,128)(2,1)S(1)} %shard_map.102.after_ref.count_ref, bf16[128,1024]{1,0:T(8,128)(2,1)S(1)} %collective-permute-done.8.refs_0_, bf16[128,1024]{1,0:T(8,128)(2,1)S(1)} %collective-permute-done.9.refs_1_, ...), custom_call_target="tpu_custom_call" | custom-call | flops 2147483648 | bytes 8388608 | tf_op jit(solution)/shard_map/pallas_call | solution.py:312
  42.8 8.4 %collective-permute-done.10.block_ref = bf16[128,512]{1,0:T(8,128)(2,1)S(1)} collective-permute-done((bf16[128,512]{1,0:T(8,128)(2,1)S(1)}, bf16[128,512]{1,0:T(8,128)(2,1)S(1)}, u32[]{:S(2)}, u32[]{:S(2)}) %collective-permute-start.10) | collective-permute-done | bytes 131104 | tf_op jit(solution)/shard_map/ppermute | solution.py:255
  51.2 1.5 %shard_map.112.own_ref = f32[1024,1024]{1,0:T(8,128)S(1)} custom-call(f32[1024,1024]{1,0:T(8,128)S(1)} %shard_map.103.after_ref.own_ref, f32[1024,1024]{1,0:T(8,128)S(1)} %shard_map.111.sum_ref, bf16[1024,2304]{1,0:T(8,128)(2,1)S(1)} %shard_map.102.after_ref.count_ref, s32[3,1024]{1,0:T(4,128)S(1)} %copy-done.6, bf16[1024,1024]{1,0:T(8,128)(2,1)S(1)} %copy-done.1, ...), custom_call_target="tpu_custom_call" | custom-call | flops 4294967296 | bytes 8388608 | tf_op jit(solution)/shard_map/pallas_call | solution.py:353
  52.8 1.2 %collective-permute-done.11.block_ref = bf16[128,512]{1,0:T(8,128)(2,1)S(1)} collective-permute-done((bf16[128,512]{1,0:T(8,128)(2,1)S(1)}, bf16[128,512]{1,0:T(8,128)(2,1)S(1)}, u32[]{:S(2)}, u32[]{:S(2)}) %collective-permute-start.11) | collective-permute-done | bytes 131104 | tf_op jit(solution)/shard_map/ppermute | solution.py:255
  54.0 2.4 %shard_map.114 = bf16[1024,1024]{1,0:T(8,128)(2,1)} custom-call(f32[1024,1024]{1,0:T(8,128)S(1)} %shard_map.112.own_ref, f32[1024,1024]{1,0:T(8,128)S(1)} %shard_map.111.sum_ref, bf16[1024,2304]{1,0:T(8,128)(2,1)S(1)} %shard_map.102.after_ref.count_ref, s32[3,1024]{1,0:T(4,128)S(1)} %copy-done.6, bf16[1024,1024]{1,0:T(8,128)(2,1)S(1)} %copy-done.1, ...), custom_call_target="tpu_custom_call" | custom-call | flops 4294967296 | bytes 8388608 | tf_op jit(solution)/shard_map/pallas_call | solution.py:361
  (42 shorter events, 3.9 us)
Async XLA Ops:
  0.0 11.9 %copy-start.6 = (s32[3,1024]{1,0:T(4,128)S(1)}, s32[3,1024]{1,0:T(4,128)}, u32[]{:S(2)}) copy-start(s32[3,1024]{1,0:T(4,128)} %deg_ref.5) | copy-start | bytes 36868
  0.0 11.9 %copy-start.9 = (s32[1024,16]{0,1:T(8,128)S(1)}, s32[1024,16]{0,1:T(8,128)}, u32[]{:S(2)}) copy-start(s32[1024,16]{0,1:T(8,128)} %param.17) | copy-start | bytes 196612
  0.0 11.9 %copy-start.8 = (s32[1024,16]{0,1:T(8,128)S(1)}, s32[1024,16]{0,1:T(8,128)}, u32[]{:S(2)}) copy-start(s32[1024,16]{0,1:T(8,128)} %param.16) | copy-start | bytes 196612
  0.0 11.9 %copy-start.11 = (s32[1024,8]{0,1:T(8,128)S(1)}, s32[1024,8]{0,1:T(8,128)}, u32[]{:S(2)}) copy-start(s32[1024,8]{0,1:T(8,128)} %param.15) | copy-start | bytes 98308
  3.0 18.7 %copy-start = (bf16[1024,1024]{1,0:T(8,128)(2,1)S(1)}, bf16[1024,1024]{1,0:T(8,128)(2,1)}, u32[]{:S(2)}) copy-start(bf16[1024,1024]{1,0:T(8,128)(2,1)} %feat_ref.9) | copy-start | bytes 6291460
  3.0 2.1 %collective-permute-start = (bf16[128,1024]{1,0:T(8,128)(2,1)}, bf16[128,1024]{1,0:T(8,128)(2,1)S(1)}, u32[]{:S(2)}, u32[]{:S(2)}) collective-permute-start(bf16[128,1024]{1,0:T(8,128)(2,1)} %get-tuple-element.14), channel_id=1, source_target_pairs={{0,1},{1,0},{2,3},{3,2},{4,5},{5,4},{6,7},{7,6},{8,9},{9,8},{10,11... | collective-permute-start | bytes 786440 | tf_op jit(solution)/shard_map/ppermute | solution.py:255
  3.7 26.0 %collective-permute-start.3 = (bf16[136,1024]{1,0:T(8,128)(2,1)}, bf16[136,1024]{1,0:T(8,128)(2,1)S(1)}, u32[]{:S(2)}, u32[]{:S(2)}) collective-permute-start(bf16[136,1024]{1,0:T(8,128)(2,1)} %get-tuple-element.18), channel_id=1, source_target_pairs={{0,6},{1,7},{2,4},{3,5},{4,2},{5,3},{6,0},{7,1},{8,14},{9,15},{10,... | collective-permute-start | bytes 835592 | tf_op jit(solution)/shard_map/ppermute | solution.py:255
  9.1 20.7 %collective-permute-start.1 = (bf16[136,1024]{1,0:T(8,128)(2,1)}, bf16[136,1024]{1,0:T(8,128)(2,1)S(1)}, u32[]{:S(2)}, u32[]{:S(2)}) collective-permute-start(bf16[136,1024]{1,0:T(8,128)(2,1)} %get-tuple-element.16), channel_id=1, source_target_pairs={{0,4},{1,5},{2,6},{3,7},{4,0},{5,1},{6,2},{7,3},{8,12},{9,13},{10,... | collective-permute-start | bytes 835592 | tf_op jit(solution)/shard_map/ppermute | solution.py:255
  11.9 17.9 %collective-permute-start.2 = (bf16[136,1024]{1,0:T(8,128)(2,1)}, bf16[136,1024]{1,0:T(8,128)(2,1)S(1)}, u32[]{:S(2)}, u32[]{:S(2)}) collective-permute-start(bf16[136,1024]{1,0:T(8,128)(2,1)} %get-tuple-element.17), channel_id=1, source_target_pairs={{0,2},{1,3},{2,0},{3,1},{4,6},{5,7},{6,4},{7,5},{8,10},{9,11},{10,... | collective-permute-start | bytes 835592 | tf_op jit(solution)/shard_map/ppermute | solution.py:255
  11.9 1.0 %copy-start.4 = (bf16[128,1024]{1,0:T(8,128)(2,1)S(1)}, bf16[128,1024]{1,0:T(8,128)(2,1)}, u32[]{:S(2)}) copy-start(bf16[128,1024]{1,0:T(8,128)(2,1)} %get-tuple-element.15.after_ref.refs_0_) | copy-start | bytes 786436
  12.8 8.9 %copy-start.12 = (bf16[1024,1024]{1,0:T(8,128)(2,1)S(1)}, bf16[1024,1024]{1,0:T(8,128)(2,1)}, u32[]{:S(2)}) copy-start(bf16[1024,1024]{1,0:T(8,128)(2,1)} %w_ref.3) | copy-start | bytes 6291460
  24.1 2.4 %copy-start.10 = (s32[1,8,128]{2,1,0:T(8,128)S(1)}, s32[1,8,128]{2,1,0:T(8,128)}, u32[]{:S(2)}) copy-start(s32[1,8,128]{2,1,0:T(8,128)} %param.19) | copy-start | bytes 12292
  26.4 3.3 %copy-start.7 = (bf16[16,1024]{1,0:T(8,128)(2,1)S(1)}, bf16[16,1024]{1,0:T(8,128)(2,1)}, u32[]{:S(2)}) copy-start(bf16[16,1024]{1,0:T(8,128)(2,1)} %get-tuple-element.13.hub_hbm.refs_0_) | copy-start | bytes 98308
  27.4 14.0 %collective-permute-start.9 = (bf16[128,1024]{1,0:T(8,128)(2,1)S(1)}, bf16[128,1024]{1,0:T(8,128)(2,1)S(1)}, u32[]{:S(2)}, u32[]{:S(2)}) collective-permute-start(bf16[128,1024]{1,0:T(8,128)(2,1)S(1)} %get-tuple-element.20), channel_id=1, source_target_pairs={{0,5},{1,4},{2,7},{3,6},{4,1},{5,0},{6,3},{7,2},{8,13},{9,12},{10,... | collective-permute-start | bytes 786440 | tf_op jit(solution)/shard_map/ppermute | solution.py:255
  29.2 12.9 %collective-permute-start.8 = (bf16[128,1024]{1,0:T(8,128)(2,1)S(1)}, bf16[128,1024]{1,0:T(8,128)(2,1)S(1)}, u32[]{:S(2)}, u32[]{:S(2)}) collective-permute-start(bf16[128,1024]{1,0:T(8,128)(2,1)S(1)} %get-tuple-element.19.refs_4_), channel_id=1, source_target_pairs={{0,3},{1,2},{2,1},{3,0},{4,7},{5,6},{6,5},{7,4},{8,11},{9,10},{10,... | collective-permute-start | bytes 786440 | tf_op jit(solution)/shard_map/ppermute | solution.py:255
  29.8 7.5 %copy-start.3 = (bf16[128,1024]{1,0:T(8,128)(2,1)S(1)}, bf16[128,1024]{1,0:T(8,128)(2,1)}, u32[]{:S(2)}) copy-start(bf16[128,1024]{1,0:T(8,128)(2,1)} %copy-done.2) | copy-start | bytes 786436
  29.8 7.5 %copy-start.5 = (bf16[128,1024]{1,0:T(8,128)(2,1)S(1)}, bf16[128,1024]{1,0:T(8,128)(2,1)}, u32[]{:S(2)}) copy-start(bf16[128,1024]{1,0:T(8,128)(2,1)} %get-tuple-element.15.after_ref.refs_0_) | copy-start | bytes 786436
  29.8 4.5 %collective-permute-start.6 = (bf16[32,1024]{1,0:T(8,128)(2,1)S(1)}, bf16[32,1024]{1,0:T(8,128)(2,1)S(1)}, u32[]{:S(2)}, u32[]{:S(2)}) collective-permute-start(bf16[32,1024]{1,0:T(8,128)(2,1)S(1)} %shard_map.106.after_ref.refs_0_), channel_id=1, source_target_pairs={{0,24},{8,16},{16,8},{24,0},{1,25},{9,17},{17,9},{25,1},{2,26},{10... | collective-permute-start | bytes 196616 | tf_op jit(solution)/shard_map/ppermute | solution.py:255
  31.0 5.4 %collective-permute-start.5 = (bf16[32,1024]{1,0:T(8,128)(2,1)S(1)}, bf16[32,1024]{1,0:T(8,128)(2,1)S(1)}, u32[]{:S(2)}, u32[]{:S(2)}) collective-permute-start(bf16[32,1024]{1,0:T(8,128)(2,1)S(1)} %shard_map.106.after_ref.refs_0_), channel_id=1, source_target_pairs={{0,16},{8,24},{16,0},{24,8},{1,17},{9,25},{17,1},{25,9},{2,18},{10... | collective-permute-start | bytes 196616 | tf_op jit(solution)/shard_map/ppermute | solution.py:255
  32.3 4.1 %collective-permute-start.4 = (bf16[32,1024]{1,0:T(8,128)(2,1)S(1)}, bf16[32,1024]{1,0:T(8,128)(2,1)S(1)}, u32[]{:S(2)}, u32[]{:S(2)}) collective-permute-start(bf16[32,1024]{1,0:T(8,128)(2,1)S(1)} %shard_map.106.after_ref.refs_0_), channel_id=1, source_target_pairs={{0,8},{8,0},{16,24},{24,16},{1,9},{9,1},{17,25},{25,17},{2,10},{10... | collective-permute-start | bytes 196616 | tf_op jit(solution)/shard_map/ppermute | solution.py:255
  34.3 16.9 %collective-permute-start.10 = (bf16[128,512]{1,0:T(8,128)(2,1)S(1)}, bf16[128,512]{1,0:T(8,128)(2,1)S(1)}, u32[]{:S(2)}, u32[]{:S(2)}) collective-permute-start(bf16[128,512]{1,0:T(8,128)(2,1)S(1)} %shard_map.107.refs_4_), channel_id=1, source_target_pairs={{0,7},{1,6},{2,5},{3,4},{4,3},{5,2},{6,1},{7,0},{8,15},{9,14},{10,... | collective-permute-start | bytes 393224 | tf_op jit(solution)/shard_map/ppermute | solution.py:255
  36.4 2.7 %collective-permute-start.7 = (bf16[128,1024]{1,0:T(8,128)(2,1)S(1)}, bf16[128,1024]{1,0:T(8,128)(2,1)S(1)}, u32[]{:S(2)}, u32[]{:S(2)}) collective-permute-start(bf16[128,1024]{1,0:T(8,128)(2,1)S(1)} %shard_map.108.refs_5_.refs_0_), channel_id=1, source_target_pairs={{0,1},{1,0},{2,3},{3,2},{4,5},{5,4},{6,7},{7,6},{8,9},{9,8},{10,11... | collective-permute-start | bytes 786440 | tf_op jit(solution)/shard_map/ppermute | solution.py:255
  40.3 10.9 %copy-start.1 = (bf16[1024,1024]{1,0:T(8,128)(2,1)S(1)}, bf16[1024,1024]{1,0:T(8,128)(2,1)}, u32[]{:S(2)}) copy-start(bf16[1024,1024]{1,0:T(8,128)(2,1)} %w_ref.5) | copy-start | bytes 6291460
  40.3 13.7 %collective-permute-start.11 = (bf16[128,512]{1,0:T(8,128)(2,1)S(1)}, bf16[128,512]{1,0:T(8,128)(2,1)S(1)}, u32[]{:S(2)}, u32[]{:S(2)}) collective-permute-start(bf16[128,512]{1,0:T(8,128)(2,1)S(1)} %shard_map.113), channel_id=1, source_target_pairs={{0,7},{1,6},{2,5},{3,4},{4,3},{5,2},{6,1},{7,0},{8,15},{9,14},{10,... | collective-permute-start | bytes 393224 | tf_op jit(solution)/shard_map/ppermute | solution.py:255
  (1 other events, 0.7 us)

commit v6 on v5

--- a/solution.py
+++ b/solution.py
@@ -248,7 +248,8 @@
     other = list(range(3, last, 2))
     early = [0, 1] + near + far
     order = early + [last] + other
-    spans = [slice(0, width // 2), slice(width // 2, width)]
+    cuts = [0, width // 2, 3 * width // 4, width]
+    spans = [slice(a, b) for a, b in zip(cuts, cuts[1:])]
 
     def swap(block, axis, shift):
         size = peers if axis == "member" else groups
@@ -345,32 +346,35 @@
     total = add(total, [got[s] for s in early], [caps] * len(early), rows_here, hubs, 16)
     total = add(total, [hubs, other_hubs], [hub_slots // 2] * 2, rows_here + caps * peers, total)
     late += rest([last], spans[1], total)
-    late = [swap(block, "member", last) for block in late]
     at = rows_here + caps * order.index(other[0])
     total = add(total, [got[s] for s in other], [caps] * len(other), at, total)
+    late += rest([last], spans[2], total)
+    late = [swap(block, "member", last) for block in late]
 
     at = rows_here + caps * order.index(last)
-    value = call(
-        functools.partial(late_kernel, 512, at, spans[0]),
-        vec((rows_here, width), F32),
-        [VM] * 6,
-        2 * rows_here * spans[0].stop * width,
-        8 * rows_here * width,
-        scratch=[pltpu.VMEM((rows_here, spans[0].stop), BF)],
-    )(own, total, counts, degrees, w_neigh, late[0])
+    value = own
+    for span, block in zip(spans[:-1], late):
+        value = call(
+            functools.partial(late_kernel, 512, at, span),
+            vec((rows_here, width), F32),
+            [VM] * 6,
+            2 * rows_here * (span.stop - span.start) * width,
+            8 * rows_here * width,
+            scratch=[pltpu.VMEM((rows_here, span.stop - span.start), BF)],
+        )(value, total, counts, degrees, w_neigh, block)
     return call(
-        functools.partial(last_kernel, 256, at, spans[1]),
+        functools.partial(last_kernel, 256, at, spans[-1]),
         vec((rows_here, width), BF),
         [VM] * 6,
-        2 * rows_here * (width - spans[1].start) * width,
+        2 * rows_here * (width - spans[-1].start) * width,
         8 * rows_here * width,
         scratch=[
-            pltpu.VMEM((rows_here, width - spans[1].start), BF),
+            pltpu.VMEM((rows_here, width - spans[-1].start), BF),
             pltpu.VMEM((rows_here, width), BF),
             pltpu.SemaphoreType.DMA((rows_here // 256,)),
         ],
         out_specs=ANY,
-    )(value, total, counts, degrees, w_neigh, late[1])
+    )(value, total, counts, degrees, w_neigh, late[-1])
 
 
 def solution(mesh):

time: 56.8 us -> 56.6 us (level)
  waiting for transfers between devices: 12.2 us -> 9.51 us
  starting transfers between devices: 12.8 us -> 14.1 us
  Pallas kernels: 28.7 us -> 29.9 us
    ppermute x12 -> x13, waiting for transfers between devices: 12.2 us -> 9.51 us  [swap(): return lax.ppermute(block, axis, [(i, i ^ shift) for i in range(size)])]
    ppermute x12 -> x13, starting transfers between devices: 12.8 us -> 14.1 us  [swap(): return lax.ppermute(block, axis, [(i, i ^ shift) for i in range(size)])]
    pallas_call x2 -> x3, Pallas kernels: 3.95 us -> 4.86 us  [the longest x2 2.69 us: per_device(): call(functools.partial(late_kernel, 512, at, span), vec((rows_here, width...]
    pallas_call x3 -> x4, Pallas kernels: 1.8 us -> 2.07 us  [rest(): call(functools.partial(rest_kernel, shifts, cols), [vec((caps, cols.stop...]
  transfers between devices with their start and end apart: 12 -> 13, of which waited for: 5 -> 5; matrix products, arithmetic and copies ran while one was open for 1% -> 1% of each run, Pallas kernels for 41% -> 44%
where the time goes in v6:
time: 56.6 us; the launch traced here: 56.3 us
  Pallas kernels  29.9 us (53%)
  starting transfers between devices  14.1 us (25%)
  waiting for transfers between devices  9.51 us (17%)
  local copies, waits for them, and re-layouts  2.4 us (4%)
    ppermute x13, starting transfers between devices, swap(): return lax.ppermute(block, axis, [(i, i ^ shift) for i in range(size)])  14.1 us
    ppermute x13, waiting for transfers between devices, swap(): return lax.ppermute(block, axis, [(i, i ^ shift) for i in range(size)])  9.51 us
    pallas_call x1, Pallas kernels, per_device(): call(functools.partial(table_kernel, 2 * LANES, peers, caps, hub_dev, mag...  8.86 us
    pallas_call x1, Pallas kernels, per_device(): call(functools.partial(near_kernel, near + [0]), [plain if shift % 2 else...  3.27 us
    pallas_call x3, Pallas kernels, add(): call(functools.partial(sum_kernel, 512, sizes, at), vec((rows_here, width...  3.22 us
    pallas_call x1, Pallas kernels, per_device(): call(functools.partial(first_kernel, far + [1]), [carrier] * len(far) + [...  2.96 us
    pallas_call x2, Pallas kernels, per_device(): call(functools.partial(late_kernel, 512, at, span), vec((rows_here, width...  2.69 us
    pallas_call x1, Pallas kernels, per_device(): call(functools.partial(own_kernel, 512), vec((rows_here, width), F32), [V...  2.34 us
  transfers between devices with their start and end apart: 13, of which 5 were waited for; matrix products, arithmetic and copies ran while one was open for 1% of the time, Pallas kernels for 44%

profile of v6, /device:TPU:21, one launch (start us, length us, event | category | flops | bytes accessed | tf_op | source)
XLA Modules:
  0.0 56.3 jit_solution(6956562616791859797)
XLA Ops:
  0.0 3.0 %shard_map.100 = (bf16[136,1024]{1,0:T(8,128)(2,1)}, bf16[128,1024]{1,0:T(8,128)(2,1)}, bf16[16,1024]{1,0:T(8,128)(2,1)}) custom-call(s32[8,128]{1,0:T(8,128)} %bitcast.6, s32[6]{0:T(128)} %hub_hbm.1, bf16[1024,1024]{1,0:T(8,128)(2,1)} %feat_ref.11), custom_call_target="tpu_custom_call" | custom-call | bytes 2097152 | tf_op jit(solution)/shard_map/pallas_call | solution.py:260
  3.0 0.7 %collective-permute-start = (bf16[128,1024]{1,0:T(8,128)(2,1)}, bf16[128,1024]{1,0:T(8,128)(2,1)S(1)}, u32[]{:S(2)}, u32[]{:S(2)}) collective-permute-start(bf16[128,1024]{1,0:T(8,128)(2,1)} %get-tuple-element.14), channel_id=1, source_target_pairs={{0,1},{1,0},{2,3},{3,2},{4,5},{5,4},{6,7},{7,6},{8,9},{9,8},{10,11... | collective-permute-start | bytes 786440 | tf_op jit(solution)/shard_map/ppermute | solution.py:256
  5.1 0.7 %copy-done.2 = bf16[128,1024]{1,0:T(8,128)(2,1)} copy-done((bf16[128,1024]{1,0:T(8,128)(2,1)}, bf16[128,1024]{1,0:T(8,128)(2,1)S(1)}, u32[]{:S(2)}) %copy-start.2) | copy-done | bytes 262168
  5.8 3.3 %shard_map.101 = (bf16[136,1024]{1,0:T(8,128)(2,1)}, bf16[136,1024]{1,0:T(8,128)(2,1)}, bf16[128,1024]{1,0:T(8,128)(2,1)}) custom-call(s32[8,128]{1,0:T(8,128)} %bitcast.7, bf16[16,1024]{1,0:T(8,128)(2,1)} %get-tuple-element.13.hub_hbm.refs_0_, bf16[1024,1024]{1,0:T(8,128)(2,1)} %feat_ref.11, bf16[128,1024]{1,0:T(8,128)(2,1)} %copy-done.2), custom_call_target="tpu_custom_call" | custom-call | bytes 2097152 | tf_op jit(solution)/shard_map/pallas_call | solution.py:271
  9.1 2.8 %collective-permute-start.1 = (bf16[136,1024]{1,0:T(8,128)(2,1)}, bf16[136,1024]{1,0:T(8,128)(2,1)S(1)}, u32[]{:S(2)}, u32[]{:S(2)}) collective-permute-start(bf16[136,1024]{1,0:T(8,128)(2,1)} %get-tuple-element.16), channel_id=1, source_target_pairs={{0,4},{1,5},{2,6},{3,7},{4,0},{5,1},{6,2},{7,3},{8,12},{9,13},{10,... | collective-permute-start | bytes 835592 | tf_op jit(solution)/shard_map/ppermute | solution.py:256
  11.9 0.9 %copy-done.4 = bf16[128,1024]{1,0:T(8,128)(2,1)S(1)} copy-done((bf16[128,1024]{1,0:T(8,128)(2,1)S(1)}, bf16[128,1024]{1,0:T(8,128)(2,1)}, u32[]{:S(2)}) %copy-start.4) | copy-done | bytes 262168
  12.9 8.9 %shard_map.102.after_ref.count_ref = bf16[1024,2304]{1,0:T(8,128)(2,1)S(1)} custom-call(s32[16,1024]{1,0:T(8,128)S(1)} %bitcast.4, s32[8,1024]{1,0:T(8,128)S(1)} %bitcast.12, s32[16,1024]{1,0:T(8,128)S(1)} %bitcast.5, s32[3,1024]{1,0:T(4,128)S(1)} %copy-done.6, bf16[128,1024]{1,0:T(8,128)(2,1)S(1)} %copy-done.4), custom_call_target="tpu_custom_call" | custom-call | flops 201326592 | bytes 4718592 | tf_op jit(solution)/shard_map/pallas_call | solution.py:284
  21.8 2.3 %shard_map.103.after_ref.own_ref = f32[1024,1024]{1,0:T(8,128)S(1)} custom-call(bf16[1024,1024]{1,0:T(8,128)(2,1)S(1)} %copy-done, bf16[1024,1024]{1,0:T(8,128)(2,1)S(1)} %copy-done.12, bf16[1,1024]{1,0:T(2,128)(2,1)S(1)} %reshape.6.bias_ref, bf16[1024,2304]{1,0:T(8,128)(2,1)S(1)} %shard_map.102.after_ref.count_ref), custom_call_target="tpu_custom_call" | custom-call | flops 8589934592 | bytes 8388608 | tf_op jit(solution)/shard_map/pallas_call | solution.py:322
  24.1 2.3 %shard_map.104.after_ref.sum_ref = f32[1024,1024]{1,0:T(8,128)S(1)} custom-call(bf16[1024,1024]{1,0:T(8,128)(2,1)S(1)} %copy-done, bf16[1024,2304]{1,0:T(8,128)(2,1)S(1)} %shard_map.102.after_ref.count_ref, f32[1024,1024]{1,0:T(8,128)S(1)} %shard_map.103.after_ref.own_ref), custom_call_target="tpu_custom_call" | custom-call | flops 8589934592 | bytes 8388608 | tf_op jit(solution)/shard_map/pallas_call | solution.py:329
  26.5 0.9 %shard_map.105 = (bf16[128,1024]{1,0:T(8,128)(2,1)S(1)}, bf16[128,1024]{1,0:T(8,128)(2,1)S(1)}) custom-call(s32[8,128]{1,0:T(8,128)S(1)} %bitcast.8, bf16[1024,1024]{1,0:T(8,128)(2,1)S(1)} %copy-done, f32[1024,1024]{1,0:T(8,128)S(1)} %shard_map.104.after_ref.sum_ref), custom_call_target="tpu_custom_call" | custom-call | flops 2147483648 | bytes 2097152 | tf_op jit(solution)/shard_map/pallas_call | solution.py:293
  27.4 1.8 %collective-permute-start.9 = (bf16[128,1024]{1,0:T(8,128)(2,1)S(1)}, bf16[128,1024]{1,0:T(8,128)(2,1)S(1)}, u32[]{:S(2)}, u32[]{:S(2)}) collective-permute-start(bf16[128,1024]{1,0:T(8,128)(2,1)S(1)} %get-tuple-element.20), channel_id=1, source_target_pairs={{0,5},{1,4},{2,7},{3,6},{4,1},{5,0},{6,3},{7,2},{8,13},{9,12},{10,... | collective-permute-start | bytes 786440 | tf_op jit(solution)/shard_map/ppermute | solution.py:256
  29.8 1.2 %collective-permute-start.6 = (bf16[32,1024]{1,0:T(8,128)(2,1)S(1)}, bf16[32,1024]{1,0:T(8,128)(2,1)S(1)}, u32[]{:S(2)}, u32[]{:S(2)}) collective-permute-start(bf16[32,1024]{1,0:T(8,128)(2,1)S(1)} %shard_map.106.after_ref.refs_0_), channel_id=1, source_target_pairs={{0,24},{8,16},{16,8},{24,0},{1,25},{9,17},{17,9},{25,1},{2,26},{10... | collective-permute-start | bytes 196616 | tf_op jit(solution)/shard_map/ppermute | solution.py:256
  31.0 1.2 %collective-permute-start.5 = (bf16[32,1024]{1,0:T(8,128)(2,1)S(1)}, bf16[32,1024]{1,0:T(8,128)(2,1)S(1)}, u32[]{:S(2)}, u32[]{:S(2)}) collective-permute-start(bf16[32,1024]{1,0:T(8,128)(2,1)S(1)} %shard_map.106.after_ref.refs_0_), channel_id=1, source_target_pairs={{0,16},{8,24},{16,0},{24,8},{1,17},{9,25},{17,1},{25,9},{2,18},{10... | collective-permute-start | bytes 196616 | tf_op jit(solution)/shard_map/ppermute | solution.py:256
  33.0 1.4 %collective-permute-done.6.refs_3_ = bf16[32,1024]{1,0:T(8,128)(2,1)S(1)} collective-permute-done((bf16[32,1024]{1,0:T(8,128)(2,1)S(1)}, bf16[32,1024]{1,0:T(8,128)(2,1)S(1)}, u32[]{:S(2)}, u32[]{:S(2)}) %collective-permute-start.6) | collective-permute-done | bytes 65568 | tf_op jit(solution)/shard_map/ppermute | solution.py:256
  34.3 2.1 %collective-permute-start.10 = (bf16[128,512]{1,0:T(8,128)(2,1)S(1)}, bf16[128,512]{1,0:T(8,128)(2,1)S(1)}, u32[]{:S(2)}, u32[]{:S(2)}) collective-permute-start(bf16[128,512]{1,0:T(8,128)(2,1)S(1)} %shard_map.107.refs_4_), channel_id=1, source_target_pairs={{0,7},{1,6},{2,5},{3,4},{4,3},{5,2},{6,1},{7,0},{8,15},{9,14},{10,... | collective-permute-start | bytes 393224 | tf_op jit(solution)/shard_map/ppermute | solution.py:256
  36.4 0.9 %collective-permute-start.7 = (bf16[128,1024]{1,0:T(8,128)(2,1)S(1)}, bf16[128,1024]{1,0:T(8,128)(2,1)S(1)}, u32[]{:S(2)}, u32[]{:S(2)}) collective-permute-start(bf16[128,1024]{1,0:T(8,128)(2,1)S(1)} %shard_map.108.refs_5_.refs_0_), channel_id=1, source_target_pairs={{0,1},{1,0},{2,3},{3,2},{4,5},{5,4},{6,7},{7,6},{8,9},{9,8},{10,11... | collective-permute-start | bytes 786440 | tf_op jit(solution)/shard_map/ppermute | solution.py:256
  37.3 1.8 %shard_map.109.sum_ref.refs_2_ = f32[1024,1024]{1,0:T(8,128)S(1)} custom-call(f32[1024,1024]{1,0:T(8,128)S(1)} %shard_map.104.after_ref.sum_ref, bf16[1024,2304]{1,0:T(8,128)(2,1)S(1)} %shard_map.102.after_ref.count_ref, bf16[128,1024]{1,0:T(8,128)(2,1)S(1)} %copy-done.5, bf16[128,1024]{1,0:T(8,128)(2,1)S(1)} %copy-done.3, ...), custom_call_target="tpu_custom_call" | custom-call | flops 85899345920 | bytes 8388608 | tf_op jit(solution)/shard_map/pallas_call | solution.py:313
  40.2 1.1 %collective-permute-start.11 = (bf16[128,256]{1,0:T(8,128)(2,1)S(1)}, bf16[128,256]{1,0:T(8,128)(2,1)S(1)}, u32[]{:S(2)}, u32[]{:S(2)}) collective-permute-start(bf16[128,256]{1,0:T(8,128)(2,1)S(1)} %shard_map.113), channel_id=1, source_target_pairs={{0,7},{1,6},{2,5},{3,4},{4,3},{5,2},{6,1},{7,0},{8,15},{9,14},{10,... | collective-permute-start | bytes 196616 | tf_op jit(solution)/shard_map/ppermute | solution.py:256
  41.3 0.8 %collective-permute-done.8.refs_0_ = bf16[128,1024]{1,0:T(8,128)(2,1)S(1)} collective-permute-done((bf16[128,1024]{1,0:T(8,128)(2,1)S(1)}, bf16[128,1024]{1,0:T(8,128)(2,1)S(1)}, u32[]{:S(2)}, u32[]{:S(2)}) %collective-permute-start.8) | collective-permute-done | bytes 262176 | tf_op jit(solution)/shard_map/ppermute | solution.py:256
  43.2 1.2 %collective-permute-start.12 = (bf16[128,256]{1,0:T(8,128)(2,1)S(1)}, bf16[128,256]{1,0:T(8,128)(2,1)S(1)}, u32[]{:S(2)}, u32[]{:S(2)}) collective-permute-start(bf16[128,256]{1,0:T(8,128)(2,1)S(1)} %shard_map.115), channel_id=1, source_target_pairs={{0,7},{1,6},{2,5},{3,4},{4,3},{5,2},{6,1},{7,0},{8,15},{9,14},{10,... | collective-permute-start | bytes 196616 | tf_op jit(solution)/shard_map/ppermute | solution.py:256
  44.5 6.7 %collective-permute-done.10.block_ref = bf16[128,512]{1,0:T(8,128)(2,1)S(1)} collective-permute-done((bf16[128,512]{1,0:T(8,128)(2,1)S(1)}, bf16[128,512]{1,0:T(8,128)(2,1)S(1)}, u32[]{:S(2)}, u32[]{:S(2)}) %collective-permute-start.10) | collective-permute-done | bytes 131104 | tf_op jit(solution)/shard_map/ppermute | solution.py:256
  51.2 1.5 %shard_map.112.own_ref = f32[1024,1024]{1,0:T(8,128)S(1)} custom-call(f32[1024,1024]{1,0:T(8,128)S(1)} %shard_map.103.after_ref.own_ref, f32[1024,1024]{1,0:T(8,128)S(1)} %shard_map.111.sum_ref.after_ref, bf16[1024,2304]{1,0:T(8,128)(2,1)S(1)} %shard_map.102.after_ref.count_ref, s32[3,1024]{1,0:T(4,128)S(1)} %copy-done.6, bf16[1024,1024]{1,0:T(8,128)(2,1)S(1)} %copy-done.1, ...), custom_call_target="tpu_custom_call" | custom-call | flops 4294967296 | bytes 8388608 | tf_op jit(solution)/shard_map/pallas_call | solution.py:357
  52.8 1.1 %shard_map.114.own_ref = f32[1024,1024]{1,0:T(8,128)S(1)} custom-call(f32[1024,1024]{1,0:T(8,128)S(1)} %shard_map.112.own_ref, f32[1024,1024]{1,0:T(8,128)S(1)} %shard_map.111.sum_ref.after_ref, bf16[1024,2304]{1,0:T(8,128)(2,1)S(1)} %shard_map.102.after_ref.count_ref, s32[3,1024]{1,0:T(4,128)S(1)} %copy-done.6, bf16[1024,1024]{1,0:T(8,128)(2,1)S(1)} %copy-done.1, ...), custom_call_target="tpu_custom_call" | custom-call | flops 2147483648 | bytes 8388608 | tf_op jit(solution)/shard_map/pallas_call | solution.py:357
  54.0 2.2 %shard_map.116 = bf16[1024,1024]{1,0:T(8,128)(2,1)} custom-call(f32[1024,1024]{1,0:T(8,128)S(1)} %shard_map.114.own_ref, f32[1024,1024]{1,0:T(8,128)S(1)} %shard_map.111.sum_ref.after_ref, bf16[1024,2304]{1,0:T(8,128)(2,1)S(1)} %shard_map.102.after_ref.count_ref, s32[3,1024]{1,0:T(4,128)S(1)} %copy-done.6, bf16[1024,1024]{1,0:T(8,128)(2,1)S(1)} %copy-done.1, ...), custom_call_target="tpu_custom_call" | custom-call | flops 2147483648 | bytes 8388608 | tf_op jit(solution)/shard_map/pallas_call | solution.py:365
  (46 shorter events, 4.9 us)
Async XLA Ops:
  0.0 11.9 %copy-start.6 = (s32[3,1024]{1,0:T(4,128)S(1)}, s32[3,1024]{1,0:T(4,128)}, u32[]{:S(2)}) copy-start(s32[3,1024]{1,0:T(4,128)} %deg_ref.7) | copy-start | bytes 36868
  0.0 11.9 %copy-start.9 = (s32[1024,16]{0,1:T(8,128)S(1)}, s32[1024,16]{0,1:T(8,128)}, u32[]{:S(2)}) copy-start(s32[1024,16]{0,1:T(8,128)} %param.17) | copy-start | bytes 196612
  0.0 11.9 %copy-start.8 = (s32[1024,16]{0,1:T(8,128)S(1)}, s32[1024,16]{0,1:T(8,128)}, u32[]{:S(2)}) copy-start(s32[1024,16]{0,1:T(8,128)} %param.16) | copy-start | bytes 196612
  0.0 11.9 %copy-start.11 = (s32[1024,8]{0,1:T(8,128)S(1)}, s32[1024,8]{0,1:T(8,128)}, u32[]{:S(2)}) copy-start(s32[1024,8]{0,1:T(8,128)} %param.15) | copy-start | bytes 98308
  3.0 18.8 %copy-start = (bf16[1024,1024]{1,0:T(8,128)(2,1)S(1)}, bf16[1024,1024]{1,0:T(8,128)(2,1)}, u32[]{:S(2)}) copy-start(bf16[1024,1024]{1,0:T(8,128)(2,1)} %feat_ref.11) | copy-start | bytes 6291460
  3.0 2.1 %collective-permute-start = (bf16[128,1024]{1,0:T(8,128)(2,1)}, bf16[128,1024]{1,0:T(8,128)(2,1)S(1)}, u32[]{:S(2)}, u32[]{:S(2)}) collective-permute-start(bf16[128,1024]{1,0:T(8,128)(2,1)} %get-tuple-element.14), channel_id=1, source_target_pairs={{0,1},{1,0},{2,3},{3,2},{4,5},{5,4},{6,7},{7,6},{8,9},{9,8},{10,11... | collective-permute-start | bytes 786440 | tf_op jit(solution)/shard_map/ppermute | solution.py:256
  3.7 26.0 %collective-permute-start.3 = (bf16[136,1024]{1,0:T(8,128)(2,1)}, bf16[136,1024]{1,0:T(8,128)(2,1)S(1)}, u32[]{:S(2)}, u32[]{:S(2)}) collective-permute-start(bf16[136,1024]{1,0:T(8,128)(2,1)} %get-tuple-element.18), channel_id=1, source_target_pairs={{0,6},{1,7},{2,4},{3,5},{4,2},{5,3},{6,0},{7,1},{8,14},{9,15},{10,... | collective-permute-start | bytes 835592 | tf_op jit(solution)/shard_map/ppermute | solution.py:256
  9.1 20.7 %collective-permute-start.1 = (bf16[136,1024]{1,0:T(8,128)(2,1)}, bf16[136,1024]{1,0:T(8,128)(2,1)S(1)}, u32[]{:S(2)}, u32[]{:S(2)}) collective-permute-start(bf16[136,1024]{1,0:T(8,128)(2,1)} %get-tuple-element.16), channel_id=1, source_target_pairs={{0,4},{1,5},{2,6},{3,7},{4,0},{5,1},{6,2},{7,3},{8,12},{9,13},{10,... | collective-permute-start | bytes 835592 | tf_op jit(solution)/shard_map/ppermute | solution.py:256
  11.9 17.9 %collective-permute-start.2 = (bf16[136,1024]{1,0:T(8,128)(2,1)}, bf16[136,1024]{1,0:T(8,128)(2,1)S(1)}, u32[]{:S(2)}, u32[]{:S(2)}) collective-permute-start(bf16[136,1024]{1,0:T(8,128)(2,1)} %get-tuple-element.17), channel_id=1, source_target_pairs={{0,2},{1,3},{2,0},{3,1},{4,6},{5,7},{6,4},{7,5},{8,10},{9,11},{10,... | collective-permute-start | bytes 835592 | tf_op jit(solution)/shard_map/ppermute | solution.py:256
  12.9 8.9 %copy-start.12 = (bf16[1024,1024]{1,0:T(8,128)(2,1)S(1)}, bf16[1024,1024]{1,0:T(8,128)(2,1)}, u32[]{:S(2)}) copy-start(bf16[1024,1024]{1,0:T(8,128)(2,1)} %w_ref.4) | copy-start | bytes 6291460
  24.1 2.4 %copy-start.10 = (s32[1,8,128]{2,1,0:T(8,128)S(1)}, s32[1,8,128]{2,1,0:T(8,128)}, u32[]{:S(2)}) copy-start(s32[1,8,128]{2,1,0:T(8,128)} %param.19) | copy-start | bytes 12292
  26.5 3.3 %copy-start.7 = (bf16[16,1024]{1,0:T(8,128)(2,1)S(1)}, bf16[16,1024]{1,0:T(8,128)(2,1)}, u32[]{:S(2)}) copy-start(bf16[16,1024]{1,0:T(8,128)(2,1)} %get-tuple-element.13.hub_hbm.refs_0_) | copy-start | bytes 98308
  27.4 13.9 %collective-permute-start.9 = (bf16[128,1024]{1,0:T(8,128)(2,1)S(1)}, bf16[128,1024]{1,0:T(8,128)(2,1)S(1)}, u32[]{:S(2)}, u32[]{:S(2)}) collective-permute-start(bf16[128,1024]{1,0:T(8,128)(2,1)S(1)} %get-tuple-element.20), channel_id=1, source_target_pairs={{0,5},{1,4},{2,7},{3,6},{4,1},{5,0},{6,3},{7,2},{8,13},{9,12},{10,... | collective-permute-start | bytes 786440 | tf_op jit(solution)/shard_map/ppermute | solution.py:256
  29.2 12.9 %collective-permute-start.8 = (bf16[128,1024]{1,0:T(8,128)(2,1)S(1)}, bf16[128,1024]{1,0:T(8,128)(2,1)S(1)}, u32[]{:S(2)}, u32[]{:S(2)}) collective-permute-start(bf16[128,1024]{1,0:T(8,128)(2,1)S(1)} %get-tuple-element.19.refs_4_), channel_id=1, source_target_pairs={{0,3},{1,2},{2,1},{3,0},{4,7},{5,6},{6,5},{7,4},{8,11},{9,10},{10,... | collective-permute-start | bytes 786440 | tf_op jit(solution)/shard_map/ppermute | solution.py:256
  29.8 7.5 %copy-start.3 = (bf16[128,1024]{1,0:T(8,128)(2,1)S(1)}, bf16[128,1024]{1,0:T(8,128)(2,1)}, u32[]{:S(2)}) copy-start(bf16[128,1024]{1,0:T(8,128)(2,1)} %copy-done.2) | copy-start | bytes 786436
  29.8 7.5 %copy-start.5 = (bf16[128,1024]{1,0:T(8,128)(2,1)S(1)}, bf16[128,1024]{1,0:T(8,128)(2,1)}, u32[]{:S(2)}) copy-start(bf16[128,1024]{1,0:T(8,128)(2,1)} %get-tuple-element.15.after_ref.refs_0_) | copy-start | bytes 786436
  29.8 4.5 %collective-permute-start.6 = (bf16[32,1024]{1,0:T(8,128)(2,1)S(1)}, bf16[32,1024]{1,0:T(8,128)(2,1)S(1)}, u32[]{:S(2)}, u32[]{:S(2)}) collective-permute-start(bf16[32,1024]{1,0:T(8,128)(2,1)S(1)} %shard_map.106.after_ref.refs_0_), channel_id=1, source_target_pairs={{0,24},{8,16},{16,8},{24,0},{1,25},{9,17},{17,9},{25,1},{2,26},{10... | collective-permute-start | bytes 196616 | tf_op jit(solution)/shard_map/ppermute | solution.py:256
  31.0 5.4 %collective-permute-start.5 = (bf16[32,1024]{1,0:T(8,128)(2,1)S(1)}, bf16[32,1024]{1,0:T(8,128)(2,1)S(1)}, u32[]{:S(2)}, u32[]{:S(2)}) collective-permute-start(bf16[32,1024]{1,0:T(8,128)(2,1)S(1)} %shard_map.106.after_ref.refs_0_), channel_id=1, source_target_pairs={{0,16},{8,24},{16,0},{24,8},{1,17},{9,25},{17,1},{25,9},{2,18},{10... | collective-permute-start | bytes 196616 | tf_op jit(solution)/shard_map/ppermute | solution.py:256
  32.3 4.1 %collective-permute-start.4 = (bf16[32,1024]{1,0:T(8,128)(2,1)S(1)}, bf16[32,1024]{1,0:T(8,128)(2,1)S(1)}, u32[]{:S(2)}, u32[]{:S(2)}) collective-permute-start(bf16[32,1024]{1,0:T(8,128)(2,1)S(1)} %shard_map.106.after_ref.refs_0_), channel_id=1, source_target_pairs={{0,8},{8,0},{16,24},{24,16},{1,9},{9,1},{17,25},{25,17},{2,10},{10... | collective-permute-start | bytes 196616 | tf_op jit(solution)/shard_map/ppermute | solution.py:256
  34.3 16.9 %collective-permute-start.10 = (bf16[128,512]{1,0:T(8,128)(2,1)S(1)}, bf16[128,512]{1,0:T(8,128)(2,1)S(1)}, u32[]{:S(2)}, u32[]{:S(2)}) collective-permute-start(bf16[128,512]{1,0:T(8,128)(2,1)S(1)} %shard_map.107.refs_4_), channel_id=1, source_target_pairs={{0,7},{1,6},{2,5},{3,4},{4,3},{5,2},{6,1},{7,0},{8,15},{9,14},{10,... | collective-permute-start | bytes 393224 | tf_op jit(solution)/shard_map/ppermute | solution.py:256
  36.4 2.7 %collective-permute-start.7 = (bf16[128,1024]{1,0:T(8,128)(2,1)S(1)}, bf16[128,1024]{1,0:T(8,128)(2,1)S(1)}, u32[]{:S(2)}, u32[]{:S(2)}) collective-permute-start(bf16[128,1024]{1,0:T(8,128)(2,1)S(1)} %shard_map.108.refs_5_.refs_0_), channel_id=1, source_target_pairs={{0,1},{1,0},{2,3},{3,2},{4,5},{5,4},{6,7},{7,6},{8,9},{9,8},{10,11... | collective-permute-start | bytes 786440 | tf_op jit(solution)/shard_map/ppermute | solution.py:256
  40.2 12.5 %collective-permute-start.11 = (bf16[128,256]{1,0:T(8,128)(2,1)S(1)}, bf16[128,256]{1,0:T(8,128)(2,1)S(1)}, u32[]{:S(2)}, u32[]{:S(2)}) collective-permute-start(bf16[128,256]{1,0:T(8,128)(2,1)S(1)} %shard_map.113), channel_id=1, source_target_pairs={{0,7},{1,6},{2,5},{3,4},{4,3},{5,2},{6,1},{7,0},{8,15},{9,14},{10,... | collective-permute-start | bytes 196616 | tf_op jit(solution)/shard_map/ppermute | solution.py:256
  42.8 8.4 %copy-start.1 = (bf16[1024,1024]{1,0:T(8,128)(2,1)S(1)}, bf16[1024,1024]{1,0:T(8,128)(2,1)}, u32[]{:S(2)}) copy-start(bf16[1024,1024]{1,0:T(8,128)(2,1)} %w_ref.7) | copy-start | bytes 6291460
  43.2 10.8 %collective-permute-start.12 = (bf16[128,256]{1,0:T(8,128)(2,1)S(1)}, bf16[128,256]{1,0:T(8,128)(2,1)S(1)}, u32[]{:S(2)}, u32[]{:S(2)}) collective-permute-start(bf16[128,256]{1,0:T(8,128)(2,1)S(1)} %shard_map.115), channel_id=1, source_target_pairs={{0,7},{1,6},{2,5},{3,4},{4,3},{5,2},{6,1},{7,0},{8,15},{9,14},{10,... | collective-permute-start | bytes 196616 | tf_op jit(solution)/shard_map/ppermute | solution.py:256
  (2 other events, 1.7 us)

commit v7 on v6

--- a/solution.py
+++ b/solution.py
@@ -174,7 +174,7 @@
 
 
 def own_kernel(rb, feat_ref, w_ref, bias_ref, after_ref, out_ref):
-    bias = bias_ref[...].astype(F32)
+    bias = bias_ref[...].astype(F32)[None, :]
     for i in range(feat_ref.shape[0] // rb):
         span = pl.ds(i * rb, rb)
         out_ref[span, :] = jnp.dot(feat_ref[span, :], w_ref[...], preferred_element_type=F32) + bias
@@ -325,7 +325,7 @@
         [VM] * 3 + [ANY],
         2 * rows_here * width * width,
         8 * rows_here * width,
-    )(features, w_self, bias.reshape(1, width), counts)
+    )(features, w_self, bias, counts)
     total = call(
         functools.partial(local_kernel, 512),
         vec((rows_here, width), F32),

time: 56.6 us -> 56.3 us (level)
  waiting for transfers between devices: 9.51 us -> 10.4 us
  starting transfers between devices: 14.1 us -> 13.3 us
  local copies, waits for them, and re-layouts: 2.4 us -> 1.72 us
    ppermute x13, waiting for transfers between devices: 9.51 us -> 10.4 us  [swap(): return lax.ppermute(block, axis, [(i, i ^ shift) for i in range(size)])]
    ppermute x13, starting transfers between devices: 14.1 us -> 13.3 us  [swap(): return lax.ppermute(block, axis, [(i, i ^ shift) for i in range(size)])]
    reshape x1 -> x0, local copies, waits for them, and re-layouts: 0.69 us -> none  [per_device(): bias.reshape(1, width)]
    unnamed x26 -> x28, local copies, waits for them, and re-layouts: 1.71 us -> 1.72 us
  transfers between devices with their start and end apart: 13 -> 13, of which waited for: 5 -> 6; matrix products, arithmetic and copies ran while one was open for 1% -> 0% of each run, Pallas kernels for 44% -> 44%
where the time goes in v7:
time: 56.3 us; the launch traced here: 55.6 us
  Pallas kernels  29.8 us (53%)
  starting transfers between devices  13.3 us (24%)
  waiting for transfers between devices  10.4 us (18%)
  local copies, waits for them, and re-layouts  1.72 us (3%)
    ppermute x13, starting transfers between devices, swap(): return lax.ppermute(block, axis, [(i, i ^ shift) for i in range(size)])  13.3 us
    ppermute x13, waiting for transfers between devices, swap(): return lax.ppermute(block, axis, [(i, i ^ shift) for i in range(size)])  10.4 us
    pallas_call x1, Pallas kernels, per_device(): call(functools.partial(table_kernel, 2 * LANES, peers, caps, hub_dev, mag...  8.86 us
    pallas_call x1, Pallas kernels, per_device(): call(functools.partial(near_kernel, near + [0]), [plain if shift % 2 else...  3.23 us
    pallas_call x3, Pallas kernels, add(): call(functools.partial(sum_kernel, 512, sizes, at), vec((rows_here, width...  3.21 us
    pallas_call x1, Pallas kernels, per_device(): call(functools.partial(first_kernel, far + [1]), [carrier] * len(far) + [...  2.96 us
    pallas_call x2, Pallas kernels, per_device(): call(functools.partial(late_kernel, 512, at, span), vec((rows_here, width...  2.69 us
    pallas_call x1, Pallas kernels, per_device(): call(functools.partial(own_kernel, 512), vec((rows_here, width), F32), [V...  2.34 us
  transfers between devices with their start and end apart: 13, of which 6 were waited for; matrix products, arithmetic and copies ran while one was open for 0% of the time, Pallas kernels for 44%

profile of v7, /device:TPU:21, one launch (start us, length us, event | category | flops | bytes accessed | tf_op | source)
XLA Modules:
  0.0 55.6 jit_solution(11572648549049789612)
XLA Ops:
  0.0 3.0 %shard_map.100 = (bf16[136,1024]{1,0:T(8,128)(2,1)}, bf16[128,1024]{1,0:T(8,128)(2,1)}, bf16[16,1024]{1,0:T(8,128)(2,1)}) custom-call(s32[8,128]{1,0:T(8,128)} %bitcast.6, s32[6]{0:T(128)} %hub_hbm.1, bf16[1024,1024]{1,0:T(8,128)(2,1)} %feat_ref.11), custom_call_target="tpu_custom_call" | custom-call | bytes 2097152 | tf_op jit(solution)/shard_map/pallas_call | solution.py:260
  3.0 0.7 %collective-permute-start = (bf16[128,1024]{1,0:T(8,128)(2,1)}, bf16[128,1024]{1,0:T(8,128)(2,1)S(1)}, u32[]{:S(2)}, u32[]{:S(2)}) collective-permute-start(bf16[128,1024]{1,0:T(8,128)(2,1)} %get-tuple-element.14), channel_id=1, source_target_pairs={{0,1},{1,0},{2,3},{3,2},{4,5},{5,4},{6,7},{7,6},{8,9},{9,8},{10,11... | collective-permute-start | bytes 786440 | tf_op jit(solution)/shard_map/ppermute | solution.py:256
  3.9 1.2 %collective-permute-done.after_ref.refs_1_ = bf16[128,1024]{1,0:T(8,128)(2,1)S(1)} collective-permute-done((bf16[128,1024]{1,0:T(8,128)(2,1)}, bf16[128,1024]{1,0:T(8,128)(2,1)S(1)}, u32[]{:S(2)}, u32[]{:S(2)}) %collective-permute-start) | collective-permute-done | bytes 262176 | tf_op jit(solution)/shard_map/ppermute | solution.py:256
  5.1 0.7 %copy-done.2 = bf16[128,1024]{1,0:T(8,128)(2,1)} copy-done((bf16[128,1024]{1,0:T(8,128)(2,1)}, bf16[128,1024]{1,0:T(8,128)(2,1)S(1)}, u32[]{:S(2)}) %copy-start.2) | copy-done | bytes 262168
  5.8 3.2 %shard_map.101 = (bf16[136,1024]{1,0:T(8,128)(2,1)}, bf16[136,1024]{1,0:T(8,128)(2,1)}, bf16[128,1024]{1,0:T(8,128)(2,1)}) custom-call(s32[8,128]{1,0:T(8,128)} %bitcast.7, bf16[16,1024]{1,0:T(8,128)(2,1)} %get-tuple-element.13.hub_hbm.refs_0_, bf16[1024,1024]{1,0:T(8,128)(2,1)} %feat_ref.11, bf16[128,1024]{1,0:T(8,128)(2,1)} %copy-done.2), custom_call_target="tpu_custom_call" | custom-call | bytes 2097152 | tf_op jit(solution)/shard_map/pallas_call | solution.py:271
  9.1 2.1 %collective-permute-start.1 = (bf16[136,1024]{1,0:T(8,128)(2,1)}, bf16[136,1024]{1,0:T(8,128)(2,1)S(1)}, u32[]{:S(2)}, u32[]{:S(2)}) collective-permute-start(bf16[136,1024]{1,0:T(8,128)(2,1)} %get-tuple-element.16), channel_id=1, source_target_pairs={{0,4},{1,5},{2,6},{3,7},{4,0},{5,1},{6,2},{7,3},{8,12},{9,13},{10,... | collective-permute-start | bytes 835592 | tf_op jit(solution)/shard_map/ppermute | solution.py:256
  11.2 0.9 %copy-done.4 = bf16[128,1024]{1,0:T(8,128)(2,1)S(1)} copy-done((bf16[128,1024]{1,0:T(8,128)(2,1)S(1)}, bf16[128,1024]{1,0:T(8,128)(2,1)}, u32[]{:S(2)}) %copy-start.4) | copy-done | bytes 262168
  12.1 8.9 %shard_map.102.after_ref.count_ref = bf16[1024,2304]{1,0:T(8,128)(2,1)S(1)} custom-call(s32[16,1024]{1,0:T(8,128)S(1)} %bitcast.4, s32[8,1024]{1,0:T(8,128)S(1)} %bitcast.12, s32[16,1024]{1,0:T(8,128)S(1)} %bitcast.5, s32[3,1024]{1,0:T(4,128)S(1)} %copy-done.6, bf16[128,1024]{1,0:T(8,128)(2,1)S(1)} %copy-done.4), custom_call_target="tpu_custom_call" | custom-call | flops 201326592 | bytes 4718592 | tf_op jit(solution)/shard_map/pallas_call | solution.py:284
  21.0 2.3 %shard_map.103.after_ref.own_ref = f32[1024,1024]{1,0:T(8,128)S(1)} custom-call(bf16[1024,1024]{1,0:T(8,128)(2,1)S(1)} %copy-done, bf16[1024,1024]{1,0:T(8,128)(2,1)S(1)} %copy-done.12, bf16[1024]{0:T(1024)(128)(2,1)S(1)} %copy-done.13, bf16[1024,2304]{1,0:T(8,128)(2,1)S(1)} %shard_map.102.after_ref.count_ref), custom_call_target="tpu_custom_call" | custom-call | flops 8589934592 | bytes 8388608 | tf_op jit(solution)/shard_map/pallas_call | solution.py:322
  23.4 2.3 %shard_map.104.after_ref.sum_ref = f32[1024,1024]{1,0:T(8,128)S(1)} custom-call(bf16[1024,1024]{1,0:T(8,128)(2,1)S(1)} %copy-done, bf16[1024,2304]{1,0:T(8,128)(2,1)S(1)} %shard_map.102.after_ref.count_ref, f32[1024,1024]{1,0:T(8,128)S(1)} %shard_map.103.after_ref.own_ref), custom_call_target="tpu_custom_call" | custom-call | flops 8589934592 | bytes 8388608 | tf_op jit(solution)/shard_map/pallas_call | solution.py:329
  25.8 0.9 %shard_map.105 = (bf16[128,1024]{1,0:T(8,128)(2,1)S(1)}, bf16[128,1024]{1,0:T(8,128)(2,1)S(1)}) custom-call(s32[8,128]{1,0:T(8,128)S(1)} %bitcast.8, bf16[1024,1024]{1,0:T(8,128)(2,1)S(1)} %copy-done, f32[1024,1024]{1,0:T(8,128)S(1)} %shard_map.104.after_ref.sum_ref), custom_call_target="tpu_custom_call" | custom-call | flops 2147483648 | bytes 2097152 | tf_op jit(solution)/shard_map/pallas_call | solution.py:293
  26.7 2.5 %collective-permute-start.9 = (bf16[128,1024]{1,0:T(8,128)(2,1)S(1)}, bf16[128,1024]{1,0:T(8,128)(2,1)S(1)}, u32[]{:S(2)}, u32[]{:S(2)}) collective-permute-start(bf16[128,1024]{1,0:T(8,128)(2,1)S(1)} %get-tuple-element.20), channel_id=1, source_target_pairs={{0,5},{1,4},{2,7},{3,6},{4,1},{5,0},{6,3},{7,2},{8,13},{9,12},{10,... | collective-permute-start | bytes 786440 | tf_op jit(solution)/shard_map/ppermute | solution.py:256
  29.2 1.2 %collective-permute-start.6 = (bf16[32,1024]{1,0:T(8,128)(2,1)S(1)}, bf16[32,1024]{1,0:T(8,128)(2,1)S(1)}, u32[]{:S(2)}, u32[]{:S(2)}) collective-permute-start(bf16[32,1024]{1,0:T(8,128)(2,1)S(1)} %shard_map.106.after_ref.refs_0_), channel_id=1, source_target_pairs={{0,24},{8,16},{16,8},{24,0},{1,25},{9,17},{17,9},{25,1},{2,26},{10... | collective-permute-start | bytes 196616 | tf_op jit(solution)/shard_map/ppermute | solution.py:256
  30.5 1.2 %collective-permute-start.5 = (bf16[32,1024]{1,0:T(8,128)(2,1)S(1)}, bf16[32,1024]{1,0:T(8,128)(2,1)S(1)}, u32[]{:S(2)}, u32[]{:S(2)}) collective-permute-start(bf16[32,1024]{1,0:T(8,128)(2,1)S(1)} %shard_map.106.after_ref.refs_0_), channel_id=1, source_target_pairs={{0,16},{8,24},{16,0},{24,8},{1,17},{9,25},{17,1},{25,9},{2,18},{10... | collective-permute-start | bytes 196616 | tf_op jit(solution)/shard_map/ppermute | solution.py:256
  32.4 1.2 %collective-permute-done.6.refs_3_ = bf16[32,1024]{1,0:T(8,128)(2,1)S(1)} collective-permute-done((bf16[32,1024]{1,0:T(8,128)(2,1)S(1)}, bf16[32,1024]{1,0:T(8,128)(2,1)S(1)}, u32[]{:S(2)}, u32[]{:S(2)}) %collective-permute-start.6) | collective-permute-done | bytes 65568 | tf_op jit(solution)/shard_map/ppermute | solution.py:256
  33.6 2.1 %collective-permute-start.10 = (bf16[128,512]{1,0:T(8,128)(2,1)S(1)}, bf16[128,512]{1,0:T(8,128)(2,1)S(1)}, u32[]{:S(2)}, u32[]{:S(2)}) collective-permute-start(bf16[128,512]{1,0:T(8,128)(2,1)S(1)} %shard_map.107.refs_4_), channel_id=1, source_target_pairs={{0,7},{1,6},{2,5},{3,4},{4,3},{5,2},{6,1},{7,0},{8,15},{9,14},{10,... | collective-permute-start | bytes 393224 | tf_op jit(solution)/shard_map/ppermute | solution.py:256
  35.7 1.5 %collective-permute-start.7 = (bf16[128,1024]{1,0:T(8,128)(2,1)S(1)}, bf16[128,1024]{1,0:T(8,128)(2,1)S(1)}, u32[]{:S(2)}, u32[]{:S(2)}) collective-permute-start(bf16[128,1024]{1,0:T(8,128)(2,1)S(1)} %shard_map.108.refs_5_.refs_0_), channel_id=1, source_target_pairs={{0,1},{1,0},{2,3},{3,2},{4,5},{5,4},{6,7},{7,6},{8,9},{9,8},{10,11... | collective-permute-start | bytes 786440 | tf_op jit(solution)/shard_map/ppermute | solution.py:256
  37.2 1.8 %shard_map.109.sum_ref.refs_2_ = f32[1024,1024]{1,0:T(8,128)S(1)} custom-call(f32[1024,1024]{1,0:T(8,128)S(1)} %shard_map.104.after_ref.sum_ref, bf16[1024,2304]{1,0:T(8,128)(2,1)S(1)} %shard_map.102.after_ref.count_ref, bf16[128,1024]{1,0:T(8,128)(2,1)S(1)} %copy-done.5, bf16[128,1024]{1,0:T(8,128)(2,1)S(1)} %copy-done.3, ...), custom_call_target="tpu_custom_call" | custom-call | flops 85899345920 | bytes 8388608 | tf_op jit(solution)/shard_map/pallas_call | solution.py:313
  40.8 0.9 %collective-permute-done.8.refs_0_ = bf16[128,1024]{1,0:T(8,128)(2,1)S(1)} collective-permute-done((bf16[128,1024]{1,0:T(8,128)(2,1)S(1)}, bf16[128,1024]{1,0:T(8,128)(2,1)S(1)}, u32[]{:S(2)}, u32[]{:S(2)}) %collective-permute-start.8) | collective-permute-done | bytes 262176 | tf_op jit(solution)/shard_map/ppermute | solution.py:256
  42.8 1.0 %collective-permute-start.12 = (bf16[128,256]{1,0:T(8,128)(2,1)S(1)}, bf16[128,256]{1,0:T(8,128)(2,1)S(1)}, u32[]{:S(2)}, u32[]{:S(2)}) collective-permute-start(bf16[128,256]{1,0:T(8,128)(2,1)S(1)} %shard_map.115), channel_id=1, source_target_pairs={{0,7},{1,6},{2,5},{3,4},{4,3},{5,2},{6,1},{7,0},{8,15},{9,14},{10,... | collective-permute-start | bytes 196616 | tf_op jit(solution)/shard_map/ppermute | solution.py:256
  43.8 6.7 %collective-permute-done.10.block_ref = bf16[128,512]{1,0:T(8,128)(2,1)S(1)} collective-permute-done((bf16[128,512]{1,0:T(8,128)(2,1)S(1)}, bf16[128,512]{1,0:T(8,128)(2,1)S(1)}, u32[]{:S(2)}, u32[]{:S(2)}) %collective-permute-start.10) | collective-permute-done | bytes 131104 | tf_op jit(solution)/shard_map/ppermute | solution.py:256
  50.5 1.5 %shard_map.112.own_ref = f32[1024,1024]{1,0:T(8,128)S(1)} custom-call(f32[1024,1024]{1,0:T(8,128)S(1)} %shard_map.103.after_ref.own_ref, f32[1024,1024]{1,0:T(8,128)S(1)} %shard_map.111.sum_ref.after_ref, bf16[1024,2304]{1,0:T(8,128)(2,1)S(1)} %shard_map.102.after_ref.count_ref, s32[3,1024]{1,0:T(4,128)S(1)} %copy-done.6, bf16[1024,1024]{1,0:T(8,128)(2,1)S(1)} %copy-done.1, ...), custom_call_target="tpu_custom_call" | custom-call | flops 4294967296 | bytes 8388608 | tf_op jit(solution)/shard_map/pallas_call | solution.py:357
  52.1 1.1 %shard_map.114.own_ref = f32[1024,1024]{1,0:T(8,128)S(1)} custom-call(f32[1024,1024]{1,0:T(8,128)S(1)} %shard_map.112.own_ref, f32[1024,1024]{1,0:T(8,128)S(1)} %shard_map.111.sum_ref.after_ref, bf16[1024,2304]{1,0:T(8,128)(2,1)S(1)} %shard_map.102.after_ref.count_ref, s32[3,1024]{1,0:T(4,128)S(1)} %copy-done.6, bf16[1024,1024]{1,0:T(8,128)(2,1)S(1)} %copy-done.1, ...), custom_call_target="tpu_custom_call" | custom-call | flops 2147483648 | bytes 8388608 | tf_op jit(solution)/shard_map/pallas_call | solution.py:357
  53.3 2.2 %shard_map.116 = bf16[1024,1024]{1,0:T(8,128)(2,1)} custom-call(f32[1024,1024]{1,0:T(8,128)S(1)} %shard_map.114.own_ref, f32[1024,1024]{1,0:T(8,128)S(1)} %shard_map.111.sum_ref.after_ref, bf16[1024,2304]{1,0:T(8,128)(2,1)S(1)} %shard_map.102.after_ref.count_ref, s32[3,1024]{1,0:T(4,128)S(1)} %copy-done.6, bf16[1024,1024]{1,0:T(8,128)(2,1)S(1)} %copy-done.1, ...), custom_call_target="tpu_custom_call" | custom-call | flops 2147483648 | bytes 8388608 | tf_op jit(solution)/shard_map/pallas_call | solution.py:365
  (47 shorter events, 4.0 us)
Async XLA Ops:
  0.0 11.2 %copy-start.6 = (s32[3,1024]{1,0:T(4,128)S(1)}, s32[3,1024]{1,0:T(4,128)}, u32[]{:S(2)}) copy-start(s32[3,1024]{1,0:T(4,128)} %deg_ref.7) | copy-start | bytes 36868
  0.0 11.2 %copy-start.9 = (s32[1024,16]{0,1:T(8,128)S(1)}, s32[1024,16]{0,1:T(8,128)}, u32[]{:S(2)}) copy-start(s32[1024,16]{0,1:T(8,128)} %param.17) | copy-start | bytes 196612
  0.0 11.2 %copy-start.8 = (s32[1024,16]{0,1:T(8,128)S(1)}, s32[1024,16]{0,1:T(8,128)}, u32[]{:S(2)}) copy-start(s32[1024,16]{0,1:T(8,128)} %param.16) | copy-start | bytes 196612
  0.0 11.2 %copy-start.11 = (s32[1024,8]{0,1:T(8,128)S(1)}, s32[1024,8]{0,1:T(8,128)}, u32[]{:S(2)}) copy-start(s32[1024,8]{0,1:T(8,128)} %param.15) | copy-start | bytes 98308
  3.0 18.0 %copy-start = (bf16[1024,1024]{1,0:T(8,128)(2,1)S(1)}, bf16[1024,1024]{1,0:T(8,128)(2,1)}, u32[]{:S(2)}) copy-start(bf16[1024,1024]{1,0:T(8,128)(2,1)} %feat_ref.11) | copy-start | bytes 6291460
  3.0 18.0 %copy-start.13 = (bf16[1024]{0:T(1024)(128)(2,1)S(1)}, bf16[1024]{0:T(1024)(128)(2,1)}, u32[]{:S(2)}) copy-start(bf16[1024]{0:T(1024)(128)(2,1)} %bias_ref.1) | copy-start | bytes 6148
  3.0 2.1 %collective-permute-start = (bf16[128,1024]{1,0:T(8,128)(2,1)}, bf16[128,1024]{1,0:T(8,128)(2,1)S(1)}, u32[]{:S(2)}, u32[]{:S(2)}) collective-permute-start(bf16[128,1024]{1,0:T(8,128)(2,1)} %get-tuple-element.14), channel_id=1, source_target_pairs={{0,1},{1,0},{2,3},{3,2},{4,5},{5,4},{6,7},{7,6},{8,9},{9,8},{10,11... | collective-permute-start | bytes 786440 | tf_op jit(solution)/shard_map/ppermute | solution.py:256
  3.7 25.4 %collective-permute-start.3 = (bf16[136,1024]{1,0:T(8,128)(2,1)}, bf16[136,1024]{1,0:T(8,128)(2,1)S(1)}, u32[]{:S(2)}, u32[]{:S(2)}) collective-permute-start(bf16[136,1024]{1,0:T(8,128)(2,1)} %get-tuple-element.18), channel_id=1, source_target_pairs={{0,6},{1,7},{2,4},{3,5},{4,2},{5,3},{6,0},{7,1},{8,14},{9,15},{10,... | collective-permute-start | bytes 835592 | tf_op jit(solution)/shard_map/ppermute | solution.py:256
  9.1 20.1 %collective-permute-start.1 = (bf16[136,1024]{1,0:T(8,128)(2,1)}, bf16[136,1024]{1,0:T(8,128)(2,1)S(1)}, u32[]{:S(2)}, u32[]{:S(2)}) collective-permute-start(bf16[136,1024]{1,0:T(8,128)(2,1)} %get-tuple-element.16), channel_id=1, source_target_pairs={{0,4},{1,5},{2,6},{3,7},{4,0},{5,1},{6,2},{7,3},{8,12},{9,13},{10,... | collective-permute-start | bytes 835592 | tf_op jit(solution)/shard_map/ppermute | solution.py:256
  11.2 18.0 %collective-permute-start.2 = (bf16[136,1024]{1,0:T(8,128)(2,1)}, bf16[136,1024]{1,0:T(8,128)(2,1)S(1)}, u32[]{:S(2)}, u32[]{:S(2)}) collective-permute-start(bf16[136,1024]{1,0:T(8,128)(2,1)} %get-tuple-element.17), channel_id=1, source_target_pairs={{0,2},{1,3},{2,0},{3,1},{4,6},{5,7},{6,4},{7,5},{8,10},{9,11},{10,... | collective-permute-start | bytes 835592 | tf_op jit(solution)/shard_map/ppermute | solution.py:256
  12.1 8.9 %copy-start.12 = (bf16[1024,1024]{1,0:T(8,128)(2,1)S(1)}, bf16[1024,1024]{1,0:T(8,128)(2,1)}, u32[]{:S(2)}) copy-start(bf16[1024,1024]{1,0:T(8,128)(2,1)} %w_ref.4) | copy-start | bytes 6291460
  25.7 3.5 %copy-start.7 = (bf16[16,1024]{1,0:T(8,128)(2,1)S(1)}, bf16[16,1024]{1,0:T(8,128)(2,1)}, u32[]{:S(2)}) copy-start(bf16[16,1024]{1,0:T(8,128)(2,1)} %get-tuple-element.13.hub_hbm.refs_0_) | copy-start | bytes 98308
  26.7 14.2 %collective-permute-start.9 = (bf16[128,1024]{1,0:T(8,128)(2,1)S(1)}, bf16[128,1024]{1,0:T(8,128)(2,1)S(1)}, u32[]{:S(2)}, u32[]{:S(2)}) collective-permute-start(bf16[128,1024]{1,0:T(8,128)(2,1)S(1)} %get-tuple-element.20), channel_id=1, source_target_pairs={{0,5},{1,4},{2,7},{3,6},{4,1},{5,0},{6,3},{7,2},{8,13},{9,12},{10,... | collective-permute-start | bytes 786440 | tf_op jit(solution)/shard_map/ppermute | solution.py:256
  29.2 12.6 %collective-permute-start.8 = (bf16[128,1024]{1,0:T(8,128)(2,1)S(1)}, bf16[128,1024]{1,0:T(8,128)(2,1)S(1)}, u32[]{:S(2)}, u32[]{:S(2)}) collective-permute-start(bf16[128,1024]{1,0:T(8,128)(2,1)S(1)} %get-tuple-element.19.refs_4_), channel_id=1, source_target_pairs={{0,3},{1,2},{2,1},{3,0},{4,7},{5,6},{6,5},{7,4},{8,11},{9,10},{10,... | collective-permute-start | bytes 786440 | tf_op jit(solution)/shard_map/ppermute | solution.py:256
  29.2 8.0 %copy-start.3 = (bf16[128,1024]{1,0:T(8,128)(2,1)S(1)}, bf16[128,1024]{1,0:T(8,128)(2,1)}, u32[]{:S(2)}) copy-start(bf16[128,1024]{1,0:T(8,128)(2,1)} %copy-done.2) | copy-start | bytes 786436
  29.2 7.9 %copy-start.5 = (bf16[128,1024]{1,0:T(8,128)(2,1)S(1)}, bf16[128,1024]{1,0:T(8,128)(2,1)}, u32[]{:S(2)}) copy-start(bf16[128,1024]{1,0:T(8,128)(2,1)} %get-tuple-element.15.after_ref.refs_0_) | copy-start | bytes 786436
  29.2 4.4 %collective-permute-start.6 = (bf16[32,1024]{1,0:T(8,128)(2,1)S(1)}, bf16[32,1024]{1,0:T(8,128)(2,1)S(1)}, u32[]{:S(2)}, u32[]{:S(2)}) collective-permute-start(bf16[32,1024]{1,0:T(8,128)(2,1)S(1)} %shard_map.106.after_ref.refs_0_), channel_id=1, source_target_pairs={{0,24},{8,16},{16,8},{24,0},{1,25},{9,17},{17,9},{25,1},{2,26},{10... | collective-permute-start | bytes 196616 | tf_op jit(solution)/shard_map/ppermute | solution.py:256
  30.5 5.2 %collective-permute-start.5 = (bf16[32,1024]{1,0:T(8,128)(2,1)S(1)}, bf16[32,1024]{1,0:T(8,128)(2,1)S(1)}, u32[]{:S(2)}, u32[]{:S(2)}) collective-permute-start(bf16[32,1024]{1,0:T(8,128)(2,1)S(1)} %shard_map.106.after_ref.refs_0_), channel_id=1, source_target_pairs={{0,16},{8,24},{16,0},{24,8},{1,17},{9,25},{17,1},{25,9},{2,18},{10... | collective-permute-start | bytes 196616 | tf_op jit(solution)/shard_map/ppermute | solution.py:256
  31.7 4.0 %collective-permute-start.4 = (bf16[32,1024]{1,0:T(8,128)(2,1)S(1)}, bf16[32,1024]{1,0:T(8,128)(2,1)S(1)}, u32[]{:S(2)}, u32[]{:S(2)}) collective-permute-start(bf16[32,1024]{1,0:T(8,128)(2,1)S(1)} %shard_map.106.after_ref.refs_0_), channel_id=1, source_target_pairs={{0,8},{8,0},{16,24},{24,16},{1,9},{9,1},{17,25},{25,17},{2,10},{10... | collective-permute-start | bytes 196616 | tf_op jit(solution)/shard_map/ppermute | solution.py:256
  33.6 16.9 %collective-permute-start.10 = (bf16[128,512]{1,0:T(8,128)(2,1)S(1)}, bf16[128,512]{1,0:T(8,128)(2,1)S(1)}, u32[]{:S(2)}, u32[]{:S(2)}) collective-permute-start(bf16[128,512]{1,0:T(8,128)(2,1)S(1)} %shard_map.107.refs_4_), channel_id=1, source_target_pairs={{0,7},{1,6},{2,5},{3,4},{4,3},{5,2},{6,1},{7,0},{8,15},{9,14},{10,... | collective-permute-start | bytes 393224 | tf_op jit(solution)/shard_map/ppermute | solution.py:256
  35.7 3.3 %collective-permute-start.7 = (bf16[128,1024]{1,0:T(8,128)(2,1)S(1)}, bf16[128,1024]{1,0:T(8,128)(2,1)S(1)}, u32[]{:S(2)}, u32[]{:S(2)}) collective-permute-start(bf16[128,1024]{1,0:T(8,128)(2,1)S(1)} %shard_map.108.refs_5_.refs_0_), channel_id=1, source_target_pairs={{0,1},{1,0},{2,3},{3,2},{4,5},{5,4},{6,7},{7,6},{8,9},{9,8},{10,11... | collective-permute-start | bytes 786440 | tf_op jit(solution)/shard_map/ppermute | solution.py:256
  40.1 12.0 %collective-permute-start.11 = (bf16[128,256]{1,0:T(8,128)(2,1)S(1)}, bf16[128,256]{1,0:T(8,128)(2,1)S(1)}, u32[]{:S(2)}, u32[]{:S(2)}) collective-permute-start(bf16[128,256]{1,0:T(8,128)(2,1)S(1)} %shard_map.113), channel_id=1, source_target_pairs={{0,7},{1,6},{2,5},{3,4},{4,3},{5,2},{6,1},{7,0},{8,15},{9,14},{10,... | collective-permute-start | bytes 196616 | tf_op jit(solution)/shard_map/ppermute | solution.py:256
  42.5 8.1 %copy-start.1 = (bf16[1024,1024]{1,0:T(8,128)(2,1)S(1)}, bf16[1024,1024]{1,0:T(8,128)(2,1)}, u32[]{:S(2)}) copy-start(bf16[1024,1024]{1,0:T(8,128)(2,1)} %w_ref.7) | copy-start | bytes 6291460
  42.8 10.5 %collective-permute-start.12 = (bf16[128,256]{1,0:T(8,128)(2,1)S(1)}, bf16[128,256]{1,0:T(8,128)(2,1)S(1)}, u32[]{:S(2)}, u32[]{:S(2)}) collective-permute-start(bf16[128,256]{1,0:T(8,128)(2,1)S(1)} %shard_map.115), channel_id=1, source_target_pairs={{0,7},{1,6},{2,5},{3,4},{4,3},{5,2},{6,1},{7,0},{8,15},{9,14},{10,... | collective-permute-start | bytes 196616 | tf_op jit(solution)/shard_map/ppermute | solution.py:256
  (3 other events, 4.0 us)
